TPU v7x, 32 devices: a whole 2x2x4 slice. The times are simulated.
32 devices in a mesh: seq: 4 (over x, core), blk: 8 (over z, y).
Axes of the slice: x: 2, y: 2, z: 4, core: 2. Of those that a mesh axis runs over, the one named last changes fastest.
Arguments:
- latents: bfloat16 [4, 8192, 512], P('seq', 'blk'), may hold values from -6 to 6
- tokens: bfloat16 [4, 8192, 512], P('seq', 'blk'), may hold values from -6 to 6
- lengths: int32 [4, 4], P('seq'), may hold values from 1792 to 2048, as said below
- gain_lat: float32 [512], replicated, may hold values from 0.1 to 1.9
- gain_tok: float32 [512], replicated, may hold values from 0.1 to 1.9
- gain_mlp: float32 [512], replicated, may hold values from 0.1 to 1.9
- w_query: bfloat16 [512, 512], replicated, may hold values from -0.625 to 0.625
- w_key: bfloat16 [512, 512], replicated, may hold values from -0.25 to 0.25
- w_value: bfloat16 [512, 512], replicated, may hold values from -0.25 to 0.25
- w_out: bfloat16 [512, 512], replicated, may hold values from -0.5 to 0.5
- w_up: bfloat16 [512, 2048], replicated, may hold values from -0.25 to 0.25
- w_down: bfloat16 [2048, 512], replicated, may hold values from -0.125 to 0.125
- d_out: bfloat16 [4, 8192, 512], P('seq', 'blk'), may hold values from -6 to 6
Outputs:
- out_latents: bfloat16 [4, 8192, 512], P('seq', 'blk')
- d_latents: float32 [4, 8192, 512], P('seq', 'blk')
- d_tokens: float32 [4, 8192, 512], P('seq', 'blk')
- d_w_query: float32 [512, 512], replicated
- d_w_key: float32 [512, 512], replicated
- d_w_value: float32 [512, 512], replicated
- d_w_out: float32 [512, 512], replicated
- d_w_up: float32 [512, 2048], replicated
- d_w_down: float32 [2048, 512], replicated
- d_gain_lat: float32 [512], replicated
- d_gain_tok: float32 [512], replicated
- d_gain_mlp: float32 [512], replicated
Inputs may be any that keep to these rules, and one draw needn't show every extreme that they name: Positions past the sum of a row's lengths are padding.
All inputs are finite; a program needn't handle non-finite values.
Results may differ from a plain program's by a relative error of at most 0.024.
Values may be sent and summed in bfloat16 or wider, within the bound.
No kernel may reach another device: no remote copies, remote signals or barrier semaphores. Data moves between devices by JAX's collectives and lax.ppermute only.
A program may use at most 256 MiB of HBM per device.

v0:
```python
import functools
import math

import jax
import jax.numpy as jnp
from jax import lax
from jax.experimental import pallas as pl
from jax.experimental.pallas import tpu as pltpu
from jax.sharding import PartitionSpec as P

EPSILON = 1e-05
NEGATIVE = -1e30
ROOM = (64 << 20) - (160 << 10)
LOG2E = 1.4426950408889634
GELU_C = math.sqrt(2.0 / math.pi)
GELU_A = 0.044715
F32 = jnp.float32
BF16 = jnp.bfloat16
NN = (((1,), (0,)), ((), ()))
NT = (((1,), (1,)), ((), ()))
TN = (((0,), (0,)), ((), ()))


def dot(left, right, dims=NN):
    return lax.dot_general(left, right, dims, preferred_element_type=F32)


def norm_parts(rows):
    center = rows - jnp.mean(rows, axis=-1, keepdims=True)
    spread = jnp.mean(center * center, axis=-1, keepdims=True)
    inverse = lax.rsqrt(spread + EPSILON)
    return center * inverse, inverse


def norm_back(d_normed, unit, inverse, gain):
    d_unit = d_normed * gain
    mean_d = jnp.mean(d_unit, axis=-1, keepdims=True)
    mean_p = jnp.mean(d_unit * unit, axis=-1, keepdims=True)
    return inverse * (d_unit - mean_d - unit * mean_p)


def vmem_call(kernel, name, outs, args, limit, scratch=(), smem=0):
    held = sum(math.prod(shape) * jnp.dtype(dtype).itemsize for shape, dtype in scratch)
    in_vmem = pl.BlockSpec(memory_space=pltpu.VMEM)
    in_smem = pl.BlockSpec(memory_space=pltpu.SMEM)
    return pl.pallas_call(
        kernel,
        in_specs=[in_smem] * smem + [in_vmem] * (len(args) - smem),
        out_specs=[in_vmem] * len(outs),
        out_shape=[jax.ShapeDtypeStruct(shape, dtype) for shape, dtype in outs],
        scratch_shapes=[pltpu.VMEM(shape, dtype) for shape, dtype in scratch],
        compiler_params=pltpu.CompilerParams(vmem_limit_bytes=(limit << 20) + held),
        cost_estimate=pl.CostEstimate(flops=0, bytes_accessed=0, transcendentals=0),
        name=name,
    )(*args)


class Flow:
    AHEAD = 64 << 20

    def __init__(self, loads, stores, semaphores):
        self.loads = loads
        self.stores = stores
        self.semaphores = semaphores
        self.started = 0
        self.waiting = set(range(len(loads)))
        self.begun = []
        self.whole = set()
        self.start_more(-1)

    def start_more(self, least):
        def size(j):
            held = self.loads[j][1]
            return math.prod(held.shape) * jnp.dtype(held.dtype).itemsize

        flying = sum(size(j) for j in self.waiting if j < self.started)
        while self.started < len(self.loads) and (self.started <= least or flying + size(self.started) <= self.AHEAD):
            flying += size(self.started)
            self.loads[self.started][2].start()
            self.started += 1

    def need(self, *refs):
        wanted = [j for j, load in enumerate(self.loads) if j in self.waiting and any(load[1] is r for r in refs)]
        for j in wanted:
            self.start_more(j)
        for j in wanted:
            self.waiting.discard(j)
            self.loads[j][2].wait()
        self.start_more(-1)

    def emit(self, ref, *where):
        for j, (out, held) in enumerate(self.stores):
            if held is ref:
                self.whole.add(j)
                source, target = (held.at[where], out.at[where]) if where else (held, out)
                copy = pltpu.make_async_copy(source, target, self.semaphores.at[len(self.begun)])
                copy.start()
                self.begun.append(copy)

    def close(self):
        self.need(*[held for _, held, _ in self.loads])
        for j, (_, held) in enumerate(self.stores):
            if j not in self.whole:
                self.emit(held)
        for copy in self.begun:
            copy.wait()


def hbm_call(kernel, name, outs, args, limit, scratch=(), smem=0, fixed_in=(), fixed_out=(), stores=None):
    arrays = args[smem:]
    moves_in = [j for j in range(len(arrays)) if j not in fixed_in]
    moves_out = [j for j in range(len(outs)) if j not in fixed_out]
    held = [(arrays[j].shape, arrays[j].dtype) for j in moves_in] + [outs[j] for j in moves_out] + list(scratch)
    size = sum(math.prod(shape) * jnp.dtype(dtype).itemsize for shape, dtype in held)

    resident = [(arrays[j].shape, arrays[j].dtype) for j in fixed_in] + [outs[j] for j in fixed_out]
    rest = sum(math.prod(shape) * jnp.dtype(dtype).itemsize for shape, dtype in resident)
    limit = max((limit << 20) + size, ROOM - rest)

    def body(*refs):
        scalars, refs = refs[:smem], refs[smem:]
        ins, refs = list(refs[: len(arrays)]), refs[len(arrays) :]
        results, refs = list(refs[: len(outs)]), refs[len(outs) :]
        *kept, load_sems, store_sems = refs
        loads, kept_out = [], []
        for n, j in enumerate(moves_in):
            loads.append((ins[j], kept[n], pltpu.make_async_copy(ins[j], kept[n], load_sems.at[n])))
            ins[j] = kept[n]
        kept = kept[len(moves_in) :]
        for n, j in enumerate(moves_out):
            kept_out.append((results[j], kept[n]))
            results[j] = kept[n]
        flow = Flow(loads, kept_out, store_sems)
        kernel(flow, *scalars, *ins, *results, *kept[len(moves_out) :])
        flow.close()

    def place(count, fixed):
        return [pl.BlockSpec(memory_space=pltpu.VMEM if j in fixed else pl.ANY) for j in range(count)]

    return pl.pallas_call(
        body,
        in_specs=[pl.BlockSpec(memory_space=pltpu.SMEM)] * smem + place(len(arrays), fixed_in),
        out_specs=place(len(outs), fixed_out),
        out_shape=[jax.ShapeDtypeStruct(shape, dtype) for shape, dtype in outs],
        scratch_shapes=[pltpu.VMEM(shape, dtype) for shape, dtype in held]
        + [pltpu.SemaphoreType.DMA((max(len(moves_in), 1),)), pltpu.SemaphoreType.DMA((max(stores or len(moves_out), 1),))],
        compiler_params=pltpu.CompilerParams(vmem_limit_bytes=min(limit, ROOM)),
        cost_estimate=pl.CostEstimate(flops=0, bytes_accessed=0, transcendentals=0),
        name=name,
    )(*args)


def cuts(size, step):
    return [(i, min(step, size - i)) for i in range(0, size, step)]


def fold(rows):
    return jnp.sum(rows.reshape(rows.shape[0] // 8, 8, rows.shape[1]), axis=0)


def column_of(row):
    return jnp.transpose(jnp.broadcast_to(row, (8, row.shape[1])))[:, :1]


def row_of(column):
    return jnp.transpose(jnp.broadcast_to(column, (column.shape[0], 128)))[:8, :]


def join(refs, whole_ref):
    part = refs[0].shape[0]
    for j, ref in enumerate(refs):
        whole_ref[pl.ds(j * part, part), :] = ref[...]


def line_store(ref, scenes, scene, start, value):
    part = ref.shape[0] // scenes
    size = min(part, value.shape[0])
    for first in range(0, value.shape[0], size):
        at = start + first
        place = (scene ^ (at // part)) * part + at % part
        ref[pl.ds(pl.multiple_of(place, 16), size), :] = value[first : first + size]


def part_store(refs, start, value):
    part = refs[0].shape[0]
    size = min(part, value.shape[0])
    for first in range(0, value.shape[0], size):
        at = start + first
        refs[at // part][pl.ds(at % part, size), :] = value[first : first + size]


def kv_kernel(flow, tok_ref, gain_ref, wk_ref, wv_ref, k_ref, v_ref):
    flow.need(tok_ref, gain_ref, wk_ref, wv_ref)
    for start, size in cuts(tok_ref.shape[0], 256):
        rows = pl.ds(start, size)
        unit, _ = norm_parts(tok_ref[rows, :].astype(F32))
        low = (unit * gain_ref[...]).astype(BF16)
        k_ref[rows, :] = dot(low, wk_ref[...]).astype(BF16)
        v_ref[rows, :] = dot(low, wv_ref[...]).astype(BF16)
    flow.emit(k_ref)
    flow.emit(v_ref)


def keys_values(tok, gain, w_key, w_value):
    return hbm_call(kv_kernel, "keys_values", [(tok.shape, BF16)] * 2, (tok, gain, w_key, w_value), 8)


def score_piece(info_ref, p, k_ref, s_ref, query, columns, top, scale):
    begin, end = info_ref[0], info_ref[1]
    for start, size in cuts(k_ref.shape[0], 512):
        s = dot(k_ref[pl.ds(start, size), :], query, NT) * (scale * LOG2E)
        place = info_ref[2 + p] + start + lax.broadcasted_iota(jnp.int32, (size, 1), 0)
        s = s + jnp.where((place >= begin) & (place < end), 0.0, NEGATIVE)
        s_ref[pl.ds(start, size), columns] = s
        top = jnp.maximum(top, jnp.max(s.reshape(size // 8, 8, s.shape[1]), axis=0))
    return top


def weigh_piece(v_ref, s_ref, w_ref, columns, top, total, acc):
    for start, size in cuts(v_ref.shape[0], 512):
        w = jnp.exp2(s_ref[pl.ds(start, size), columns] - top)
        total = total + fold(w)
        w_ref[pl.ds(start, size), columns] = w.astype(BF16)
    part = dot(w_ref[:, columns], v_ref[...], TN)
    return total, part if acc is None else acc + part


def attend_kernel(parts, fresh, count, scale, flow, info_ref, gl_ref, wq_ref, *refs):
    new, refs = refs[: 3 * bool(fresh) + fresh], refs[3 * bool(fresh) + fresh :]
    lat_refs, refs = refs[:parts], refs[parts:]
    given = count - fresh
    k_refs, v_refs, refs = refs[:given], refs[given : 2 * given], refs[2 * given :]
    q_ref, acc_ref, top_ref, tot_ref, lat_ref = refs[:5]
    refs = refs[5:]
    k_refs, v_refs, refs = refs[:fresh] + k_refs, refs[fresh : 2 * fresh] + v_refs, refs[2 * fresh :]
    w_refs, s_refs = refs[:count], refs[count:]
    flow.need(*lat_refs, gl_ref, wq_ref)
    join(lat_refs, lat_ref)
    for j in range(fresh):
        kv_kernel(flow, new[3 + j], *new[:3], k_refs[j], v_refs[j])
    for start, size in cuts(lat_ref.shape[0], 512):
        rows = columns = pl.ds(start, size)
        unit, _ = norm_parts(lat_ref[rows, :].astype(F32))
        query = dot((unit * gl_ref[...]).astype(BF16), wq_ref[...]).astype(BF16)
        q_ref[rows, :] = query
        flow.need(*k_refs)
        top = jnp.full((8, size), NEGATIVE, F32)
        for p in range(count):
            top = score_piece(info_ref, p, k_refs[p], s_refs[p], query, columns, top, scale)
        top = jnp.max(top, axis=0, keepdims=True)
        total, acc = jnp.zeros((8, size), F32), None
        flow.need(*v_refs)
        for p in range(count):
            total, acc = weigh_piece(v_refs[p], s_refs[p], w_refs[p], columns, top, total, acc)
        acc_ref[rows, :] = acc
        if start == 0:
            flow.emit(lat_ref)
        for p in range(count):
            flow.emit(w_refs[p], slice(None), columns)
        flow.emit(acc_ref, rows)
        top_ref[:, columns] = jnp.broadcast_to(top, (8, size))
        tot_ref[:, columns] = total


def attend(info, lats, gl, wq, fresh, gt, wk, wv, keys, values, scale):
    rows, width = len(lats) * lats[0].shape[0], lats[0].shape[1]
    made = [(t.shape, BF16) for t in fresh]
    pieces = [t.shape[0] for t in (*fresh, *keys)]
    outs = [((rows, width), BF16), ((rows, width), F32), ((8, rows), F32), ((8, rows), F32), ((rows, width), BF16)]
    outs += made * 2 + [((n, rows), BF16) for n in pieces]
    new = (gt, wk, wv, *fresh) if fresh else ()
    q, acc, top, total, lat, *rest = hbm_call(
        functools.partial(attend_kernel, len(lats), len(fresh), len(pieces), scale),
        "attend",
        outs,
        (info, gl, wq, *new, *lats, *keys, *values),
        12,
        [((n, rows), F32) for n in pieces],
        smem=1,
        stores=len(outs) + (len(cuts(rows, 512)) - 1) * (len(pieces) + 1),
    )
    more = len(fresh)
    return q, acc, top, total, lat, rest[2 * more :], (*rest[:more], *keys), (*rest[more : 2 * more], *values)


def finish_kernel(
    scale, flow, info_ref, tok_ref, gt_ref, wk_ref, wv_ref, top_ref, q_ref, tot_ref, acc_ref, lat_ref, gm_ref, wo_ref, wu_ref, wd_ref,
    k_ref, v_ref, w_ref, factor_ref, mixed_ref, mlp_ref, state_ref, inner_ref, slope_ref, *refs,
):
    *out_refs, s_ref = refs
    kv_kernel(flow, tok_ref, gt_ref, wk_ref, wv_ref, k_ref, v_ref)
    flow.need(top_ref, q_ref, tot_ref, acc_ref)
    hidden = wu_ref.shape[1]
    for start, size in cuts(lat_ref.shape[0], 512):
        rows = columns = pl.ds(start, size)
        old = top_ref[:1, columns]
        top = jnp.broadcast_to(old, (8, size))
        top = score_piece(info_ref, 0, k_ref, s_ref, q_ref[rows, :], columns, top, scale)
        top = jnp.max(top, axis=0, keepdims=True)
        total, acc = weigh_piece(v_ref, s_ref, w_ref, columns, top, jnp.zeros((8, size), F32), None)
        shrink = jnp.exp2(old - top)
        total = jnp.sum(total, axis=0, keepdims=True) + jnp.sum(tot_ref[:, columns], axis=0, keepdims=True) * shrink
        inverse = 1.0 / total
        late, early = column_of(inverse), column_of(shrink * inverse)
        lane = lax.broadcasted_iota(jnp.int32, (size, 128), 1)
        factor_ref[rows, :] = jnp.where(lane == 0, late, early)
        mixed_ref[rows, :] = (acc * late + acc_ref[rows, :] * early).astype(BF16)
    for ref in (w_ref, factor_ref, mixed_ref):
        flow.emit(ref)
    flow.need(lat_ref, wo_ref, gm_ref, wu_ref, wd_ref)
    for start, size in cuts(lat_ref.shape[0], 256):
        rows = pl.ds(start, size)
        state = lat_ref[rows, :].astype(F32) + dot(mixed_ref[rows, :], wo_ref[...])
        state_ref[rows, :] = state
        unit, _ = norm_parts(state)
        low = (unit * gm_ref[...]).astype(BF16)
        mlp_ref[rows, :] = low
        out = state
        for first, step in cuts(hidden, 512):
            some = pl.ds(first, step)
            u = dot(low, wu_ref[:, some])
            square = u * u
            t = jnp.tanh(u * (GELU_C + (GELU_C * GELU_A) * square))
            half = 0.5 + 0.5 * t
            inner = (u * half).astype(BF16)
            bend = u * ((0.5 * GELU_C) + (1.5 * GELU_C * GELU_A) * square)
            inner_ref[rows, some] = inner
            slope_ref[rows, some] = (half + bend * (1.0 - t * t)).astype(BF16)
            out = out + dot(inner, wd_ref[some, :])
        part_store(out_refs, start, out.astype(BF16))
        for ref in (state_ref, mlp_ref, inner_ref, slope_ref):
            flow.emit(ref, rows)


def finish(info, parts, lat, q, acc, top, total, tail, gt, wk, wv, gm, wo, wu, wd, scale):
    rows, width = lat.shape
    hidden = wu.shape[1]
    tall = (rows, width)
    outs = [(tail.shape, BF16)] * 2 + [((tail.shape[0], rows), BF16), ((rows, 128), F32), (tall, BF16), (tall, BF16), (tall, F32)]
    outs += [((rows, hidden), BF16)] * 2 + [((rows // parts, width), BF16)] * parts
    out = hbm_call(
        functools.partial(finish_kernel, scale),
        "finish",
        outs,
        (info, tail, gt, wk, wv, top, q, total, acc, lat, gm, wo, wu, wd),
        22,
        [((tail.shape[0], rows), F32)],
        smem=1,
        stores=len(outs) + 4 * (len(cuts(rows, 256)) - 1),
    )
    return out[:9], out[9:]


def mlp_back_kernel(
    parts, flow, info_ref, *refs,
):
    cot_refs, refs = refs[:parts], refs[parts:]
    wd_ref, slope_ref, wu_ref, state_ref, mixed_ref, factor_ref, gm_ref, wo_ref, inner_ref, mlp_ref, *refs = refs
    dstate_ref, late_ref, early_ref, dlate_ref, dearly_ref, keep_ref, send_ref, dwo_ref, dgain_ref = refs[:9]
    dpre_ref, dproj_ref, cot_ref = refs[9:]
    flow.need(*cot_refs, wd_ref, slope_ref)
    join(cot_refs, cot_ref)
    hidden, width = wd_ref.shape

    def pack(half, first, value):
        rows = pl.ds(first, value.shape[0])

        @pl.when(info_ref[0] == half)
        def _():
            keep_ref[rows, :] = value.astype(BF16)

        @pl.when(info_ref[0] != half)
        def _():
            send_ref[rows, :] = value.astype(BF16)

    total = jnp.zeros((8, width), F32)
    for start, size in cuts(cot_ref.shape[0], 256):
        rows = pl.ds(start, size)
        cot = cot_ref[rows, :]
        d_mlp = None
        for first, step in cuts(hidden, 512):
            some = pl.ds(first, step)
            d_inner = dot(cot, wd_ref[some, :], NT)
            d_pre = (slope_ref[rows, some].astype(F32) * d_inner).astype(BF16)
            dpre_ref[rows, some] = d_pre
            flow.need(wu_ref)
            part = dot(d_pre, wu_ref[:, some], NT)
            d_mlp = part if d_mlp is None else d_mlp + part
        flow.need(gm_ref, wo_ref, state_ref, mixed_ref, factor_ref)
        unit, inverse = norm_parts(state_ref[rows, :])
        total = total + fold(d_mlp * unit)
        d_state = cot.astype(F32) + norm_back(d_mlp, unit, inverse, gm_ref[...])
        dstate_ref[rows, :] = d_state
        d_proj = d_state.astype(BF16)
        dproj_ref[rows, :] = d_proj
        d_att = dot(d_proj, wo_ref[...], NT)
        mixed = mixed_ref[rows, :].astype(F32)
        for lane, part_ref, delta_ref in ((0, late_ref, dlate_ref), (1, early_ref, dearly_ref)):
            part = (d_att * factor_ref[rows, lane : lane + 1]).astype(BF16)
            part_ref[rows, :] = part
            delta = jnp.sum(part.astype(F32) * mixed, axis=-1, keepdims=True)
            delta_ref[:, rows] = row_of(delta)
    dgain_ref[...] = total
    for ref in (dstate_ref, late_ref, early_ref, dlate_ref, dearly_ref):
        flow.emit(ref)
    flow.need(inner_ref, mlp_ref)
    for first, step in cuts(hidden, 512):
        pack(0, first, dot(inner_ref[:, first : first + step], cot_ref[...], TN))
    for first, step in cuts(hidden, 512):
        pack(1, first, dot(mlp_ref[...], dpre_ref[:, first : first + step], TN))
    dwo_ref[...] = dot(mixed_ref[...], dproj_ref[...], TN).astype(BF16)


def mlp_back(info, cots, slope, state, mixed, mlp, inner, factor, gm, wo, wu, wd):
    rows, width = state.shape
    hidden = wu.shape[1]
    tall, flat = (rows, width), (8, rows)
    outs = [(tall, F32), (tall, BF16), (tall, BF16), (flat, F32), (flat, F32)]
    outs += [((hidden, width), BF16)] * 2 + [((width, width), BF16), ((8, width), F32)]
    return hbm_call(
        functools.partial(mlp_back_kernel, len(cots)),
        "mlp_back",
        outs,
        (info, *cots, wd, slope, wu, state, mixed, factor, gm, wo, inner, mlp),
        20,
        [((rows, hidden), BF16), (tall, BF16), (tall, BF16)],
        smem=1,
    )


def attention_back_kernel(count, start, parts, extra, scale, flow, info_ref, *refs):
    q_ref, wk_ref, wv_ref, gain_ref, *refs = refs
    datt_ref, delta_ref, *refs = refs
    v_refs, w_refs, t_refs, k_refs = (refs[j : 4 * count : 4] for j in range(4))
    refs = refs[4 * count :]
    sums, refs = refs[:start], refs[start:]
    if parts:
        lat_ref, gl_ref, wq_ref, dstate_ref, dwo_ref, dgmlp_ref, *refs = refs
    dtok_refs, refs = refs[:count], refs[count:]
    if parts:
        dlat_ref, *refs = refs
        keep_ref, send_ref, dq_ref, akey_ref, aval_ref, dgain_ref, latlow_ref, dquery_ref, *refs = refs
    else:
        dq_ref, akey_ref, aval_ref, dgain_ref, *refs = refs
    dscore_ref, low_ref, dkey_ref, dval_ref, part_ref = refs
    totals = (dq_ref, akey_ref, aval_ref, dgain_ref)
    flow.need(q_ref, wk_ref, wv_ref, gain_ref)
    for p in range(count):
        size = k_refs[p].shape[0]
        flow.need(datt_ref, delta_ref, v_refs[p], w_refs[p], t_refs[p], k_refs[p])
        begin, end, first_place = info_ref[1 + 3 * p], info_ref[2 + 3 * p], info_ref[3 + 3 * p]
        part_ref[...] = jnp.zeros_like(part_ref)
        for first, step in cuts(size, 256):
            rows = pl.ds(first, step)
            active = (first_place + first < end) & (first_place + first + step > begin)

            @pl.when(active)
            def _(p=p, rows=rows):
                d_prob = dot(v_refs[p][rows, :], datt_ref[...], NT)
                d_score = (w_refs[p][rows, :].astype(F32) * (d_prob - delta_ref[:1, :])).astype(BF16)
                dscore_ref[rows, :] = d_score
                d_key = (dot(d_score, q_ref[...]) * scale).astype(BF16)
                d_value = dot(w_refs[p][rows, :], datt_ref[...]).astype(BF16)
                dkey_ref[rows, :] = d_key
                dval_ref[rows, :] = d_value
                unit, _ = norm_parts(t_refs[p][rows, :].astype(F32))
                low_ref[rows, :] = (unit * gain_ref[...]).astype(BF16)
                d_tok = dot(d_key, wk_ref[...], NT) + dot(d_value, wv_ref[...], NT)
                dtok_refs[p][rows, :] = d_tok.astype(BF16)
                part_ref[...] += fold(d_tok * unit)

            @pl.when(jnp.logical_not(active))
            def _(p=p, rows=rows):
                for ref in (dscore_ref, dkey_ref, dval_ref, low_ref, dtok_refs[p]):
                    ref[rows, :] = jnp.zeros((rows.size, ref.shape[1]), BF16)

        flow.emit(dtok_refs[p])
        dgain = part_ref[...]
        here = pl.ds(0, size)
        news = (
            dot(dscore_ref[here, :], k_refs[p][...], TN),
            dot(low_ref[here, :], dkey_ref[here, :], TN),
            dot(low_ref[here, :], dval_ref[here, :], TN),
            dgain,
        )
        if p == 0:
            flow.need(*sums)
        for j, (ref, value) in enumerate(zip(totals, news)):
            if p == 0:
                ref[...] = value + sums[j][...] if sums else value
            else:
                ref[...] += value
    if not parts:
        return
    flow.need(lat_ref, gl_ref, wq_ref, dstate_ref, dwo_ref, dgmlp_ref)
    total = None
    width = wq_ref.shape[0]
    for first, size in cuts(lat_ref.shape[0], 256):
        rows = pl.ds(first, size)
        unit, inverse = norm_parts(lat_ref[rows, :].astype(F32))
        gain = gl_ref[...]
        latlow_ref[rows, :] = (unit * gain).astype(BF16)
        d_query = (dq_ref[rows, :] * scale).astype(BF16)
        dquery_ref[rows, :] = d_query
        d_low = dot(d_query, wq_ref[...], NT)
        line_store(dlat_ref, parts, info_ref[1 + 3 * count], first, (dstate_ref[rows, :] + norm_back(d_low, unit, inverse, gain)).astype(BF16))
        part = fold(d_low * unit)
        total = part if total is None else total + part
    flow.emit(dlat_ref)
    d_wq = dot(latlow_ref[...], dquery_ref[...], TN)
    gains = [jnp.sum(g, axis=0, keepdims=True) for g in (total, dgain_ref[...], dgmlp_ref[...])]
    line = lax.broadcasted_iota(jnp.int32, (extra, width), 0)
    block = jnp.where(line == 0, gains[0], jnp.where(line == 1, gains[1], jnp.where(line == 2, gains[2], 0.0)))
    halves = ((d_wq, akey_ref), (aval_ref, dwo_ref))
    for ref, core in ((keep_ref, info_ref[0]), (send_ref, 1 - info_ref[0])):
        ref[pl.ds(2 * width, extra), :] = block.astype(BF16)
        for h, half in enumerate(halves):

            @pl.when(core == h)
            def _(ref=ref, half=half):
                for j, piece in enumerate(half):
                    ref[pl.ds(j * width, width), :] = piece[...].astype(BF16)


def attention_back(info, q, wk, wv, gain, grads, values, weights, tokens, keys, sums, latents, parts, extra, scale):
    rows, width = q.shape
    square = ((width, width), F32)
    totals = [((rows, width), F32), square, square, ((8, width), F32)]
    most = max(k.shape[0] for k in keys)
    work = [((most, rows), BF16)] + [((most, width), BF16)] * 3 + [((8, width), F32)]
    outs = [(k.shape, BF16) for k in keys]
    by_piece = [a for piece in zip(values, weights, tokens, keys) for a in piece]
    args = (info, q, wk, wv, gain, *grads, *by_piece, *sums)
    if latents:
        args = (*args, *latents)
        outs += [((rows, width), BF16)] + [((2 * width + extra, width), BF16)] * 2
        work = totals + [((rows, width), BF16)] * 2 + work
    else:
        outs += totals
        parts = 0
    kernel = functools.partial(attention_back_kernel, len(keys), len(sums), parts, extra, scale)
    out = hbm_call(kernel, "attention_back", outs, args, 12, work, smem=1)
    return out[: len(keys)], out[len(keys) :]


def token_back_kernel(count, flow, tok_ref, gain_ref, *refs):
    flow.need(tok_ref, gain_ref, *refs[:count])
    for start, size in cuts(tok_ref.shape[0], 256):
        rows = pl.ds(start, size)
        unit, inverse = norm_parts(tok_ref[rows, :].astype(F32))
        total = refs[0][rows, :].astype(F32)
        for ref in refs[1:count]:
            total = total + ref[rows, :].astype(F32)
        refs[count][rows, :] = norm_back(total, unit, inverse, gain_ref[...])
        flow.emit(refs[count], rows)


def token_back(tok, gain, parts):
    args = (tok, gain, *parts)
    [out] = hbm_call(functools.partial(token_back_kernel, len(parts)), "token_back", [(tok.shape, F32)], args, 8, stores=len(cuts(tok.shape[0], 256)))
    return out


def picks(shape, scenes, scene, transposed=False):
    along = lax.broadcasted_iota(jnp.int32, shape, 1 if transposed else 0)
    across = lax.broadcasted_iota(jnp.int32, shape, 0 if transposed else 1)
    return jnp.where(across == along * scenes + scene, 1.0, 0.0).astype(BF16)


def sort_kernel(flow, info_ref, rows_ref, *out_refs):
    flow.need(rows_ref)
    for k, ref in enumerate(out_refs):
        take = picks((ref.shape[0], rows_ref.shape[0]), len(out_refs), info_ref[0] ^ k)
        ref[...] = dot(take, rows_ref[...]).astype(BF16)
        flow.emit(ref)


def sort_rows(info, value, scenes):
    rows, width = value.shape
    return hbm_call(sort_kernel, "sort_rows", [((rows // scenes, width), BF16)] * scenes, (info, value), 16, smem=1)


def unsort_kernel(scenes, flow, info_ref, *refs):
    *in_refs, out_ref = refs
    flow.need(*in_refs)
    if len(in_refs) == 1:
        size = out_ref.shape[0] // scenes
        in_refs = [in_refs[0].at[pl.ds(k * size, size)] for k in range(scenes)]
    rows, part = out_ref.shape[0], in_refs[0].shape[0]
    step = rows // scenes
    for start in range(0, rows, step):
        total = None
        for k, ref in enumerate(in_refs):
            some = part // scenes
            first = start // scenes
            put = picks((step, some), scenes, info_ref[0] ^ k, transposed=True)
            value = dot(put, ref[pl.ds(first, some), :])
            total = value if total is None else total + value
        out_ref[pl.ds(start, step), :] = total.astype(out_ref.dtype)
        flow.emit(out_ref, pl.ds(start, step))


def unsort_rows(info, parts, scenes, dtype):
    rows, width = sum(p.shape[0] for p in parts), parts[0].shape[1]
    kernel = functools.partial(unsort_kernel, scenes)
    [out] = hbm_call(kernel, "unsort_rows", [((rows, width), dtype)], (info, *parts), 16, smem=1, stores=scenes)
    return out


def split_kernel(count, place, extra, info_ref, *refs):
    in_refs, out_refs = refs[:count], refs[count:]
    rest = None
    if extra and out_refs[-1].shape[0] == extra and len(out_refs) == 2:
        *out_refs, rest = out_refs
    body = in_refs[0].shape[0] - extra
    step = body // len(out_refs)

    def total(start, rows):
        value = in_refs[0][pl.ds(start, rows), :].astype(F32)
        for ref in in_refs[1:]:
            value = value + ref[pl.ds(start, rows), :].astype(F32)
        return value.astype(BF16)

    shared = total(body, extra) if extra else None
    for k, ref in enumerate(out_refs):
        start = (info_ref[place] ^ k) * step if len(out_refs) > 1 else 0
        ref[pl.ds(0, step), :] = total(start if isinstance(start, int) else pl.multiple_of(start, 16), step)
        if extra and rest is None:
            ref[pl.ds(step, extra), :] = shared
    if rest is not None:
        rest[...] = shared


def split_sum(info, arrays, parts, place, extra):
    rows, width = arrays[0].shape
    step = (rows - extra) // parts
    if parts > 1:
        outs = [((step + extra, width), BF16)] * parts
    else:
        outs = [((step, width), BF16)] + ([((extra, width), BF16)] if extra else [])
    kernel = functools.partial(split_kernel, len(arrays), place, extra)
    return vmem_call(kernel, "split_sum", outs, (info, *arrays), 8, smem=1)


def unpack_kernel(width, count, crossed, info_ref, *refs):
    core, quad, line = info_ref[0], info_ref[1], info_ref[2]
    out_refs, (mine_ref, other_ref) = refs[2 * count : -2], refs[-2:]
    join(refs[:count], mine_ref)
    join(refs[count : 2 * count], other_ref)
    half = mine_ref.shape[0]
    lines = info_ref.shape[0] - 3
    block = half // (4 * lines)
    for h in range(2):
        for m in range(4):
            for z in range(lines):
                chip, spot = quad ^ m, line ^ z
                if crossed:
                    late = spot // (lines // 2)
                    chip = jnp.where(late == 0, chip, (chip % 2) * 2 + chip // 2)
                    spot = (late * 4 + chip) * (lines // 2) + spot % (lines // 2)
                else:
                    spot = chip * lines + spot
                rows = pl.ds(pl.multiple_of(spot * block, 16), block)
                value = jnp.where(core == h, mine_ref[rows, :].astype(F32), other_ref[rows, :].astype(F32))
                at = h * half + (m * lines + z) * block
                total = 0
                for ref in out_refs:
                    tall = ref.shape[0] * (ref.shape[1] // width)
                    if total <= at < total + tall:
                        inside = at - total
                        slab, row = inside // ref.shape[0], inside % ref.shape[0]
                        ref[pl.ds(row, block), pl.ds(slab * width, width)] = value
                    total += tall


class Sums:
    def __init__(self, seqs, blocks):
        self.seqs, self.blocks = seqs, blocks
        self.lines = blocks // 2
        seq, blk = lax.axis_index("seq"), lax.axis_index("blk")
        places = [seq % 2, (seq // 2) * 2 + blk % 2, blk // 2] + [seq * 0] * self.lines
        self.info = jnp.stack(places).astype(jnp.int32)

    def flip(self, value, seq_mask, blk_mask):
        pairs = [
            (s * self.blocks + b, (s ^ seq_mask) * self.blocks + (b ^ blk_mask))
            for s in range(self.seqs)
            for b in range(self.blocks)
        ]
        return lax.ppermute(value, ("seq", "blk"), pairs)

    def to_core(self, value):
        return self.flip(value, 1, 0)

    def to_quad(self, values):
        return [self.flip(v, 2 * (k // 2), k % 2) for k, v in enumerate(values, 1)]

    def to_line(self, values):
        return [self.flip(v, 0, 2 * k) for k, v in enumerate(values, 1)]

    def add_core(self, keep, received, extra=0):
        return split_sum(self.info, [keep, received], 4, 1, extra)

    def add_quad(self, keep, received, extra=0):
        return split_sum(self.info, [keep, *received], self.lines, 2, extra)

    def add_line(self, keep, received, extra=0):
        return split_sum(self.info, [keep, *received], 1, 0, extra)

    def unpack(self, mine, other, shapes, crossed=False):
        outs = [(shape, F32) for shape in shapes]
        rows, width = mine[0].shape
        kernel = functools.partial(unpack_kernel, width, len(mine), crossed)
        work = [((rows * len(mine), width), BF16)] * 2
        return vmem_call(kernel, "unpack", outs, (self.info, *mine, *other), 16, work, smem=1)


def after(value, *others):
    return lax.optimization_barrier((value, others))[0]


def local(
    sizes, latents, tokens, lengths, gain_lat, gain_tok, gain_mlp, w_query, w_key, w_value, w_out, w_up, w_down, d_out
):
    lat, tok, cot = latents[0], tokens[0], d_out[0]
    scene_lengths = lengths[0]
    scenes = scene_lengths.shape[0]
    seqs, blocks = sizes["seq"], sizes["blk"]
    group = blocks // scenes
    span, width = tok.shape
    hidden = w_up.shape[1]
    scale = width ** (-0.5)
    position = lax.axis_index("blk")
    scene, member = position // group, position % group
    scene_info = scene.astype(jnp.int32).reshape(1)
    gl, gt, gm = (g.reshape(1, width) for g in (gain_lat, gain_tok, gain_mlp))
    lines = [[m + group * k for k in range(scenes)] for m in range(group)]
    sums = Sums(seqs, blocks)

    def exchange(value, mask):
        return sums.flip(value, 0, mask)

    def across(values):
        return [exchange(v, group * k) if k else v for k, v in enumerate(values)]

    order = jnp.arange(scenes, dtype=jnp.int32)
    begin = jnp.sum(jnp.where(order < scene, scene_lengths, 0))
    end = begin + jnp.sum(jnp.where(order == scene, scene_lengths, 0))
    base = scene * group * span
    tail_rows = (scenes - 1) * group * span // 8
    starts = [base + (member ^ k) * span for k in [*range(1, group), 0]]
    main_info = jnp.stack([begin, end, *starts]).astype(jnp.int32)
    tail_info = jnp.stack([begin, end, base - tail_rows]).astype(jnp.int32)
    calls, size = [[0], []], 0
    for j in range(1, group + 1):
        if calls[-1] and size + span > 3 * span:
            calls.append([])
            size = 0
        calls[-1].append(j)
        size += span
    core = lax.axis_index("seq") % 2
    places = []
    for call in calls:
        spots = [v for j in call for v in (begin, end, (base - tail_rows, *starts)[j])]
        places.append(jnp.stack([core, *spots, scene]).astype(jnp.int32))

    lat_parts = sort_rows(scene_info, lat, scenes)
    others = [exchange(tok, k) for k in range(1, group)]
    lat_in = across(lat_parts)
    cot_parts = sort_rows(scene_info, after(cot, lat_parts), scenes)
    own_kv = keys_values(after(tok, cot_parts), gt, w_key, w_value)
    lat_in, others, cot_parts, own_kv, main_info, tail_info, places = lax.optimization_barrier(
        (lat_in, others, cot_parts, own_kv, main_info, tail_info, places)
    )
    cot_near = exchange(cot_parts[1], group)

    pieces = [tok, *others]
    lowest = (group * span - tail_rows) // span
    needed = []
    for owner in range(lowest, group):
        block = pieces[owner]
        for m in range(1, group):
            block = jnp.where(member == m, pieces[owner ^ m], block)
        needed.append(block)
    needed = jnp.concatenate(needed, axis=0) if len(needed) > 1 else needed[0]
    pairs = [(i, i + group) for i in range(blocks - group)]
    sent = needed[needed.shape[0] - tail_rows :]
    tail = lax.ppermute(sent, "blk", pairs)
    fresh = list(others) if group == 2 else []
    given = [own_kv] if fresh else [keys_values(piece, gt, w_key, w_value) for piece in others] + [own_kv]
    made_keys, made_values = zip(*given)
    query, acc, top, total, lat_set, weights, keys, values = attend(
        main_info, lat_in, gl, w_query, after(fresh, sent), gt, w_key, w_value, made_keys, made_values, scale
    )
    tail, query, cot_parts, cot_near = lax.optimization_barrier((tail, query, cot_parts, cot_near))

    cot_in = [cot_parts[0], cot_near, *[exchange(cot_parts[k], group * k) for k in range(2, scenes)]]
    saved, out_parts = finish(
        tail_info, scenes, lat_set, query, acc, top, total, tail, gt, w_key, w_value, gm, w_out, w_up, w_down, scale
    )
    tail_key, tail_value, tail_weight, factor, mixed, mlp, state, inner, slope = saved
    cot_in, out_parts, slope = lax.optimization_barrier((cot_in, out_parts, slope))
    out_back = across(out_parts)
    d_state, d_late, d_early, late, early_delta, keep, send, d_wo, dg_mlp = mlp_back(
        sums.info, cot_in, slope, state, mixed, mlp, inner, factor, gm, w_out, w_up, w_down
    )

    out_back, keep, send, d_early, d_late = lax.optimization_barrier((out_back, keep, send, d_early, d_late))
    received = sums.to_core(send)
    pieces = [(tail_value, tail_weight, tail, tail_key)]
    pieces += [(values[j], weights[j], piece, keys[j]) for j, piece in enumerate((*others, tok))]
    extra = 16
    d_toks, kept = [], []
    for j, call in enumerate(calls):
        some_values, some_weights, some_tokens, some_keys = zip(*[pieces[p] for p in call])
        latents = (lat_set, gl, w_query, d_state, d_wo, dg_mlp) if j == len(calls) - 1 else ()
        grads = (d_early, early_delta) if j else (d_late, late)
        some, kept = attention_back(
            places[j], query, w_key, w_value, gt, grads, some_values, some_weights, some_tokens, some_keys, kept,
            latents, scenes, extra, scale,
        )
        d_toks += some
        if j == 0:
            received, d_toks, kept = lax.optimization_barrier((received, d_toks, kept))
            keep, *sends = sums.add_core(keep, received)
            d_early = after(d_early, keep)
            received = sums.to_quad(sends)
            d_tail = lax.ppermute(d_toks[0], "blk", [(j, i) for i, j in pairs])
    received, d_tail, d_toks, kept = lax.optimization_barrier((received, d_tail, d_toks, kept))
    _, *returned, own = d_toks
    d_lat_set, small_keep, small_send = kept

    returned = dict(enumerate(returned, 1))
    own_tail = []
    for owner in range(lowest, group):
        start = owner * span - (group * span - tail_rows)
        chunk = d_tail[max(start, 0) : start + span]
        chunk = jnp.pad(chunk, ((span - chunk.shape[0], 0), (0, 0)))
        for k in range(1, group):
            returned[k] = returned[k] + jnp.where(member == owner ^ k, chunk, 0)
        own_tail.append(jnp.where(member == owner, chunk, 0))
    small_got = sums.to_core(small_send)
    keep, *sends = sums.add_quad(keep, received)
    received = sums.to_line(sends)
    returned = [exchange(after(returned[k], keep), k) for k in range(1, group)]
    output = unsort_rows(scene_info, after(out_back, keep), scenes, BF16)
    small_got, received, output = lax.optimization_barrier((small_got, received, output))
    [shard] = sums.add_line(keep, received)
    small_keep, *small_sends = sums.add_core(small_keep, small_got, extra)
    small_got = sums.to_quad(small_sends)
    block = shard
    for j in range(sums.lines.bit_length() - 1):
        far = sums.flip(block, 0, 2 << j)
        if j == sums.lines.bit_length() - 2:
            small_got, far = lax.optimization_barrier((small_got, far))
        block = jnp.concatenate([block, far], axis=0)
    half = block.shape[0] // 2
    near_a, near_b = block[:half], block[half:]
    far_a, far_b = sums.flip(near_a, 0, 1), sums.flip(near_b, 2, 0)
    small_keep, *small_sends = sums.add_quad(small_keep, small_got, extra)
    small_got = sums.to_line(small_sends)
    small_got, far_a, far_b, returned = lax.optimization_barrier((small_got, far_a, far_b, returned))
    two_a, two_b = jnp.concatenate([near_a, far_a], axis=0), jnp.concatenate([near_b, far_b], axis=0)
    last_a, last_b = sums.flip(two_a, 2, 0), sums.flip(two_b, 0, 1)
    small_shard, gains = sums.add_line(small_keep, small_got, extra)
    small_block = small_shard
    for j in range(sums.lines.bit_length() - 1):
        far = sums.flip(small_block, 0, 2 << j)
        if j == sums.lines.bit_length() - 2:
            leaving = after(d_lat_set, small_block)
            d_lat_back = lax.all_to_all(leaving, "blk", 0, 0, axis_index_groups=lines, tiled=True)
            d_tokens = token_back(tok, gt, [own, *own_tail, *after(returned, small_block)])
            far = after(far, d_tokens)
        small_block = jnp.concatenate([small_block, far], axis=0)
    last_a, last_b, small_block = lax.optimization_barrier((last_a, last_b, small_block))
    small_got = sums.to_quad([small_block] * 3)
    mine = [two_a, last_a, two_b, last_b]
    other = [sums.to_core(v) for v in mine]
    d_w_down, d_w_up = sums.unpack(mine, other, [(hidden, width), (width, hidden)], crossed=True)
    small_got, d_lat_back, d_w_up = lax.optimization_barrier((small_got, d_lat_back, d_w_up))
    small_mine = [small_block, *small_got]
    small_other = [sums.to_core(v) for v in small_mine]
    d_latents = unsort_rows(0 * scene_info, [after(d_lat_back, small_mine)], scenes, F32)
    squares = sums.unpack(small_mine, after(small_other, d_latents), [(width, width)] * 4)
    gains = gains.astype(F32)
    return (output[None], d_latents[None], d_tokens[None], *squares, d_w_up, d_w_down, gains[0], gains[1], gains[2])


def solution(mesh):
    split = P("seq", "blk", None)
    in_specs = (split, split, P("seq", None)) + (P(),) * 9 + (split,)
    out_specs = (split,) * 3 + (P(),) * 9
    return jax.shard_map(
        functools.partial(local, dict(mesh.shape)), mesh=mesh, in_specs=in_specs, out_specs=out_specs, check_vma=False
    )
```

profile of v0, /device:TPU:0, one launch (start us, length us, event | category | flops | bytes accessed | tf_op | source)
XLA Modules:
  0.0 277.1 jit_solution(14940040659012515244)
XLA Ops:
  0.6 3.0 %collective-permute-start.3 = (bf16[1024,512]{1,0:T(8,128)(2,1)}, bf16[1024,512]{1,0:T(8,128)(2,1)}, u32[]{:S(2)}, u32[]{:S(2)}) collective-permute-start(bf16[1024,512]{1,0:T(8,128)(2,1)} %bitcast.25), channel_id=1, source_target_pairs={{0,1},{1,0},{2,3},{3,2},{4,5},{5,4},{6,7},{7,6},{8,9},{9,8},{10,11... | collective-permute-start | bytes 3145736 | tf_op jit(solution)/shard_map/ppermute | solution.py:690
  3.7 3.2 %sort_rows.2 = (bf16[256,512]{1,0:T(8,128)(2,1)}, bf16[256,512]{1,0:T(8,128)(2,1)}, bf16[256,512]{1,0:T(8,128)(2,1)}, bf16[256,512]{1,0:T(8,128)(2,1)}) custom-call(s32[1]{0:T(128)} %bitcast.2.refs_0_, bf16[1024,512]{1,0:T(8,128)(2,1)} %bitcast.33), custom_call_target="tpu_custom_call" | custom-call | tf_op jit(solution)/shard_map/sort_rows/pallas_call | solution.py:140
  6.9 1.6 collective-permute-start
  8.5 2.6 collective-permute-start.1
  11.4 1.3 fusion.2
  12.7 3.2 %sort_rows.3 = (bf16[256,512]{1,0:T(8,128)(2,1)}, bf16[256,512]{1,0:T(8,128)(2,1)}, bf16[256,512]{1,0:T(8,128)(2,1)}, bf16[256,512]{1,0:T(8,128)(2,1)}) custom-call(s32[1]{0:T(128)} %bitcast.2.refs_0_, bf16[1024,512]{1,0:T(8,128)(2,1)} %bitcast.34), custom_call_target="tpu_custom_call" | custom-call | tf_op jit(solution)/shard_map/sort_rows/pallas_call | solution.py:140
  17.2 1.3 stack.65.refs_0_
  18.4 1.9 stack.66.refs_0_
  20.3 4.3 %keys_values.1 = (bf16[1024,512]{1,0:T(8,128)(2,1)}, bf16[1024,512]{1,0:T(8,128)(2,1)}) custom-call(bf16[1024,512]{1,0:T(8,128)(2,1)} %bitcast.26, f32[1,512]{1,0:T(1,128)} %bitcast.36, bf16[512,512]{1,0:T(8,128)(2,1)} %refs_2_.7, bf16[512,512]{1,0:T(8,128)(2,1)} %refs_3_.7), custom_call_target="tpu_custom_call" | custom-call | tf_op jit(solution)/shard_map/keys_values/pallas_call | solution.py:140
  24.6 1.3 pad_add_fusion.1.refs_0_
  25.9 1.3 pad_add_fusion.2.refs_0_
  27.2 3.1 %collective-permute-done.1.refs_9_ = bf16[256,512]{1,0:T(8,128)(2,1)} collective-permute-done((bf16[256,512]{1,0:T(8,128)(2,1)}, bf16[256,512]{1,0:T(8,128)(2,1)}, u32[]{:S(2)}, u32[]{:S(2)}) %collective-permute-start.1) | collective-permute-done | bytes 262176 | tf_op jit(solution)/shard_map/ppermute | solution.py:690
  30.2 2.3 slice_select_fusion
  32.6 7.5 %collective-permute-start.4 = (bf16[768,512]{1,0:T(8,128)(2,1)}, bf16[768,512]{1,0:T(8,128)(2,1)}, u32[]{:S(2)}, u32[]{:S(2)}) collective-permute-start(bf16[768,512]{1,0:T(8,128)(2,1)} %slice_select_fusion), channel_id=1, source_target_pairs={{0,2},{1,3},{2,4},{3,5},{4,6},{5,7},{8,10},{9,11},{10,12},{11,13},... | collective-permute-start | bytes 2359304 | tf_op jit(solution)/shard_map/ppermute | solution.py:788
  40.9 12.3 %attend.1 = (bf16[1024,512]{1,0:T(8,128)(2,1)}, f32[1024,512]{1,0:T(8,128)}, f32[8,1024]{1,0:T(8,128)}, f32[8,1024]{1,0:T(8,128)}, bf16[1024,512]{1,0:T(8,128)(2...) custom-call(s32[4]{0:T(128)} %pad_add_fusion.1.refs_0_, ...), custom_call_target="tpu_custom_call" | custom-call | tf_op jit(solution)/shard_map/attend/pallas_call | solution.py:140
  53.2 7.4 %collective-permute-done.5.refs_2_ = bf16[256,512]{1,0:T(8,128)(2,1)} collective-permute-done((bf16[256,512]{1,0:T(8,128)(2,1)}, bf16[256,512]{1,0:T(8,128)(2,1)}, u32[]{:S(2)}, u32[]{:S(2)}) %collective-permute-start.5) | collective-permute-done | bytes 262176 | tf_op jit(solution)/shard_map/ppermute | solution.py:690
  61.5 4.0 %collective-permute-start.7 = (bf16[256,512]{1,0:T(8,128)(2,1)}, bf16[256,512]{1,0:T(8,128)(2,1)}, u32[]{:S(2)}, u32[]{:S(2)}) collective-permute-start(bf16[256,512]{1,0:T(8,128)(2,1)} %get-tuple-element.209), channel_id=1, source_target_pairs={{0,6},{1,7},{2,4},{3,5},{4,2},{5,3},{6,0},{7,1},{8,14},{9,15},{10,... | collective-permute-start | bytes 786440 | tf_op jit(solution)/shard_map/ppermute | solution.py:690
  65.5 18.4 %finish.1 = (bf16[768,512]{1,0:T(8,128)(2,1)}, bf16[768,512]{1,0:T(8,128)(2,1)}, bf16[768,1024]{1,0:T(8,128)(2,1)}, f32[1024,128]{1,0:T(8,128)}, bf16[1024,512]{...) custom-call(s32[3]{0:T(128)} %pad_add_fusion.2.refs_0_, ...), custom_call_target="tpu_custom_call" | custom-call | tf_op jit(solution)/shard_map/finish/pallas_call | solution.py:140
  84.6 1.5 collective-permute-start.9
  86.1 2.3 collective-permute-start.10
  89.0 21.1 %mlp_back.1 = (f32[1024,512]{1,0:T(8,128)}, bf16[1024,512]{1,0:T(8,128)(2,1)}, bf16[1024,512]{1,0:T(8,128)(2,1)}, f32[8,1024]{1,0:T(8,128)}, f32[8,1024]{1,0:T(8...) custom-call(s32[7]{0:T(128)} %pad_add_fusion.refs_0_.info_ref, ...), custom_call_target="tpu_custom_call" | custom-call | tf_op jit(solution)/shard_map/mlp_back/pallas_call | solution.py:140
  110.3 7.3 %attention_back.2 = (bf16[768,512]{1,0:T(8,128)(2,1)}, f32[1024,512]{1,0:T(8,128)}, f32[512,512]{1,0:T(8,128)}, f32[512,512]{1,0:T(8,128)}, f32[8,512]{1,0:T(8,128)}) custom-call(s32[5]{0:T(128)} %stack.65.refs_0_, bf16[1024,512]{1,0:T(8,128)(2,1)} %get-tuple-element.213.refs_6_.refs_1_, bf16[512,512]{1,0:T(8,128)(2,1)} %refs_2_.7, ...), custom_call_target="tpu_custom_call" | custom-call | tf_op jit(solution)/shard_map/attention_back/pallas_call | solution.py:140
  117.6 1.5 collective-permute-start.15
  119.2 1.6 copy-done
  120.7 3.1 %split_sum.6 = (bf16[512,512]{1,0:T(8,128)(2,1)S(1)}, bf16[512,512]{1,0:T(8,128)(2,1)}, bf16[512,512]{1,0:T(8,128)(2,1)}, bf16[512,512]{1,0:T(8,128)(2,1)}) custom-call(s32[7]{0:T(128)S(1)} %copy-done.6, bf16[2048,512]{1,0:T(8,128)(2,1)S(1)} %copy-done, bf16[2048,512]{1,0:T(8,128)(2,1)} %collective-permute-done.11.refs_1_), custom_call_target="tpu_custom_call" | custom-call | tf_op jit(solution)/shard_map/split_sum/pallas_call | solution.py:46
  125.2 1.5 collective-permute-start.13
  126.6 1.5 collective-permute-start.14
  128.1 23.6 %attention_back.3 = (bf16[1024,512]{1,0:T(8,128)(2,1)}, bf16[1024,512]{1,0:T(8,128)(2,1)}, bf16[1024,512]{1,0:T(8,128)(2,1)}, bf16[1040,512]{1,0:T(8,128)(2,1)}, bf16[1040,512]{1,0:T(8,128)(2,1)}) custom-call(s32[8]{0:T(128)} %stack.66.refs_0_, bf16[1024,512]{1,0:T(8,128)(2,1)} %get-tuple-element.213.refs_6_.refs_1_, bf16[512,512]{1,0:T(8,128)(2,1)} %refs_2_.7, ...), custom_call_target="tpu_custom_call" | custom-call | tf_op jit(solution)/shard_map/attention_back/pallas_call | solution.py:140
  152.7 1.0 copy-done.3
  153.8 2.3 split_sum.7
  156.8 2.8 %pad_select_fusion = (bf16[1024,512]{1,0:T(8,128)(2,1)}, bf16[1024,512]{1,0:T(8,128)(2,1)}) fusion(bf16[768,512]{1,0:T(8,128)(2,1)} %collective-permute-done.15, pred[]{:T(512)S(6)} %eq.16, bf16[1024,512]{1,0:T(8,128)(2,1)S(1)} %copy-done.7, pred[]{:T(512)S(6)} %eq.18), kind=kLoop, calls=%fused_computation | loop fusion | flops 3145728 | bytes 3932162 | tf_op jit(solution)/shard_map/jit(_where)/select_n | solution.py:841
  160.1 1.7 collective-permute-start.17
  161.9 4.5 %collective-permute-start.18 = (bf16[128,512]{1,0:T(8,128)(2,1)}, bf16[128,512]{1,0:T(8,128)(2,1)}, u32[]{:S(2)}, u32[]{:S(2)}) collective-permute-start(bf16[128,512]{1,0:T(8,128)(2,1)} %get-tuple-element.284), channel_id=1, source_target_pairs={{0,4},{1,5},{2,6},{3,7},{4,0},{5,1},{6,2},{7,3},{8,12},{9,13},{10,... | collective-permute-start | bytes 393224 | tf_op jit(solution)/shard_map/ppermute | solution.py:690
  166.4 3.2 %unsort_rows.2 = bf16[1024,512]{1,0:T(8,128)(2,1)} custom-call(s32[1]{0:T(128)} %bitcast.2.refs_0_, bf16[256,512]{1,0:T(8,128)(2,1)} %get-tuple-element.291.refs_1_, bf16[256,512]{1,0:T(8,128)(2,1)} %collective-permute-done.8.refs_2_, bf16[256,512]{1,0:T(8,128)(2,1)} %collective-permute-done.9.refs_3_, bf16[256,512]{1,0:T(8,128)(2,1)} %collective-permute-done.10.refs_4_), custom_call_target="tpu_custom_call" | custom-call | tf_op jit(solution)/shard_map/unsort_rows/pallas_call | solution.py:140
  169.6 7.0 %collective-permute-done.18.refs_2_ = bf16[128,512]{1,0:T(8,128)(2,1)} collective-permute-done((bf16[128,512]{1,0:T(8,128)(2,1)}, bf16[128,512]{1,0:T(8,128)(2,1)}, u32[]{:S(2)}, u32[]{:S(2)}) %collective-permute-start.18) | collective-permute-done | bytes 131104 | tf_op jit(solution)/shard_map/ppermute | solution.py:690
  177.5 1.1 split_sum.8
  178.7 2.7 collective-permute-start.20
  181.4 1.2 copy-done.1
  182.6 1.5 split_sum.9
  184.1 1.6 collective-permute-start.21
  185.7 1.5 collective-permute-start.22
  187.7 1.0 collective-permute-start.24
  188.7 4.2 %collective-permute-done.21.refs_1_ = bf16[272,512]{1,0:T(8,128)(2,1)S(1)} collective-permute-done((bf16[272,512]{1,0:T(8,128)(2,1)S(1)}, bf16[272,512]{1,0:T(8,128)(2,1)S(1)}, u32[]{:S(2)}, u32[]{:S(2)}) %collective-permute-start.21) | collective-permute-done | bytes 278560 | tf_op jit(solution)/shard_map/ppermute | solution.py:690
  192.9 1.5 collective-permute-start.28
  195.3 3.8 %collective-permute-done.23.refs_3_ = bf16[272,512]{1,0:T(8,128)(2,1)S(1)} collective-permute-done((bf16[272,512]{1,0:T(8,128)(2,1)S(1)}, bf16[272,512]{1,0:T(8,128)(2,1)S(1)}, u32[]{:S(2)}, u32[]{:S(2)}) %collective-permute-start.23) | collective-permute-done | bytes 278560 | tf_op jit(solution)/shard_map/ppermute | solution.py:690
  199.1 1.4 collective-permute-done.24
  200.5 1.5 collective-permute-start.29
  202.8 3.6 %collective-permute-start.26 = (bf16[80,512]{1,0:T(8,128)(2,1)S(1)}, bf16[80,512]{1,0:T(8,128)(2,1)S(1)}, u32[]{:S(2)}, u32[]{:S(2)}) collective-permute-start(bf16[80,512]{1,0:T(8,128)(2,1)S(1)} %get-tuple-element.309), channel_id=1, source_target_pairs={{0,4},{1,5},{2,6},{3,7},{4,0},{5,1},{6,2},{7,3},{8,12},{9,13},{10,... | collective-permute-start | bytes 245768 | tf_op jit(solution)/shard_map/ppermute | solution.py:690
  207.9 3.7 %collective-permute-done.26.refs_2_ = bf16[80,512]{1,0:T(8,128)(2,1)S(1)} collective-permute-done((bf16[80,512]{1,0:T(8,128)(2,1)S(1)}, bf16[80,512]{1,0:T(8,128)(2,1)S(1)}, u32[]{:S(2)}, u32[]{:S(2)}) %collective-permute-start.26) | collective-permute-done | bytes 81952 | tf_op jit(solution)/shard_map/ppermute | solution.py:690
  211.6 1.2 collective-permute-done.27.refs_3_
  213.4 1.2 collective-permute-start.33
  215.2 2.5 collective-permute-done.33
  218.3 4.4 %all-to-all-start = ((bf16[4,256,512]{2,1,0:T(8,128)(2,1)}), bf16[4,256,512]{2,1,0:T(8,128)(2,1)}, u32[]{:S(2)}, u32[]{:S(2)}) async-start(bf16[4,256,512]{2,1,0:T(8,128)(2,1)} %bitcast.35), calls=%async_computation | async-start | bytes 2097152 | tf_op jit(solution)/shard_map/all_to_all | solution.py:871
  224.2 1.5 collective-permute-start.32
  227.6 2.9 %collective-permute-start.34 = (bf16[128,512]{1,0:T(8,128)(2,1)}, bf16[128,512]{1,0:T(8,128)(2,1)}, u32[]{:S(2)}, u32[]{:S(2)}) collective-permute-start(bf16[128,512]{1,0:T(8,128)(2,1)} %constant_dynamic-update-slice_fusion.2), channel_id=1, source_target_pairs={{0,4},{1,5},{2,6},{3,7},{4,0},{5,1},{6,2},{7,3},{8,12},{9,13},{10,... | collective-permute-start | bytes 393224 | tf_op jit(solution)/shard_map/ppermute | solution.py:690
  230.5 4.5 %token_back.1 = f32[1024,512]{1,0:T(8,128)} custom-call(bf16[1024,512]{1,0:T(8,128)(2,1)} %bitcast.29, f32[1,512]{1,0:T(1,128)} %bitcast.41, bf16[1024,512]{1,0:T(8,128)(2,1)} %get-tuple-element.322.refs_2_, bf16[1024,512]{1,0:T(8,128)(2,1)} %get-tuple-element.350.refs_3_, bf16[1024,512]{1,0:T(8,128)(2,1)} %collective-permute-done.30.refs_4_), custom_call_target="tpu_custom_call" | custom-call | tf_op jit(solution)/shard_map/token_back/pallas_call | solution.py:140
  235.0 16.3 %collective-permute-done.34 = bf16[128,512]{1,0:T(8,128)(2,1)} collective-permute-done((bf16[128,512]{1,0:T(8,128)(2,1)}, bf16[128,512]{1,0:T(8,128)(2,1)}, u32[]{:S(2)}, u32[]{:S(2)}) %collective-permute-start.34) | collective-permute-done | bytes 131104 | tf_op jit(solution)/shard_map/ppermute | solution.py:690
  251.3 1.6 pad_maximum_fusion.2.refs_0_
  253.5 1.5 collective-permute-start.37
  255.0 1.5 collective-permute-start.36
  257.0 6.6 %unpack.2 = (f32[2048,512]{1,0:T(8,128)}, f32[512,2048]{1,0:T(8,128)}) custom-call(s32[7]{0:T(128)S(1)} %copy-done.6, bf16[512,512]{1,0:T(8,128)(2,1)} %pad_maximum_fusion.refs_0_, bf16[512,512]{1,0:T(8,128)(2,1)} %collective-permute-done.31.refs_1_, bf16[512,512]{1,0:T(8,128)(2,1)} %constant_dynamic-update-slice_fusion.refs_2_, ...), custom_call_target="tpu_custom_call" | custom-call | tf_op jit(solution)/shard_map/unpack/pallas_call | solution.py:46
  263.9 4.8 %collective-permute-done.36.refs_2_ = bf16[256,512]{1,0:T(8,128)(2,1)} collective-permute-done((bf16[256,512]{1,0:T(8,128)(2,1)}, bf16[256,512]{1,0:T(8,128)(2,1)}, u32[]{:S(2)}, u32[]{:S(2)}) %collective-permute-start.36) | collective-permute-done | bytes 262176 | tf_op jit(solution)/shard_map/ppermute | solution.py:690
  269.9 3.3 %unsort_rows.3 = f32[1024,512]{1,0:T(8,128)} custom-call(s32[1]{0:T(128)} %constant.61.clone.1.refs_0_, bf16[1024,512]{1,0:T(8,128)(2,1)} %bitcast.17.refs_1_), custom_call_target="tpu_custom_call" | custom-call | tf_op jit(solution)/shard_map/unsort_rows/pallas_call | solution.py:140
  273.2 3.8 %unpack.3 = (f32[512,512]{1,0:T(8,128)}, f32[512,512]{1,0:T(8,128)}, f32[512,512]{1,0:T(8,128)}, f32[512,512]{1,0:T(8,128)}) custom-call(s32[7]{0:T(128)S(1)} %copy-done.6, bf16[256,512]{1,0:T(8,128)(2,1)} %pad_maximum_fusion.2.refs_0_, bf16[256,512]{1,0:T(8,128)(2,1)} %collective-permute-done.35.refs_1_, bf16[256,512]{1,0:T(8,128)(2,1)} %collective-permute-done.36.refs_2_, ...), custom_call_target="tpu_custom_call" | custom-call | tf_op jit(solution)/shard_map/unpack/pallas_call | solution.py:46
  (84 shorter events, 18.8 us)
Async XLA Ops:
  0.6 29.6 %collective-permute-start.3 = (bf16[1024,512]{1,0:T(8,128)(2,1)}, bf16[1024,512]{1,0:T(8,128)(2,1)}, u32[]{:S(2)}, u32[]{:S(2)}) collective-permute-start(bf16[1024,512]{1,0:T(8,128)(2,1)} %bitcast.25), channel_id=1, source_target_pairs={{0,1},{1,0},{2,3},{3,2},{4,5},{5,4},{6,7},{7,6},{8,9},{9,8},{10,11... | collective-permute-start | bytes 3145736 | tf_op jit(solution)/shard_map/ppermute | solution.py:690
  6.9 20.3 %collective-permute-start = (bf16[256,512]{1,0:T(8,128)(2,1)}, bf16[256,512]{1,0:T(8,128)(2,1)}, u32[]{:S(2)}, u32[]{:S(2)}) collective-permute-start(bf16[256,512]{1,0:T(8,128)(2,1)} %get-tuple-element.181), channel_id=1, source_target_pairs={{0,2},{1,3},{2,0},{3,1},{4,6},{5,7},{6,4},{7,5},{8,10},{9,11},{10,... | collective-permute-start | bytes 786440 | tf_op jit(solution)/shard_map/ppermute | solution.py:690
  8.5 21.7 %collective-permute-start.1 = (bf16[256,512]{1,0:T(8,128)(2,1)}, bf16[256,512]{1,0:T(8,128)(2,1)}, u32[]{:S(2)}, u32[]{:S(2)}) collective-permute-start(bf16[256,512]{1,0:T(8,128)(2,1)} %get-tuple-element.182), channel_id=1, source_target_pairs={{0,4},{1,5},{2,6},{3,7},{4,0},{5,1},{6,2},{7,3},{8,12},{9,13},{10,... | collective-permute-start | bytes 786440 | tf_op jit(solution)/shard_map/ppermute | solution.py:690
  11.1 19.1 %collective-permute-start.2 = (bf16[256,512]{1,0:T(8,128)(2,1)}, bf16[256,512]{1,0:T(8,128)(2,1)}, u32[]{:S(2)}, u32[]{:S(2)}) collective-permute-start(bf16[256,512]{1,0:T(8,128)(2,1)} %get-tuple-element.183), channel_id=1, source_target_pairs={{0,6},{1,7},{2,4},{3,5},{4,2},{5,3},{6,0},{7,1},{8,14},{9,15},{10,... | collective-permute-start | bytes 786440 | tf_op jit(solution)/shard_map/ppermute | solution.py:690
  32.6 28.1 %collective-permute-start.4 = (bf16[768,512]{1,0:T(8,128)(2,1)}, bf16[768,512]{1,0:T(8,128)(2,1)}, u32[]{:S(2)}, u32[]{:S(2)}) collective-permute-start(bf16[768,512]{1,0:T(8,128)(2,1)} %slice_select_fusion), channel_id=1, source_target_pairs={{0,2},{1,3},{2,4},{3,5},{4,6},{5,7},{8,10},{9,11},{10,12},{11,13},... | collective-permute-start | bytes 2359304 | tf_op jit(solution)/shard_map/ppermute | solution.py:788
  40.1 20.6 %collective-permute-start.5 = (bf16[256,512]{1,0:T(8,128)(2,1)}, bf16[256,512]{1,0:T(8,128)(2,1)}, u32[]{:S(2)}, u32[]{:S(2)}) collective-permute-start(bf16[256,512]{1,0:T(8,128)(2,1)} %get-tuple-element.203), channel_id=1, source_target_pairs={{0,2},{1,3},{2,0},{3,1},{4,6},{5,7},{6,4},{7,5},{8,10},{9,11},{10,... | collective-permute-start | bytes 786440 | tf_op jit(solution)/shard_map/ppermute | solution.py:690
  60.7 23.3 %collective-permute-start.6 = (bf16[256,512]{1,0:T(8,128)(2,1)}, bf16[256,512]{1,0:T(8,128)(2,1)}, u32[]{:S(2)}, u32[]{:S(2)}) collective-permute-start(bf16[256,512]{1,0:T(8,128)(2,1)} %get-tuple-element.208), channel_id=1, source_target_pairs={{0,4},{1,5},{2,6},{3,7},{4,0},{5,1},{6,2},{7,3},{8,12},{9,13},{10,... | collective-permute-start | bytes 786440 | tf_op jit(solution)/shard_map/ppermute | solution.py:690
  61.5 22.4 %collective-permute-start.7 = (bf16[256,512]{1,0:T(8,128)(2,1)}, bf16[256,512]{1,0:T(8,128)(2,1)}, u32[]{:S(2)}, u32[]{:S(2)}) collective-permute-start(bf16[256,512]{1,0:T(8,128)(2,1)} %get-tuple-element.209), channel_id=1, source_target_pairs={{0,6},{1,7},{2,4},{3,5},{4,2},{5,3},{6,0},{7,1},{8,14},{9,15},{10,... | collective-permute-start | bytes 786440 | tf_op jit(solution)/shard_map/ppermute | solution.py:690
  84.0 26.2 %collective-permute-start.8 = (bf16[256,512]{1,0:T(8,128)(2,1)}, bf16[256,512]{1,0:T(8,128)(2,1)}, u32[]{:S(2)}, u32[]{:S(2)}) collective-permute-start(bf16[256,512]{1,0:T(8,128)(2,1)} %get-tuple-element.223), channel_id=1, source_target_pairs={{0,2},{1,3},{2,0},{3,1},{4,6},{5,7},{6,4},{7,5},{8,10},{9,11},{10,... | collective-permute-start | bytes 786440 | tf_op jit(solution)/shard_map/ppermute | solution.py:690
  84.6 25.6 %collective-permute-start.9 = (bf16[256,512]{1,0:T(8,128)(2,1)}, bf16[256,512]{1,0:T(8,128)(2,1)}, u32[]{:S(2)}, u32[]{:S(2)}) collective-permute-start(bf16[256,512]{1,0:T(8,128)(2,1)} %get-tuple-element.224), channel_id=1, source_target_pairs={{0,4},{1,5},{2,6},{3,7},{4,0},{5,1},{6,2},{7,3},{8,12},{9,13},{10,... | collective-permute-start | bytes 786440 | tf_op jit(solution)/shard_map/ppermute | solution.py:690
  86.1 24.1 %collective-permute-start.10 = (bf16[256,512]{1,0:T(8,128)(2,1)}, bf16[256,512]{1,0:T(8,128)(2,1)}, u32[]{:S(2)}, u32[]{:S(2)}) collective-permute-start(bf16[256,512]{1,0:T(8,128)(2,1)} %get-tuple-element.225), channel_id=1, source_target_pairs={{0,6},{1,7},{2,4},{3,5},{4,2},{5,3},{6,0},{7,1},{8,14},{9,15},{10,... | collective-permute-start | bytes 786440 | tf_op jit(solution)/shard_map/ppermute | solution.py:690
  110.2 7.4 %collective-permute-start.11 = (bf16[2048,512]{1,0:T(8,128)(2,1)}, bf16[2048,512]{1,0:T(8,128)(2,1)}, u32[]{:S(2)}, u32[]{:S(2)}) collective-permute-start(bf16[2048,512]{1,0:T(8,128)(2,1)} %get-tuple-element.241), channel_id=1, source_target_pairs={{0,8},{1,9},{2,10},{3,11},{4,12},{5,13},{6,14},{7,15},{8,0},{9,1},... | collective-permute-start | bytes 6291464 | tf_op jit(solution)/shard_map/ppermute | solution.py:690
  110.3 8.9 %copy-start.6 = (s32[7]{0:T(128)S(1)}, s32[7]{0:T(128)}, u32[]{:S(2)}) copy-start(s32[7]{0:T(128)} %pad_add_fusion.refs_0_.info_ref) | copy-start | bytes 88
  117.6 34.1 %collective-permute-start.15 = (bf16[768,512]{1,0:T(8,128)(2,1)}, bf16[768,512]{1,0:T(8,128)(2,1)}, u32[]{:S(2)}, u32[]{:S(2)}) collective-permute-start(bf16[768,512]{1,0:T(8,128)(2,1)} %get-tuple-element.257), channel_id=1, source_target_pairs={{2,0},{3,1},{4,2},{5,3},{6,4},{7,5},{10,8},{11,9},{12,10},{13,11},... | collective-permute-start | bytes 2359304 | tf_op jit(solution)/shard_map/ppermute | solution.py:828
  119.1 1.6 copy-start
  123.8 0.8 copy-start.2
  124.6 27.1 %collective-permute-start.12 = (bf16[512,512]{1,0:T(8,128)(2,1)}, bf16[512,512]{1,0:T(8,128)(2,1)}, u32[]{:S(2)}, u32[]{:S(2)}) collective-permute-start(bf16[512,512]{1,0:T(8,128)(2,1)} %get-tuple-element.254), channel_id=1, source_target_pairs={{0,1},{1,0},{2,3},{3,2},{4,5},{5,4},{6,7},{7,6},{8,9},{9,8},{10,11... | collective-permute-start | bytes 1572872 | tf_op jit(solution)/shard_map/ppermute | solution.py:690
  125.2 26.5 %collective-permute-start.13 = (bf16[512,512]{1,0:T(8,128)(2,1)}, bf16[512,512]{1,0:T(8,128)(2,1)}, u32[]{:S(2)}, u32[]{:S(2)}) collective-permute-start(bf16[512,512]{1,0:T(8,128)(2,1)} %get-tuple-element.255), channel_id=1, source_target_pairs={{0,16},{1,17},{2,18},{3,19},{4,20},{5,21},{6,22},{7,23},{8,24},{9,... | collective-permute-start | bytes 1572872 | tf_op jit(solution)/shard_map/ppermute | solution.py:690
  126.6 25.1 %collective-permute-start.14 = (bf16[512,512]{1,0:T(8,128)(2,1)}, bf16[512,512]{1,0:T(8,128)(2,1)}, u32[]{:S(2)}, u32[]{:S(2)}) collective-permute-start(bf16[512,512]{1,0:T(8,128)(2,1)} %get-tuple-element.256), channel_id=1, source_target_pairs={{0,17},{1,16},{2,19},{3,18},{4,21},{5,20},{6,23},{7,22},{8,25},{9,... | collective-permute-start | bytes 1572872 | tf_op jit(solution)/shard_map/ppermute | solution.py:690
  151.7 24.9 %collective-permute-start.16 = (bf16[1040,512]{1,0:T(8,128)(2,1)}, bf16[1040,512]{1,0:T(8,128)(2,1)}, u32[]{:S(2)}, u32[]{:S(2)}) collective-permute-start(bf16[1040,512]{1,0:T(8,128)(2,1)} %get-tuple-element.279), channel_id=1, source_target_pairs={{0,8},{1,9},{2,10},{3,11},{4,12},{5,13},{6,14},{7,15},{8,0},{9,1},... | collective-permute-start | bytes 3194888 | tf_op jit(solution)/shard_map/ppermute | solution.py:690
  152.7 1.0 copy-start.3
  153.8 3.0 %copy-start.7 = (bf16[1024,512]{1,0:T(8,128)(2,1)S(1)}, bf16[1024,512]{1,0:T(8,128)(2,1)}, u32[]{:S(2)}) copy-start(bf16[1024,512]{1,0:T(8,128)(2,1)} %get-tuple-element.312) | copy-start | bytes 3145732
  156.1 0.7 copy-start.4
  159.6 46.8 %collective-permute-start.30 = (bf16[1024,512]{1,0:T(8,128)(2,1)}, bf16[1024,512]{1,0:T(8,128)(2,1)}, u32[]{:S(2)}, u32[]{:S(2)}) collective-permute-start(bf16[1024,512]{1,0:T(8,128)(2,1)} %get-tuple-element.314), channel_id=1, source_target_pairs={{0,1},{1,0},{2,3},{3,2},{4,5},{5,4},{6,7},{7,6},{8,9},{9,8},{10,11... | collective-permute-start | bytes 3145736 | tf_op jit(solution)/shard_map/ppermute | solution.py:690
  160.1 9.5 %collective-permute-start.17 = (bf16[128,512]{1,0:T(8,128)(2,1)}, bf16[128,512]{1,0:T(8,128)(2,1)}, u32[]{:S(2)}, u32[]{:S(2)}) collective-permute-start(bf16[128,512]{1,0:T(8,128)(2,1)} %get-tuple-element.283), channel_id=1, source_target_pairs={{0,2},{1,3},{2,0},{3,1},{4,6},{5,7},{6,4},{7,5},{8,10},{9,11},{10,... | collective-permute-start | bytes 393224 | tf_op jit(solution)/shard_map/ppermute | solution.py:690
  161.9 14.8 %collective-permute-start.18 = (bf16[128,512]{1,0:T(8,128)(2,1)}, bf16[128,512]{1,0:T(8,128)(2,1)}, u32[]{:S(2)}, u32[]{:S(2)}) collective-permute-start(bf16[128,512]{1,0:T(8,128)(2,1)} %get-tuple-element.284), channel_id=1, source_target_pairs={{0,4},{1,5},{2,6},{3,7},{4,0},{5,1},{6,2},{7,3},{8,12},{9,13},{10,... | collective-permute-start | bytes 393224 | tf_op jit(solution)/shard_map/ppermute | solution.py:690
  166.4 10.2 %collective-permute-start.19 = (bf16[128,512]{1,0:T(8,128)(2,1)}, bf16[128,512]{1,0:T(8,128)(2,1)}, u32[]{:S(2)}, u32[]{:S(2)}) collective-permute-start(bf16[128,512]{1,0:T(8,128)(2,1)} %get-tuple-element.285), channel_id=1, source_target_pairs={{0,6},{1,7},{2,4},{3,5},{4,2},{5,3},{6,0},{7,1},{8,14},{9,15},{10,... | collective-permute-start | bytes 393224 | tf_op jit(solution)/shard_map/ppermute | solution.py:690
  176.6 0.9 copy-start.5
  178.7 9.0 %collective-permute-start.20 = (bf16[128,512]{1,0:T(8,128)(2,1)S(1)}, bf16[128,512]{1,0:T(8,128)(2,1)S(1)}, u32[]{:S(2)}, u32[]{:S(2)}) collective-permute-start(bf16[128,512]{1,0:T(8,128)(2,1)S(1)} %split_sum.8), channel_id=1, source_target_pairs={{0,2},{1,3},{2,0},{3,1},{4,6},{5,7},{6,4},{7,5},{8,10},{9,11},{10,... | collective-permute-start | bytes 393224 | tf_op jit(solution)/shard_map/ppermute | solution.py:690
  181.4 1.2 copy-start.1
  184.1 8.9 %collective-permute-start.21 = (bf16[272,512]{1,0:T(8,128)(2,1)S(1)}, bf16[272,512]{1,0:T(8,128)(2,1)S(1)}, u32[]{:S(2)}, u32[]{:S(2)}) collective-permute-start(bf16[272,512]{1,0:T(8,128)(2,1)S(1)} %get-tuple-element.302), channel_id=1, source_target_pairs={{0,1},{1,0},{2,3},{3,2},{4,5},{5,4},{6,7},{7,6},{8,9},{9,8},{10,11... | collective-permute-start | bytes 835592 | tf_op jit(solution)/shard_map/ppermute | solution.py:690
  185.7 9.6 %collective-permute-start.22 = (bf16[272,512]{1,0:T(8,128)(2,1)S(1)}, bf16[272,512]{1,0:T(8,128)(2,1)S(1)}, u32[]{:S(2)}, u32[]{:S(2)}) collective-permute-start(bf16[272,512]{1,0:T(8,128)(2,1)S(1)} %get-tuple-element.303), channel_id=1, source_target_pairs={{0,16},{1,17},{2,18},{3,19},{4,20},{5,21},{6,22},{7,23},{8,24},{9,... | collective-permute-start | bytes 835592 | tf_op jit(solution)/shard_map/ppermute | solution.py:690
  187.2 11.9 %collective-permute-start.23 = (bf16[272,512]{1,0:T(8,128)(2,1)S(1)}, bf16[272,512]{1,0:T(8,128)(2,1)S(1)}, u32[]{:S(2)}, u32[]{:S(2)}) collective-permute-start(bf16[272,512]{1,0:T(8,128)(2,1)S(1)} %get-tuple-element.304), channel_id=1, source_target_pairs={{0,17},{1,16},{2,19},{3,18},{4,21},{5,20},{6,23},{7,22},{8,25},{9,... | collective-permute-start | bytes 835592 | tf_op jit(solution)/shard_map/ppermute | solution.py:690
  187.7 12.8 %collective-permute-start.24 = (bf16[256,512]{1,0:T(8,128)(2,1)S(1)}, bf16[256,512]{1,0:T(8,128)(2,1)S(1)}, u32[]{:S(2)}, u32[]{:S(2)}) collective-permute-start(bf16[256,512]{1,0:T(8,128)(2,1)S(1)} %pad_maximum_fusion.1), channel_id=1, source_target_pairs={{0,4},{1,5},{2,6},{3,7},{4,0},{5,1},{6,2},{7,3},{8,12},{9,13},{10,... | collective-permute-start | bytes 786440 | tf_op jit(solution)/shard_map/ppermute | solution.py:690
  192.9 14.2 %collective-permute-start.28 = (bf16[256,512]{1,0:T(8,128)(2,1)S(1)}, bf16[256,512]{1,0:T(8,128)(2,1)S(1)}, u32[]{:S(2)}, u32[]{:S(2)}) collective-permute-start(bf16[256,512]{1,0:T(8,128)(2,1)S(1)} %pad_maximum_fusion.1), channel_id=1, source_target_pairs={{0,1},{1,0},{2,3},{3,2},{4,5},{5,4},{6,7},{7,6},{8,9},{9,8},{10,11... | collective-permute-start | bytes 786440 | tf_op jit(solution)/shard_map/ppermute | solution.py:690
  200.5 12.3 %collective-permute-start.29 = (bf16[256,512]{1,0:T(8,128)(2,1)S(1)}, bf16[256,512]{1,0:T(8,128)(2,1)S(1)}, u32[]{:S(2)}, u32[]{:S(2)}) collective-permute-start(bf16[256,512]{1,0:T(8,128)(2,1)S(1)} %collective-permute-done.24), channel_id=1, source_target_pairs={{0,16},{1,17},{2,18},{3,19},{4,20},{5,21},{6,22},{7,23},{8,24},{9,... | collective-permute-start | bytes 786440 | tf_op jit(solution)/shard_map/ppermute | solution.py:690
  202.7 5.2 %collective-permute-start.25 = (bf16[80,512]{1,0:T(8,128)(2,1)S(1)}, bf16[80,512]{1,0:T(8,128)(2,1)S(1)}, u32[]{:S(2)}, u32[]{:S(2)}) collective-permute-start(bf16[80,512]{1,0:T(8,128)(2,1)S(1)} %get-tuple-element.308), channel_id=1, source_target_pairs={{0,2},{1,3},{2,0},{3,1},{4,6},{5,7},{6,4},{7,5},{8,10},{9,11},{10,... | collective-permute-start | bytes 245768 | tf_op jit(solution)/shard_map/ppermute | solution.py:690
  202.8 8.8 %collective-permute-start.26 = (bf16[80,512]{1,0:T(8,128)(2,1)S(1)}, bf16[80,512]{1,0:T(8,128)(2,1)S(1)}, u32[]{:S(2)}, u32[]{:S(2)}) collective-permute-start(bf16[80,512]{1,0:T(8,128)(2,1)S(1)} %get-tuple-element.309), channel_id=1, source_target_pairs={{0,4},{1,5},{2,6},{3,7},{4,0},{5,1},{6,2},{7,3},{8,12},{9,13},{10,... | collective-permute-start | bytes 245768 | tf_op jit(solution)/shard_map/ppermute | solution.py:690
  206.4 6.3 %collective-permute-start.27 = (bf16[80,512]{1,0:T(8,128)(2,1)S(1)}, bf16[80,512]{1,0:T(8,128)(2,1)S(1)}, u32[]{:S(2)}, u32[]{:S(2)}) collective-permute-start(bf16[80,512]{1,0:T(8,128)(2,1)S(1)} %get-tuple-element.310), channel_id=1, source_target_pairs={{0,6},{1,7},{2,4},{3,5},{4,2},{5,3},{6,0},{7,1},{8,14},{9,15},{10,... | collective-permute-start | bytes 245768 | tf_op jit(solution)/shard_map/ppermute | solution.py:690
  213.4 4.3 %collective-permute-start.33 = (bf16[64,512]{1,0:T(8,128)(2,1)S(1)}, bf16[64,512]{1,0:T(8,128)(2,1)S(1)}, u32[]{:S(2)}, u32[]{:S(2)}) collective-permute-start(bf16[64,512]{1,0:T(8,128)(2,1)S(1)} %get-tuple-element.321), channel_id=1, source_target_pairs={{0,2},{1,3},{2,0},{3,1},{4,6},{5,7},{6,4},{7,5},{8,10},{9,11},{10,... | collective-permute-start | bytes 196616 | tf_op jit(solution)/shard_map/ppermute | solution.py:690
  217.7 8.8 %copy-start.8 = (bf16[64,512]{1,0:T(8,128)(2,1)}, bf16[64,512]{1,0:T(8,128)(2,1)S(1)}, u32[]{:S(2)}) copy-start(bf16[64,512]{1,0:T(8,128)(2,1)S(1)} %collective-permute-done.33) | copy-start | bytes 196612
  218.3 50.3 %all-to-all-start = ((bf16[4,256,512]{2,1,0:T(8,128)(2,1)}), bf16[4,256,512]{2,1,0:T(8,128)(2,1)}, u32[]{:S(2)}, u32[]{:S(2)}) async-start(bf16[4,256,512]{2,1,0:T(8,128)(2,1)} %bitcast.35), calls=%async_computation | async-start | bytes 2097152 | tf_op jit(solution)/shard_map/all_to_all | solution.py:871
  224.2 28.8 %collective-permute-start.32 = (bf16[512,512]{1,0:T(8,128)(2,1)}, bf16[512,512]{1,0:T(8,128)(2,1)}, u32[]{:S(2)}, u32[]{:S(2)}) collective-permute-start(bf16[512,512]{1,0:T(8,128)(2,1)} %constant_dynamic-update-slice_fusion.refs_2_), channel_id=1, source_target_pairs={{0,1},{1,0},{2,3},{3,2},{4,5},{5,4},{6,7},{7,6},{8,9},{9,8},{10,11... | collective-permute-start | bytes 1572872 | tf_op jit(solution)/shard_map/ppermute | solution.py:690
  226.5 26.4 %collective-permute-start.31 = (bf16[512,512]{1,0:T(8,128)(2,1)}, bf16[512,512]{1,0:T(8,128)(2,1)}, u32[]{:S(2)}, u32[]{:S(2)}) collective-permute-start(bf16[512,512]{1,0:T(8,128)(2,1)} %pad_maximum_fusion.refs_0_), channel_id=1, source_target_pairs={{0,16},{1,17},{2,18},{3,19},{4,20},{5,21},{6,22},{7,23},{8,24},{9,... | collective-permute-start | bytes 1572872 | tf_op jit(solution)/shard_map/ppermute | solution.py:690
  227.1 27.9 %collective-permute-start.40 = (bf16[512,512]{1,0:T(8,128)(2,1)}, bf16[512,512]{1,0:T(8,128)(2,1)}, u32[]{:S(2)}, u32[]{:S(2)}) collective-permute-start(bf16[512,512]{1,0:T(8,128)(2,1)} %constant_dynamic-update-slice_fusion.refs_2_), channel_id=1, source_target_pairs={{0,8},{1,9},{2,10},{3,11},{4,12},{5,13},{6,14},{7,15},{8,0},{9,1},... | collective-permute-start | bytes 1572872 | tf_op jit(solution)/shard_map/ppermute | solution.py:690
  227.1 29.4 %collective-permute-start.38 = (bf16[512,512]{1,0:T(8,128)(2,1)}, bf16[512,512]{1,0:T(8,128)(2,1)}, u32[]{:S(2)}, u32[]{:S(2)}) collective-permute-start(bf16[512,512]{1,0:T(8,128)(2,1)} %pad_maximum_fusion.refs_0_), channel_id=1, source_target_pairs={{0,8},{1,9},{2,10},{3,11},{4,12},{5,13},{6,14},{7,15},{8,0},{9,1},... | collective-permute-start | bytes 1572872 | tf_op jit(solution)/shard_map/ppermute | solution.py:690
  227.6 23.7 %collective-permute-start.34 = (bf16[128,512]{1,0:T(8,128)(2,1)}, bf16[128,512]{1,0:T(8,128)(2,1)}, u32[]{:S(2)}, u32[]{:S(2)}) collective-permute-start(bf16[128,512]{1,0:T(8,128)(2,1)} %constant_dynamic-update-slice_fusion.2), channel_id=1, source_target_pairs={{0,4},{1,5},{2,6},{3,7},{4,0},{5,1},{6,2},{7,3},{8,12},{9,13},{10,... | collective-permute-start | bytes 393224 | tf_op jit(solution)/shard_map/ppermute | solution.py:690
  253.0 4.0 %collective-permute-start.39 = (bf16[512,512]{1,0:T(8,128)(2,1)}, bf16[512,512]{1,0:T(8,128)(2,1)S(1)}, u32[]{:S(2)}, u32[]{:S(2)}) collective-permute-start(bf16[512,512]{1,0:T(8,128)(2,1)} %collective-permute-done.31.refs_1_), channel_id=1, source_target_pairs={{0,8},{1,9},{2,10},{3,11},{4,12},{5,13},{6,14},{7,15},{8,0},{9,1},... | collective-permute-start | bytes 1572872 | tf_op jit(solution)/shard_map/ppermute | solution.py:690
  253.0 4.0 %collective-permute-start.41 = (bf16[512,512]{1,0:T(8,128)(2,1)}, bf16[512,512]{1,0:T(8,128)(2,1)S(1)}, u32[]{:S(2)}, u32[]{:S(2)}) collective-permute-start(bf16[512,512]{1,0:T(8,128)(2,1)} %collective-permute-done.32.refs_3_), channel_id=1, source_target_pairs={{0,8},{1,9},{2,10},{3,11},{4,12},{5,13},{6,14},{7,15},{8,0},{9,1},... | collective-permute-start | bytes 1572872 | tf_op jit(solution)/shard_map/ppermute | solution.py:690
  253.5 10.4 %collective-permute-start.37 = (bf16[256,512]{1,0:T(8,128)(2,1)}, bf16[256,512]{1,0:T(8,128)(2,1)}, u32[]{:S(2)}, u32[]{:S(2)}) collective-permute-start(bf16[256,512]{1,0:T(8,128)(2,1)} %pad_maximum_fusion.2.refs_0_), channel_id=1, source_target_pairs={{0,17},{1,16},{2,19},{3,18},{4,21},{5,20},{6,23},{7,22},{8,25},{9,... | collective-permute-start | bytes 786440 | tf_op jit(solution)/shard_map/ppermute | solution.py:690
  255.0 13.7 %collective-permute-start.36 = (bf16[256,512]{1,0:T(8,128)(2,1)}, bf16[256,512]{1,0:T(8,128)(2,1)}, u32[]{:S(2)}, u32[]{:S(2)}) collective-permute-start(bf16[256,512]{1,0:T(8,128)(2,1)} %pad_maximum_fusion.2.refs_0_), channel_id=1, source_target_pairs={{0,16},{1,17},{2,18},{3,19},{4,20},{5,21},{6,22},{7,23},{8,24},{9,... | collective-permute-start | bytes 786440 | tf_op jit(solution)/shard_map/ppermute | solution.py:690
  256.4 12.2 %collective-permute-start.35 = (bf16[256,512]{1,0:T(8,128)(2,1)}, bf16[256,512]{1,0:T(8,128)(2,1)}, u32[]{:S(2)}, u32[]{:S(2)}) collective-permute-start(bf16[256,512]{1,0:T(8,128)(2,1)} %pad_maximum_fusion.2.refs_0_), channel_id=1, source_target_pairs={{0,1},{1,0},{2,3},{3,2},{4,5},{5,4},{6,7},{7,6},{8,9},{9,8},{10,11... | collective-permute-start | bytes 786440 | tf_op jit(solution)/shard_map/ppermute | solution.py:690
  257.0 16.2 %collective-permute-start.42 = (bf16[256,512]{1,0:T(8,128)(2,1)}, bf16[256,512]{1,0:T(8,128)(2,1)}, u32[]{:S(2)}, u32[]{:S(2)}) collective-permute-start(bf16[256,512]{1,0:T(8,128)(2,1)} %pad_maximum_fusion.2.refs_0_), channel_id=1, source_target_pairs={{0,8},{1,9},{2,10},{3,11},{4,12},{5,13},{6,14},{7,15},{8,0},{9,1},... | collective-permute-start | bytes 786440 | tf_op jit(solution)/shard_map/ppermute | solution.py:690
  268.7 4.5 %collective-permute-start.43 = (bf16[256,512]{1,0:T(8,128)(2,1)}, bf16[256,512]{1,0:T(8,128)(2,1)}, u32[]{:S(2)}, u32[]{:S(2)}) collective-permute-start(bf16[256,512]{1,0:T(8,128)(2,1)} %collective-permute-done.35.refs_1_), channel_id=1, source_target_pairs={{0,8},{1,9},{2,10},{3,11},{4,12},{5,13},{6,14},{7,15},{8,0},{9,1},... | collective-permute-start | bytes 786440 | tf_op jit(solution)/shard_map/ppermute | solution.py:690
  268.7 4.5 %collective-permute-start.44 = (bf16[256,512]{1,0:T(8,128)(2,1)}, bf16[256,512]{1,0:T(8,128)(2,1)}, u32[]{:S(2)}, u32[]{:S(2)}) collective-permute-start(bf16[256,512]{1,0:T(8,128)(2,1)} %collective-permute-done.36.refs_2_), channel_id=1, source_target_pairs={{0,8},{1,9},{2,10},{3,11},{4,12},{5,13},{6,14},{7,15},{8,0},{9,1},... | collective-permute-start | bytes 786440 | tf_op jit(solution)/shard_map/ppermute | solution.py:690
  269.2 4.0 %collective-permute-start.45 = (bf16[256,512]{1,0:T(8,128)(2,1)}, bf16[256,512]{1,0:T(8,128)(2,1)}, u32[]{:S(2)}, u32[]{:S(2)}) collective-permute-start(bf16[256,512]{1,0:T(8,128)(2,1)} %collective-permute-done.37.refs_3_), channel_id=1, source_target_pairs={{0,8},{1,9},{2,10},{3,11},{4,12},{5,13},{6,14},{7,15},{8,0},{9,1},... | collective-permute-start | bytes 786440 | tf_op jit(solution)/shard_map/ppermute | solution.py:690
where the time goes:
time: 282 us; the launch traced here: 277 us
  Pallas kernels  124 us (44%)
  starting transfers between devices  68.3 us (24%)
  waiting for transfers between devices  57.4 us (20%)
  local copies, waits for them, and re-layouts  12.7 us (5%)
  other arithmetic  12.1 us (4%)
    pallas_call x11, Pallas kernels, hbm_call(): pl.pallas_call(body, in_specs=[pl.BlockSpec(memory_space=pltpu.SMEM)] * s...  104 us
    ppermute x44, waiting for transfers between devices, flip(): return lax.ppermute(value, ('seq', 'blk'), pairs)  57.4 us
    ppermute x44, starting transfers between devices, flip(): return lax.ppermute(value, ('seq', 'blk'), pairs)  54.9 us
    pallas_call x8, Pallas kernels, vmem_call(): pl.pallas_call(kernel, in_specs=[in_smem] * smem + [in_vmem] * (len(args)...  19.7 us
    unnamed x20, local copies, waits for them, and re-layouts  7.59 us
    ppermute x1, starting transfers between devices, local(): tail = lax.ppermute(sent, 'blk', pairs)  7.52 us
  transfers between devices with their start and end apart: 47, of which 14 were waited for; matrix products, arithmetic and copies ran while one was open for 6% of the time, Pallas kernels for 43%

commit v1 on v0

--- a/solution.py
+++ b/solution.py
@@ -570,8 +570,11 @@
 def sort_kernel(flow, info_ref, rows_ref, *out_refs):
     flow.need(rows_ref)
     for k, ref in enumerate(out_refs):
-        take = picks((ref.shape[0], rows_ref.shape[0]), len(out_refs), info_ref[0] ^ k)
-        ref[...] = dot(take, rows_ref[...]).astype(BF16)
+        scenes, some = len(out_refs), ref.shape[0] // len(out_refs)
+        take = picks((some, some * scenes), scenes, info_ref[0] ^ k)
+        for first in range(0, ref.shape[0], some):
+            given = rows_ref[pl.ds(first * scenes, some * scenes), :]
+            ref[pl.ds(first, some), :] = dot(take, given).astype(BF16)
         flow.emit(ref)
 
 
@@ -867,15 +870,18 @@
     for j in range(sums.lines.bit_length() - 1):
         far = sums.flip(small_block, 0, 2 << j)
         if j == sums.lines.bit_length() - 2:
-            leaving = after(d_lat_set, small_block)
-            d_lat_back = lax.all_to_all(leaving, "blk", 0, 0, axis_index_groups=lines, tiled=True)
             d_tokens = token_back(tok, gt, [own, *own_tail, *after(returned, small_block)])
             far = after(far, d_tokens)
         small_block = jnp.concatenate([small_block, far], axis=0)
-    last_a, last_b, small_block = lax.optimization_barrier((last_a, last_b, small_block))
+    other_a, other_b = sums.to_core(two_a), sums.to_core(two_b)
+    last_a, last_b, small_block, other_a, other_b = lax.optimization_barrier(
+        (last_a, last_b, small_block, other_a, other_b)
+    )
+    leaving = after(d_lat_set, small_block)
+    d_lat_back = lax.all_to_all(leaving, "blk", 0, 0, axis_index_groups=lines, tiled=True)
     small_got = sums.to_quad([small_block] * 3)
     mine = [two_a, last_a, two_b, last_b]
-    other = [sums.to_core(v) for v in mine]
+    other = [other_a, sums.to_core(last_a), other_b, sums.to_core(last_b)]
     d_w_down, d_w_up = sums.unpack(mine, other, [(hidden, width), (width, hidden)], crossed=True)
     small_got, d_lat_back, d_w_up = lax.optimization_barrier((small_got, d_lat_back, d_w_up))
     small_mine = [small_block, *small_got]

time: 282 us -> 276 us (0.979)
  waiting for transfers between devices: 57.4 us -> 53.1 us
    ppermute x44, waiting for transfers between devices: 57.4 us -> 43.2 us  [flip(): return lax.ppermute(value, ('seq', 'blk'), pairs)]
    all_to_all x1, waiting for transfers between devices: 0.01 us -> 9.95 us  [local(): lax.all_to_all(leaving, 'blk', 0, 0, axis_index_groups=lines, tiled=True)]
  transfers between devices with their start and end apart: 47 -> 47, of which waited for: 14 -> 15; matrix products, arithmetic and copies ran while one was open for 6% -> 6% of each run, Pallas kernels for 43% -> 44%
where the time goes in v1:
time: 276 us; the launch traced here: 272 us
  Pallas kernels  123 us (45%)
  starting transfers between devices  67.5 us (24%)
  waiting for transfers between devices  53.1 us (19%)
  local copies, waits for them, and re-layouts  13.3 us (5%)
  other arithmetic  12.1 us (4%)
    pallas_call x11, Pallas kernels, hbm_call(): pl.pallas_call(body, in_specs=[pl.BlockSpec(memory_space=pltpu.SMEM)] * s...  104 us
    ppermute x44, starting transfers between devices, flip(): return lax.ppermute(value, ('seq', 'blk'), pairs)  54 us
    ppermute x44, waiting for transfers between devices, flip(): return lax.ppermute(value, ('seq', 'blk'), pairs)  43.2 us
    pallas_call x8, Pallas kernels, vmem_call(): pl.pallas_call(kernel, in_specs=[in_smem] * smem + [in_vmem] * (len(args)...  19.7 us
    all_to_all x1, waiting for transfers between devices, local(): lax.all_to_all(leaving, 'blk', 0, 0, axis_index_groups=lines, tiled=True)  9.95 us
    unnamed x20, local copies, waits for them, and re-layouts  8.22 us
    ppermute x1, starting transfers between devices, local(): tail = lax.ppermute(sent, 'blk', pairs)  7.52 us
  transfers between devices with their start and end apart: 47, of which 15 were waited for; matrix products, arithmetic and copies ran while one was open for 6% of the time, Pallas kernels for 44%

profile of v1, /device:TPU:0, one launch (start us, length us, event | category | flops | bytes accessed | tf_op | source)
XLA Modules:
  0.0 271.8 jit_solution(17574609974482081966)
XLA Ops:
  0.6 3.0 %collective-permute-start.3 = (bf16[1024,512]{1,0:T(8,128)(2,1)}, bf16[1024,512]{1,0:T(8,128)(2,1)}, u32[]{:S(2)}, u32[]{:S(2)}) collective-permute-start(bf16[1024,512]{1,0:T(8,128)(2,1)} %bitcast.25), channel_id=1, source_target_pairs={{0,1},{1,0},{2,3},{3,2},{4,5},{5,4},{6,7},{7,6},{8,9},{9,8},{10,11... | collective-permute-start | bytes 3145736 | tf_op jit(solution)/shard_map/ppermute | solution.py:693
  3.7 2.8 %sort_rows.2 = (bf16[256,512]{1,0:T(8,128)(2,1)}, bf16[256,512]{1,0:T(8,128)(2,1)}, bf16[256,512]{1,0:T(8,128)(2,1)}, bf16[256,512]{1,0:T(8,128)(2,1)}) custom-call(s32[1]{0:T(128)} %bitcast.2.refs_0_, bf16[1024,512]{1,0:T(8,128)(2,1)} %bitcast.33), custom_call_target="tpu_custom_call" | custom-call | tf_op jit(solution)/shard_map/sort_rows/pallas_call | solution.py:140
  6.5 1.6 collective-permute-start
  8.1 2.6 collective-permute-start.1
  10.9 1.3 fusion.2
  12.2 2.8 %sort_rows.3 = (bf16[256,512]{1,0:T(8,128)(2,1)}, bf16[256,512]{1,0:T(8,128)(2,1)}, bf16[256,512]{1,0:T(8,128)(2,1)}, bf16[256,512]{1,0:T(8,128)(2,1)}) custom-call(s32[1]{0:T(128)} %bitcast.2.refs_0_, bf16[1024,512]{1,0:T(8,128)(2,1)} %bitcast.34), custom_call_target="tpu_custom_call" | custom-call | tf_op jit(solution)/shard_map/sort_rows/pallas_call | solution.py:140
  16.4 1.3 stack.65.refs_0_
  17.6 1.9 stack.66.refs_0_
  19.5 4.2 %keys_values.1 = (bf16[1024,512]{1,0:T(8,128)(2,1)}, bf16[1024,512]{1,0:T(8,128)(2,1)}) custom-call(bf16[1024,512]{1,0:T(8,128)(2,1)} %bitcast.26, f32[1,512]{1,0:T(1,128)} %bitcast.36, bf16[512,512]{1,0:T(8,128)(2,1)} %refs_2_.7, bf16[512,512]{1,0:T(8,128)(2,1)} %refs_3_.7), custom_call_target="tpu_custom_call" | custom-call | tf_op jit(solution)/shard_map/keys_values/pallas_call | solution.py:140
  23.8 1.3 pad_add_fusion.1.refs_0_
  25.0 1.3 pad_add_fusion.2.refs_0_
  26.3 3.5 %collective-permute-done.1.refs_9_ = bf16[256,512]{1,0:T(8,128)(2,1)} collective-permute-done((bf16[256,512]{1,0:T(8,128)(2,1)}, bf16[256,512]{1,0:T(8,128)(2,1)}, u32[]{:S(2)}, u32[]{:S(2)}) %collective-permute-start.1) | collective-permute-done | bytes 262176 | tf_op jit(solution)/shard_map/ppermute | solution.py:693
  29.8 2.3 slice_select_fusion
  32.2 7.5 %collective-permute-start.4 = (bf16[768,512]{1,0:T(8,128)(2,1)}, bf16[768,512]{1,0:T(8,128)(2,1)}, u32[]{:S(2)}, u32[]{:S(2)}) collective-permute-start(bf16[768,512]{1,0:T(8,128)(2,1)} %slice_select_fusion), channel_id=1, source_target_pairs={{0,2},{1,3},{2,4},{3,5},{4,6},{5,7},{8,10},{9,11},{10,12},{11,13},... | collective-permute-start | bytes 2359304 | tf_op jit(solution)/shard_map/ppermute | solution.py:791
  40.5 12.3 %attend.1 = (bf16[1024,512]{1,0:T(8,128)(2,1)}, f32[1024,512]{1,0:T(8,128)}, f32[8,1024]{1,0:T(8,128)}, f32[8,1024]{1,0:T(8,128)}, bf16[1024,512]{1,0:T(8,128)(2...) custom-call(s32[4]{0:T(128)} %pad_add_fusion.1.refs_0_, ...), custom_call_target="tpu_custom_call" | custom-call | tf_op jit(solution)/shard_map/attend/pallas_call | solution.py:140
  52.8 7.5 %collective-permute-done.5.refs_2_ = bf16[256,512]{1,0:T(8,128)(2,1)} collective-permute-done((bf16[256,512]{1,0:T(8,128)(2,1)}, bf16[256,512]{1,0:T(8,128)(2,1)}, u32[]{:S(2)}, u32[]{:S(2)}) %collective-permute-start.5) | collective-permute-done | bytes 262176 | tf_op jit(solution)/shard_map/ppermute | solution.py:693
  61.1 4.0 %collective-permute-start.7 = (bf16[256,512]{1,0:T(8,128)(2,1)}, bf16[256,512]{1,0:T(8,128)(2,1)}, u32[]{:S(2)}, u32[]{:S(2)}) collective-permute-start(bf16[256,512]{1,0:T(8,128)(2,1)} %get-tuple-element.211), channel_id=1, source_target_pairs={{0,6},{1,7},{2,4},{3,5},{4,2},{5,3},{6,0},{7,1},{8,14},{9,15},{10,... | collective-permute-start | bytes 786440 | tf_op jit(solution)/shard_map/ppermute | solution.py:693
  65.1 18.4 %finish.1 = (bf16[768,512]{1,0:T(8,128)(2,1)}, bf16[768,512]{1,0:T(8,128)(2,1)}, bf16[768,1024]{1,0:T(8,128)(2,1)}, f32[1024,128]{1,0:T(8,128)}, bf16[1024,512]{...) custom-call(s32[3]{0:T(128)} %pad_add_fusion.2.refs_0_, ...), custom_call_target="tpu_custom_call" | custom-call | tf_op jit(solution)/shard_map/finish/pallas_call | solution.py:140
  84.1 1.5 collective-permute-start.9
  85.7 2.4 collective-permute-start.10
  88.6 21.1 %mlp_back.1 = (f32[1024,512]{1,0:T(8,128)}, bf16[1024,512]{1,0:T(8,128)(2,1)}, bf16[1024,512]{1,0:T(8,128)(2,1)}, f32[8,1024]{1,0:T(8,128)}, f32[8,1024]{1,0:T(8...) custom-call(s32[7]{0:T(128)} %pad_add_fusion.refs_0_.info_ref, ...), custom_call_target="tpu_custom_call" | custom-call | tf_op jit(solution)/shard_map/mlp_back/pallas_call | solution.py:140
  109.9 7.3 %attention_back.2 = (bf16[768,512]{1,0:T(8,128)(2,1)}, f32[1024,512]{1,0:T(8,128)}, f32[512,512]{1,0:T(8,128)}, f32[512,512]{1,0:T(8,128)}, f32[8,512]{1,0:T(8,128)}) custom-call(s32[5]{0:T(128)} %stack.65.refs_0_, bf16[1024,512]{1,0:T(8,128)(2,1)} %get-tuple-element.215.refs_6_.refs_1_, bf16[512,512]{1,0:T(8,128)(2,1)} %refs_2_.7, ...), custom_call_target="tpu_custom_call" | custom-call | tf_op jit(solution)/shard_map/attention_back/pallas_call | solution.py:140
  117.2 1.5 collective-permute-start.15
  118.8 1.6 copy-done
  120.3 3.1 %split_sum.6 = (bf16[512,512]{1,0:T(8,128)(2,1)S(1)}, bf16[512,512]{1,0:T(8,128)(2,1)}, bf16[512,512]{1,0:T(8,128)(2,1)}, bf16[512,512]{1,0:T(8,128)(2,1)}) custom-call(s32[7]{0:T(128)S(1)} %copy-done.6, bf16[2048,512]{1,0:T(8,128)(2,1)S(1)} %copy-done, bf16[2048,512]{1,0:T(8,128)(2,1)} %collective-permute-done.11.refs_1_), custom_call_target="tpu_custom_call" | custom-call | tf_op jit(solution)/shard_map/split_sum/pallas_call | solution.py:46
  124.7 1.5 collective-permute-start.13
  126.3 1.5 collective-permute-start.14
  127.7 23.6 %attention_back.3 = (bf16[1024,512]{1,0:T(8,128)(2,1)}, bf16[1024,512]{1,0:T(8,128)(2,1)}, bf16[1024,512]{1,0:T(8,128)(2,1)}, bf16[1040,512]{1,0:T(8,128)(2,1)}, bf16[1040,512]{1,0:T(8,128)(2,1)}) custom-call(s32[8]{0:T(128)} %stack.66.refs_0_, bf16[1024,512]{1,0:T(8,128)(2,1)} %get-tuple-element.215.refs_6_.refs_1_, bf16[512,512]{1,0:T(8,128)(2,1)} %refs_2_.7, ...), custom_call_target="tpu_custom_call" | custom-call | tf_op jit(solution)/shard_map/attention_back/pallas_call | solution.py:140
  152.3 1.0 copy-done.3
  153.4 2.3 split_sum.7
  156.4 2.8 %pad_select_fusion = (bf16[1024,512]{1,0:T(8,128)(2,1)}, bf16[1024,512]{1,0:T(8,128)(2,1)}) fusion(bf16[768,512]{1,0:T(8,128)(2,1)} %collective-permute-done.15, pred[]{:T(512)S(6)} %eq.16, bf16[1024,512]{1,0:T(8,128)(2,1)S(1)} %copy-done.7, pred[]{:T(512)S(6)} %eq.18), kind=kLoop, calls=%fused_computation | loop fusion | flops 3145728 | bytes 3932162 | tf_op jit(solution)/shard_map/jit(_where)/select_n | solution.py:844
  159.7 2.4 collective-permute-start.17
  162.1 4.5 %collective-permute-start.18 = (bf16[128,512]{1,0:T(8,128)(2,1)}, bf16[128,512]{1,0:T(8,128)(2,1)}, u32[]{:S(2)}, u32[]{:S(2)}) collective-permute-start(bf16[128,512]{1,0:T(8,128)(2,1)} %get-tuple-element.286), channel_id=1, source_target_pairs={{0,4},{1,5},{2,6},{3,7},{4,0},{5,1},{6,2},{7,3},{8,12},{9,13},{10,... | collective-permute-start | bytes 393224 | tf_op jit(solution)/shard_map/ppermute | solution.py:693
  166.6 3.2 %unsort_rows.2 = bf16[1024,512]{1,0:T(8,128)(2,1)} custom-call(s32[1]{0:T(128)} %bitcast.2.refs_0_, bf16[256,512]{1,0:T(8,128)(2,1)} %get-tuple-element.293.refs_1_, bf16[256,512]{1,0:T(8,128)(2,1)} %collective-permute-done.8.refs_2_, bf16[256,512]{1,0:T(8,128)(2,1)} %collective-permute-done.9.refs_3_, bf16[256,512]{1,0:T(8,128)(2,1)} %collective-permute-done.10.refs_4_), custom_call_target="tpu_custom_call" | custom-call | tf_op jit(solution)/shard_map/unsort_rows/pallas_call | solution.py:140
  169.8 7.0 %collective-permute-done.18.refs_2_ = bf16[128,512]{1,0:T(8,128)(2,1)} collective-permute-done((bf16[128,512]{1,0:T(8,128)(2,1)}, bf16[128,512]{1,0:T(8,128)(2,1)}, u32[]{:S(2)}, u32[]{:S(2)}) %collective-permute-start.18) | collective-permute-done | bytes 131104 | tf_op jit(solution)/shard_map/ppermute | solution.py:693
  177.8 1.1 split_sum.8
  178.9 2.7 %collective-permute-start.20 = (bf16[128,512]{1,0:T(8,128)(2,1)S(1)}, bf16[128,512]{1,0:T(8,128)(2,1)S(1)}, u32[]{:S(2)}, u32[]{:S(2)}) collective-permute-start(bf16[128,512]{1,0:T(8,128)(2,1)S(1)} %split_sum.8), channel_id=1, source_target_pairs={{0,2},{1,3},{2,0},{3,1},{4,6},{5,7},{6,4},{7,5},{8,10},{9,11},{10,... | collective-permute-start | bytes 393224 | tf_op jit(solution)/shard_map/ppermute | solution.py:693
  181.6 1.2 copy-done.1
  182.8 1.5 split_sum.9
  184.3 1.6 collective-permute-start.21
  185.9 1.2 collective-permute-start.22
  188.9 4.2 %collective-permute-done.21.refs_1_ = bf16[272,512]{1,0:T(8,128)(2,1)S(1)} collective-permute-done((bf16[272,512]{1,0:T(8,128)(2,1)S(1)}, bf16[272,512]{1,0:T(8,128)(2,1)S(1)}, u32[]{:S(2)}, u32[]{:S(2)}) %collective-permute-start.21) | collective-permute-done | bytes 278560 | tf_op jit(solution)/shard_map/ppermute | solution.py:693
  193.1 1.5 collective-permute-start.28
  195.5 3.8 %collective-permute-done.23.refs_3_ = bf16[272,512]{1,0:T(8,128)(2,1)S(1)} collective-permute-done((bf16[272,512]{1,0:T(8,128)(2,1)S(1)}, bf16[272,512]{1,0:T(8,128)(2,1)S(1)}, u32[]{:S(2)}, u32[]{:S(2)}) %collective-permute-start.23) | collective-permute-done | bytes 278560 | tf_op jit(solution)/shard_map/ppermute | solution.py:693
  199.3 1.4 collective-permute-done.24
  200.7 1.0 collective-permute-start.29
  202.5 3.9 %collective-permute-start.26 = (bf16[80,512]{1,0:T(8,128)(2,1)S(1)}, bf16[80,512]{1,0:T(8,128)(2,1)S(1)}, u32[]{:S(2)}, u32[]{:S(2)}) collective-permute-start(bf16[80,512]{1,0:T(8,128)(2,1)S(1)} %get-tuple-element.311), channel_id=1, source_target_pairs={{0,4},{1,5},{2,6},{3,7},{4,0},{5,1},{6,2},{7,3},{8,12},{9,13},{10,... | collective-permute-start | bytes 245768 | tf_op jit(solution)/shard_map/ppermute | solution.py:693
  207.6 3.7 %collective-permute-done.26.refs_2_ = bf16[80,512]{1,0:T(8,128)(2,1)S(1)} collective-permute-done((bf16[80,512]{1,0:T(8,128)(2,1)S(1)}, bf16[80,512]{1,0:T(8,128)(2,1)S(1)}, u32[]{:S(2)}, u32[]{:S(2)}) %collective-permute-start.26) | collective-permute-done | bytes 81952 | tf_op jit(solution)/shard_map/ppermute | solution.py:693
  211.3 1.4 collective-permute-done.27.refs_3_
  213.5 1.5 collective-permute-start.32
  217.4 1.2 collective-permute-start.33
  219.2 2.5 collective-permute-done.33
  223.0 1.9 collective-permute-start.34
  225.0 4.5 %token_back.1 = f32[1024,512]{1,0:T(8,128)} custom-call(bf16[1024,512]{1,0:T(8,128)(2,1)} %bitcast.29, f32[1,512]{1,0:T(1,128)} %bitcast.41, bf16[1024,512]{1,0:T(8,128)(2,1)} %get-tuple-element.324.refs_2_, bf16[1024,512]{1,0:T(8,128)(2,1)} %get-tuple-element.354.refs_3_, bf16[1024,512]{1,0:T(8,128)(2,1)} %collective-permute-done.30.refs_4_), custom_call_target="tpu_custom_call" | custom-call | tf_op jit(solution)/shard_map/token_back/pallas_call | solution.py:140
  229.5 2.2 collective-permute-done.34
  231.7 1.6 pad_maximum_fusion.2.refs_0_
  233.4 4.4 %all-to-all-start = ((bf16[4,256,512]{2,1,0:T(8,128)(2,1)}), bf16[4,256,512]{2,1,0:T(8,128)(2,1)}, u32[]{:S(2)}, u32[]{:S(2)}) async-start(bf16[4,256,512]{2,1,0:T(8,128)(2,1)} %bitcast.35), calls=%async_computation | async-start | bytes 2097152 | tf_op jit(solution)/shard_map/all_to_all | solution.py:881
  238.4 1.2 collective-permute-start.39
  240.3 1.5 collective-permute-start.37
  241.9 6.6 %unpack.2 = (f32[2048,512]{1,0:T(8,128)}, f32[512,2048]{1,0:T(8,128)}) custom-call(s32[7]{0:T(128)S(1)} %copy-done.6, bf16[512,512]{1,0:T(8,128)(2,1)} %pad_maximum_fusion.refs_0_, bf16[512,512]{1,0:T(8,128)(2,1)} %collective-permute-done.31.refs_1_, bf16[512,512]{1,0:T(8,128)(2,1)} %constant_dynamic-update-slice_fusion.refs_2_, ...), custom_call_target="tpu_custom_call" | custom-call | tf_op jit(solution)/shard_map/unpack/pallas_call | solution.py:46
  248.8 3.8 %collective-permute-done.38.refs_2_ = bf16[256,512]{1,0:T(8,128)(2,1)} collective-permute-done((bf16[256,512]{1,0:T(8,128)(2,1)}, bf16[256,512]{1,0:T(8,128)(2,1)}, u32[]{:S(2)}, u32[]{:S(2)}) %collective-permute-start.38) | collective-permute-done | bytes 262176 | tf_op jit(solution)/shard_map/ppermute | solution.py:693
  253.5 9.9 %all-to-all-done = bf16[4,256,512]{2,1,0:T(8,128)(2,1)} async-done(((bf16[4,256,512]{2,1,0:T(8,128)(2,1)}), bf16[4,256,512]{2,1,0:T(8,128)(2,1)}, u32[]{:S(2)}, u32[]{:S(2)}) %all-to-all-start) | async-done | bytes 1048608 | tf_op jit(solution)/shard_map/all_to_all | solution.py:881
  264.5 3.3 %unsort_rows.3 = f32[1024,512]{1,0:T(8,128)} custom-call(s32[1]{0:T(128)} %constant.61.clone.1.refs_0_, bf16[1024,512]{1,0:T(8,128)(2,1)} %bitcast.17.refs_1_), custom_call_target="tpu_custom_call" | custom-call | tf_op jit(solution)/shard_map/unsort_rows/pallas_call | solution.py:140
  267.9 3.8 %unpack.3 = (f32[512,512]{1,0:T(8,128)}, f32[512,512]{1,0:T(8,128)}, f32[512,512]{1,0:T(8,128)}, f32[512,512]{1,0:T(8,128)}) custom-call(s32[7]{0:T(128)S(1)} %copy-done.6, bf16[256,512]{1,0:T(8,128)(2,1)} %pad_maximum_fusion.2.refs_0_, bf16[256,512]{1,0:T(8,128)(2,1)} %collective-permute-done.37.refs_1_, bf16[256,512]{1,0:T(8,128)(2,1)} %collective-permute-done.38.refs_2_, ...), custom_call_target="tpu_custom_call" | custom-call | tf_op jit(solution)/shard_map/unpack/pallas_call | solution.py:46
  (84 shorter events, 20.8 us)
Async XLA Ops:
  0.6 29.2 %collective-permute-start.3 = (bf16[1024,512]{1,0:T(8,128)(2,1)}, bf16[1024,512]{1,0:T(8,128)(2,1)}, u32[]{:S(2)}, u32[]{:S(2)}) collective-permute-start(bf16[1024,512]{1,0:T(8,128)(2,1)} %bitcast.25), channel_id=1, source_target_pairs={{0,1},{1,0},{2,3},{3,2},{4,5},{5,4},{6,7},{7,6},{8,9},{9,8},{10,11... | collective-permute-start | bytes 3145736 | tf_op jit(solution)/shard_map/ppermute | solution.py:693
  6.5 19.8 %collective-permute-start = (bf16[256,512]{1,0:T(8,128)(2,1)}, bf16[256,512]{1,0:T(8,128)(2,1)}, u32[]{:S(2)}, u32[]{:S(2)}) collective-permute-start(bf16[256,512]{1,0:T(8,128)(2,1)} %get-tuple-element.183), channel_id=1, source_target_pairs={{0,2},{1,3},{2,0},{3,1},{4,6},{5,7},{6,4},{7,5},{8,10},{9,11},{10,... | collective-permute-start | bytes 786440 | tf_op jit(solution)/shard_map/ppermute | solution.py:693
  8.1 21.7 %collective-permute-start.1 = (bf16[256,512]{1,0:T(8,128)(2,1)}, bf16[256,512]{1,0:T(8,128)(2,1)}, u32[]{:S(2)}, u32[]{:S(2)}) collective-permute-start(bf16[256,512]{1,0:T(8,128)(2,1)} %get-tuple-element.184), channel_id=1, source_target_pairs={{0,4},{1,5},{2,6},{3,7},{4,0},{5,1},{6,2},{7,3},{8,12},{9,13},{10,... | collective-permute-start | bytes 786440 | tf_op jit(solution)/shard_map/ppermute | solution.py:693
  10.7 19.1 %collective-permute-start.2 = (bf16[256,512]{1,0:T(8,128)(2,1)}, bf16[256,512]{1,0:T(8,128)(2,1)}, u32[]{:S(2)}, u32[]{:S(2)}) collective-permute-start(bf16[256,512]{1,0:T(8,128)(2,1)} %get-tuple-element.185), channel_id=1, source_target_pairs={{0,6},{1,7},{2,4},{3,5},{4,2},{5,3},{6,0},{7,1},{8,14},{9,15},{10,... | collective-permute-start | bytes 786440 | tf_op jit(solution)/shard_map/ppermute | solution.py:693
  32.2 28.1 %collective-permute-start.4 = (bf16[768,512]{1,0:T(8,128)(2,1)}, bf16[768,512]{1,0:T(8,128)(2,1)}, u32[]{:S(2)}, u32[]{:S(2)}) collective-permute-start(bf16[768,512]{1,0:T(8,128)(2,1)} %slice_select_fusion), channel_id=1, source_target_pairs={{0,2},{1,3},{2,4},{3,5},{4,6},{5,7},{8,10},{9,11},{10,12},{11,13},... | collective-permute-start | bytes 2359304 | tf_op jit(solution)/shard_map/ppermute | solution.py:791
  39.7 20.6 %collective-permute-start.5 = (bf16[256,512]{1,0:T(8,128)(2,1)}, bf16[256,512]{1,0:T(8,128)(2,1)}, u32[]{:S(2)}, u32[]{:S(2)}) collective-permute-start(bf16[256,512]{1,0:T(8,128)(2,1)} %get-tuple-element.205), channel_id=1, source_target_pairs={{0,2},{1,3},{2,0},{3,1},{4,6},{5,7},{6,4},{7,5},{8,10},{9,11},{10,... | collective-permute-start | bytes 786440 | tf_op jit(solution)/shard_map/ppermute | solution.py:693
  60.3 23.3 %collective-permute-start.6 = (bf16[256,512]{1,0:T(8,128)(2,1)}, bf16[256,512]{1,0:T(8,128)(2,1)}, u32[]{:S(2)}, u32[]{:S(2)}) collective-permute-start(bf16[256,512]{1,0:T(8,128)(2,1)} %get-tuple-element.210), channel_id=1, source_target_pairs={{0,4},{1,5},{2,6},{3,7},{4,0},{5,1},{6,2},{7,3},{8,12},{9,13},{10,... | collective-permute-start | bytes 786440 | tf_op jit(solution)/shard_map/ppermute | solution.py:693
  61.1 22.4 %collective-permute-start.7 = (bf16[256,512]{1,0:T(8,128)(2,1)}, bf16[256,512]{1,0:T(8,128)(2,1)}, u32[]{:S(2)}, u32[]{:S(2)}) collective-permute-start(bf16[256,512]{1,0:T(8,128)(2,1)} %get-tuple-element.211), channel_id=1, source_target_pairs={{0,6},{1,7},{2,4},{3,5},{4,2},{5,3},{6,0},{7,1},{8,14},{9,15},{10,... | collective-permute-start | bytes 786440 | tf_op jit(solution)/shard_map/ppermute | solution.py:693
  83.6 26.2 %collective-permute-start.8 = (bf16[256,512]{1,0:T(8,128)(2,1)}, bf16[256,512]{1,0:T(8,128)(2,1)}, u32[]{:S(2)}, u32[]{:S(2)}) collective-permute-start(bf16[256,512]{1,0:T(8,128)(2,1)} %get-tuple-element.225), channel_id=1, source_target_pairs={{0,2},{1,3},{2,0},{3,1},{4,6},{5,7},{6,4},{7,5},{8,10},{9,11},{10,... | collective-permute-start | bytes 786440 | tf_op jit(solution)/shard_map/ppermute | solution.py:693
  84.1 25.6 %collective-permute-start.9 = (bf16[256,512]{1,0:T(8,128)(2,1)}, bf16[256,512]{1,0:T(8,128)(2,1)}, u32[]{:S(2)}, u32[]{:S(2)}) collective-permute-start(bf16[256,512]{1,0:T(8,128)(2,1)} %get-tuple-element.226), channel_id=1, source_target_pairs={{0,4},{1,5},{2,6},{3,7},{4,0},{5,1},{6,2},{7,3},{8,12},{9,13},{10,... | collective-permute-start | bytes 786440 | tf_op jit(solution)/shard_map/ppermute | solution.py:693
  85.7 24.1 %collective-permute-start.10 = (bf16[256,512]{1,0:T(8,128)(2,1)}, bf16[256,512]{1,0:T(8,128)(2,1)}, u32[]{:S(2)}, u32[]{:S(2)}) collective-permute-start(bf16[256,512]{1,0:T(8,128)(2,1)} %get-tuple-element.227), channel_id=1, source_target_pairs={{0,6},{1,7},{2,4},{3,5},{4,2},{5,3},{6,0},{7,1},{8,14},{9,15},{10,... | collective-permute-start | bytes 786440 | tf_op jit(solution)/shard_map/ppermute | solution.py:693
  109.8 7.4 %collective-permute-start.11 = (bf16[2048,512]{1,0:T(8,128)(2,1)}, bf16[2048,512]{1,0:T(8,128)(2,1)}, u32[]{:S(2)}, u32[]{:S(2)}) collective-permute-start(bf16[2048,512]{1,0:T(8,128)(2,1)} %get-tuple-element.243), channel_id=1, source_target_pairs={{0,8},{1,9},{2,10},{3,11},{4,12},{5,13},{6,14},{7,15},{8,0},{9,1},... | collective-permute-start | bytes 6291464 | tf_op jit(solution)/shard_map/ppermute | solution.py:693
  109.9 8.9 %copy-start.6 = (s32[7]{0:T(128)S(1)}, s32[7]{0:T(128)}, u32[]{:S(2)}) copy-start(s32[7]{0:T(128)} %pad_add_fusion.refs_0_.info_ref) | copy-start | bytes 88
  117.2 34.1 %collective-permute-start.15 = (bf16[768,512]{1,0:T(8,128)(2,1)}, bf16[768,512]{1,0:T(8,128)(2,1)}, u32[]{:S(2)}, u32[]{:S(2)}) collective-permute-start(bf16[768,512]{1,0:T(8,128)(2,1)} %get-tuple-element.259), channel_id=1, source_target_pairs={{2,0},{3,1},{4,2},{5,3},{6,4},{7,5},{10,8},{11,9},{12,10},{13,11},... | collective-permute-start | bytes 2359304 | tf_op jit(solution)/shard_map/ppermute | solution.py:831
  118.8 1.6 copy-start
  123.4 0.8 copy-start.2
  124.2 27.1 %collective-permute-start.12 = (bf16[512,512]{1,0:T(8,128)(2,1)}, bf16[512,512]{1,0:T(8,128)(2,1)}, u32[]{:S(2)}, u32[]{:S(2)}) collective-permute-start(bf16[512,512]{1,0:T(8,128)(2,1)} %get-tuple-element.256), channel_id=1, source_target_pairs={{0,1},{1,0},{2,3},{3,2},{4,5},{5,4},{6,7},{7,6},{8,9},{9,8},{10,11... | collective-permute-start | bytes 1572872 | tf_op jit(solution)/shard_map/ppermute | solution.py:693
  124.7 26.6 %collective-permute-start.13 = (bf16[512,512]{1,0:T(8,128)(2,1)}, bf16[512,512]{1,0:T(8,128)(2,1)}, u32[]{:S(2)}, u32[]{:S(2)}) collective-permute-start(bf16[512,512]{1,0:T(8,128)(2,1)} %get-tuple-element.257), channel_id=1, source_target_pairs={{0,16},{1,17},{2,18},{3,19},{4,20},{5,21},{6,22},{7,23},{8,24},{9,... | collective-permute-start | bytes 1572872 | tf_op jit(solution)/shard_map/ppermute | solution.py:693
  126.3 25.1 %collective-permute-start.14 = (bf16[512,512]{1,0:T(8,128)(2,1)}, bf16[512,512]{1,0:T(8,128)(2,1)}, u32[]{:S(2)}, u32[]{:S(2)}) collective-permute-start(bf16[512,512]{1,0:T(8,128)(2,1)} %get-tuple-element.258), channel_id=1, source_target_pairs={{0,17},{1,16},{2,19},{3,18},{4,21},{5,20},{6,23},{7,22},{8,25},{9,... | collective-permute-start | bytes 1572872 | tf_op jit(solution)/shard_map/ppermute | solution.py:693
  151.3 25.5 %collective-permute-start.16 = (bf16[1040,512]{1,0:T(8,128)(2,1)}, bf16[1040,512]{1,0:T(8,128)(2,1)}, u32[]{:S(2)}, u32[]{:S(2)}) collective-permute-start(bf16[1040,512]{1,0:T(8,128)(2,1)} %get-tuple-element.281), channel_id=1, source_target_pairs={{0,8},{1,9},{2,10},{3,11},{4,12},{5,13},{6,14},{7,15},{8,0},{9,1},... | collective-permute-start | bytes 3194888 | tf_op jit(solution)/shard_map/ppermute | solution.py:693
  152.3 1.0 copy-start.3
  153.4 3.0 %copy-start.7 = (bf16[1024,512]{1,0:T(8,128)(2,1)S(1)}, bf16[1024,512]{1,0:T(8,128)(2,1)}, u32[]{:S(2)}) copy-start(bf16[1024,512]{1,0:T(8,128)(2,1)} %get-tuple-element.314) | copy-start | bytes 3145732
  155.7 0.7 copy-start.4
  159.2 47.2 %collective-permute-start.30 = (bf16[1024,512]{1,0:T(8,128)(2,1)}, bf16[1024,512]{1,0:T(8,128)(2,1)}, u32[]{:S(2)}, u32[]{:S(2)}) collective-permute-start(bf16[1024,512]{1,0:T(8,128)(2,1)} %get-tuple-element.316), channel_id=1, source_target_pairs={{0,1},{1,0},{2,3},{3,2},{4,5},{5,4},{6,7},{7,6},{8,9},{9,8},{10,11... | collective-permute-start | bytes 3145736 | tf_op jit(solution)/shard_map/ppermute | solution.py:693
  159.7 10.1 %collective-permute-start.17 = (bf16[128,512]{1,0:T(8,128)(2,1)}, bf16[128,512]{1,0:T(8,128)(2,1)}, u32[]{:S(2)}, u32[]{:S(2)}) collective-permute-start(bf16[128,512]{1,0:T(8,128)(2,1)} %get-tuple-element.285), channel_id=1, source_target_pairs={{0,2},{1,3},{2,0},{3,1},{4,6},{5,7},{6,4},{7,5},{8,10},{9,11},{10,... | collective-permute-start | bytes 393224 | tf_op jit(solution)/shard_map/ppermute | solution.py:693
  162.1 14.7 %collective-permute-start.18 = (bf16[128,512]{1,0:T(8,128)(2,1)}, bf16[128,512]{1,0:T(8,128)(2,1)}, u32[]{:S(2)}, u32[]{:S(2)}) collective-permute-start(bf16[128,512]{1,0:T(8,128)(2,1)} %get-tuple-element.286), channel_id=1, source_target_pairs={{0,4},{1,5},{2,6},{3,7},{4,0},{5,1},{6,2},{7,3},{8,12},{9,13},{10,... | collective-permute-start | bytes 393224 | tf_op jit(solution)/shard_map/ppermute | solution.py:693
  166.6 10.2 %collective-permute-start.19 = (bf16[128,512]{1,0:T(8,128)(2,1)}, bf16[128,512]{1,0:T(8,128)(2,1)}, u32[]{:S(2)}, u32[]{:S(2)}) collective-permute-start(bf16[128,512]{1,0:T(8,128)(2,1)} %get-tuple-element.287), channel_id=1, source_target_pairs={{0,6},{1,7},{2,4},{3,5},{4,2},{5,3},{6,0},{7,1},{8,14},{9,15},{10,... | collective-permute-start | bytes 393224 | tf_op jit(solution)/shard_map/ppermute | solution.py:693
  176.8 0.9 copy-start.5
  178.9 9.0 %collective-permute-start.20 = (bf16[128,512]{1,0:T(8,128)(2,1)S(1)}, bf16[128,512]{1,0:T(8,128)(2,1)S(1)}, u32[]{:S(2)}, u32[]{:S(2)}) collective-permute-start(bf16[128,512]{1,0:T(8,128)(2,1)S(1)} %split_sum.8), channel_id=1, source_target_pairs={{0,2},{1,3},{2,0},{3,1},{4,6},{5,7},{6,4},{7,5},{8,10},{9,11},{10,... | collective-permute-start | bytes 393224 | tf_op jit(solution)/shard_map/ppermute | solution.py:693
  181.6 1.2 copy-start.1
  184.3 8.8 %collective-permute-start.21 = (bf16[272,512]{1,0:T(8,128)(2,1)S(1)}, bf16[272,512]{1,0:T(8,128)(2,1)S(1)}, u32[]{:S(2)}, u32[]{:S(2)}) collective-permute-start(bf16[272,512]{1,0:T(8,128)(2,1)S(1)} %get-tuple-element.304), channel_id=1, source_target_pairs={{0,1},{1,0},{2,3},{3,2},{4,5},{5,4},{6,7},{7,6},{8,9},{9,8},{10,11... | collective-permute-start | bytes 835592 | tf_op jit(solution)/shard_map/ppermute | solution.py:693
  185.9 9.6 %collective-permute-start.22 = (bf16[272,512]{1,0:T(8,128)(2,1)S(1)}, bf16[272,512]{1,0:T(8,128)(2,1)S(1)}, u32[]{:S(2)}, u32[]{:S(2)}) collective-permute-start(bf16[272,512]{1,0:T(8,128)(2,1)S(1)} %get-tuple-element.305), channel_id=1, source_target_pairs={{0,16},{1,17},{2,18},{3,19},{4,20},{5,21},{6,22},{7,23},{8,24},{9,... | collective-permute-start | bytes 835592 | tf_op jit(solution)/shard_map/ppermute | solution.py:693
  187.2 12.2 %collective-permute-start.23 = (bf16[272,512]{1,0:T(8,128)(2,1)S(1)}, bf16[272,512]{1,0:T(8,128)(2,1)S(1)}, u32[]{:S(2)}, u32[]{:S(2)}) collective-permute-start(bf16[272,512]{1,0:T(8,128)(2,1)S(1)} %get-tuple-element.306), channel_id=1, source_target_pairs={{0,17},{1,16},{2,19},{3,18},{4,21},{5,20},{6,23},{7,22},{8,25},{9,... | collective-permute-start | bytes 835592 | tf_op jit(solution)/shard_map/ppermute | solution.py:693
  187.9 12.8 %collective-permute-start.24 = (bf16[256,512]{1,0:T(8,128)(2,1)S(1)}, bf16[256,512]{1,0:T(8,128)(2,1)S(1)}, u32[]{:S(2)}, u32[]{:S(2)}) collective-permute-start(bf16[256,512]{1,0:T(8,128)(2,1)S(1)} %pad_maximum_fusion.1), channel_id=1, source_target_pairs={{0,4},{1,5},{2,6},{3,7},{4,0},{5,1},{6,2},{7,3},{8,12},{9,13},{10,... | collective-permute-start | bytes 786440 | tf_op jit(solution)/shard_map/ppermute | solution.py:693
  193.1 14.5 %collective-permute-start.28 = (bf16[256,512]{1,0:T(8,128)(2,1)S(1)}, bf16[256,512]{1,0:T(8,128)(2,1)S(1)}, u32[]{:S(2)}, u32[]{:S(2)}) collective-permute-start(bf16[256,512]{1,0:T(8,128)(2,1)S(1)} %pad_maximum_fusion.1), channel_id=1, source_target_pairs={{0,1},{1,0},{2,3},{3,2},{4,5},{5,4},{6,7},{7,6},{8,9},{9,8},{10,11... | collective-permute-start | bytes 786440 | tf_op jit(solution)/shard_map/ppermute | solution.py:693
  200.7 12.0 %collective-permute-start.29 = (bf16[256,512]{1,0:T(8,128)(2,1)S(1)}, bf16[256,512]{1,0:T(8,128)(2,1)S(1)}, u32[]{:S(2)}, u32[]{:S(2)}) collective-permute-start(bf16[256,512]{1,0:T(8,128)(2,1)S(1)} %collective-permute-done.24), channel_id=1, source_target_pairs={{0,16},{1,17},{2,18},{3,19},{4,20},{5,21},{6,22},{7,23},{8,24},{9,... | collective-permute-start | bytes 786440 | tf_op jit(solution)/shard_map/ppermute | solution.py:693
  202.4 5.2 %collective-permute-start.25 = (bf16[80,512]{1,0:T(8,128)(2,1)S(1)}, bf16[80,512]{1,0:T(8,128)(2,1)S(1)}, u32[]{:S(2)}, u32[]{:S(2)}) collective-permute-start(bf16[80,512]{1,0:T(8,128)(2,1)S(1)} %get-tuple-element.310), channel_id=1, source_target_pairs={{0,2},{1,3},{2,0},{3,1},{4,6},{5,7},{6,4},{7,5},{8,10},{9,11},{10,... | collective-permute-start | bytes 245768 | tf_op jit(solution)/shard_map/ppermute | solution.py:693
  202.5 8.8 %collective-permute-start.26 = (bf16[80,512]{1,0:T(8,128)(2,1)S(1)}, bf16[80,512]{1,0:T(8,128)(2,1)S(1)}, u32[]{:S(2)}, u32[]{:S(2)}) collective-permute-start(bf16[80,512]{1,0:T(8,128)(2,1)S(1)} %get-tuple-element.311), channel_id=1, source_target_pairs={{0,4},{1,5},{2,6},{3,7},{4,0},{5,1},{6,2},{7,3},{8,12},{9,13},{10,... | collective-permute-start | bytes 245768 | tf_op jit(solution)/shard_map/ppermute | solution.py:693
  206.4 6.3 %collective-permute-start.27 = (bf16[80,512]{1,0:T(8,128)(2,1)S(1)}, bf16[80,512]{1,0:T(8,128)(2,1)S(1)}, u32[]{:S(2)}, u32[]{:S(2)}) collective-permute-start(bf16[80,512]{1,0:T(8,128)(2,1)S(1)} %get-tuple-element.312), channel_id=1, source_target_pairs={{0,6},{1,7},{2,4},{3,5},{4,2},{5,3},{6,0},{7,1},{8,14},{9,15},{10,... | collective-permute-start | bytes 245768 | tf_op jit(solution)/shard_map/ppermute | solution.py:693
  213.5 19.9 %collective-permute-start.36 = (bf16[512,512]{1,0:T(8,128)(2,1)}, bf16[512,512]{1,0:T(8,128)(2,1)}, u32[]{:S(2)}, u32[]{:S(2)}) collective-permute-start(bf16[512,512]{1,0:T(8,128)(2,1)} %constant_dynamic-update-slice_fusion.refs_2_), channel_id=1, source_target_pairs={{0,8},{1,9},{2,10},{3,11},{4,12},{5,13},{6,14},{7,15},{8,0},{9,1},... | collective-permute-start | bytes 1572872 | tf_op jit(solution)/shard_map/ppermute | solution.py:693
  213.5 19.9 %collective-permute-start.32 = (bf16[512,512]{1,0:T(8,128)(2,1)}, bf16[512,512]{1,0:T(8,128)(2,1)}, u32[]{:S(2)}, u32[]{:S(2)}) collective-permute-start(bf16[512,512]{1,0:T(8,128)(2,1)} %constant_dynamic-update-slice_fusion.refs_2_), channel_id=1, source_target_pairs={{0,1},{1,0},{2,3},{3,2},{4,5},{5,4},{6,7},{7,6},{8,9},{9,8},{10,11... | collective-permute-start | bytes 1572872 | tf_op jit(solution)/shard_map/ppermute | solution.py:693
  215.8 17.5 %collective-permute-start.35 = (bf16[512,512]{1,0:T(8,128)(2,1)}, bf16[512,512]{1,0:T(8,128)(2,1)}, u32[]{:S(2)}, u32[]{:S(2)}) collective-permute-start(bf16[512,512]{1,0:T(8,128)(2,1)} %pad_maximum_fusion.refs_0_), channel_id=1, source_target_pairs={{0,8},{1,9},{2,10},{3,11},{4,12},{5,13},{6,14},{7,15},{8,0},{9,1},... | collective-permute-start | bytes 1572872 | tf_op jit(solution)/shard_map/ppermute | solution.py:693
  216.0 17.3 %collective-permute-start.31 = (bf16[512,512]{1,0:T(8,128)(2,1)}, bf16[512,512]{1,0:T(8,128)(2,1)}, u32[]{:S(2)}, u32[]{:S(2)}) collective-permute-start(bf16[512,512]{1,0:T(8,128)(2,1)} %pad_maximum_fusion.refs_0_), channel_id=1, source_target_pairs={{0,16},{1,17},{2,18},{3,19},{4,20},{5,21},{6,22},{7,23},{8,24},{9,... | collective-permute-start | bytes 1572872 | tf_op jit(solution)/shard_map/ppermute | solution.py:693
  217.4 4.3 %collective-permute-start.33 = (bf16[64,512]{1,0:T(8,128)(2,1)S(1)}, bf16[64,512]{1,0:T(8,128)(2,1)S(1)}, u32[]{:S(2)}, u32[]{:S(2)}) collective-permute-start(bf16[64,512]{1,0:T(8,128)(2,1)S(1)} %get-tuple-element.323), channel_id=1, source_target_pairs={{0,2},{1,3},{2,0},{3,1},{4,6},{5,7},{6,4},{7,5},{8,10},{9,11},{10,... | collective-permute-start | bytes 196616 | tf_op jit(solution)/shard_map/ppermute | solution.py:693
  221.8 0.6 copy-start.8
  223.0 8.7 %collective-permute-start.34 = (bf16[128,512]{1,0:T(8,128)(2,1)}, bf16[128,512]{1,0:T(8,128)(2,1)}, u32[]{:S(2)}, u32[]{:S(2)}) collective-permute-start(bf16[128,512]{1,0:T(8,128)(2,1)} %constant_dynamic-update-slice_fusion.2), channel_id=1, source_target_pairs={{0,4},{1,5},{2,6},{3,7},{4,0},{5,1},{6,2},{7,3},{8,12},{9,13},{10,... | collective-permute-start | bytes 393224 | tf_op jit(solution)/shard_map/ppermute | solution.py:693
  233.4 30.1 %all-to-all-start = ((bf16[4,256,512]{2,1,0:T(8,128)(2,1)}), bf16[4,256,512]{2,1,0:T(8,128)(2,1)}, u32[]{:S(2)}, u32[]{:S(2)}) async-start(bf16[4,256,512]{2,1,0:T(8,128)(2,1)} %bitcast.35), calls=%async_computation | async-start | bytes 2097152 | tf_op jit(solution)/shard_map/all_to_all | solution.py:881
  237.8 4.1 %collective-permute-start.40 = (bf16[512,512]{1,0:T(8,128)(2,1)}, bf16[512,512]{1,0:T(8,128)(2,1)S(1)}, u32[]{:S(2)}, u32[]{:S(2)}) collective-permute-start(bf16[512,512]{1,0:T(8,128)(2,1)} %collective-permute-done.31.refs_1_), channel_id=1, source_target_pairs={{0,8},{1,9},{2,10},{3,11},{4,12},{5,13},{6,14},{7,15},{8,0},{9,1},... | collective-permute-start | bytes 1572872 | tf_op jit(solution)/shard_map/ppermute | solution.py:693
  237.9 4.0 %collective-permute-start.41 = (bf16[512,512]{1,0:T(8,128)(2,1)}, bf16[512,512]{1,0:T(8,128)(2,1)S(1)}, u32[]{:S(2)}, u32[]{:S(2)}) collective-permute-start(bf16[512,512]{1,0:T(8,128)(2,1)} %collective-permute-done.32.refs_3_), channel_id=1, source_target_pairs={{0,8},{1,9},{2,10},{3,11},{4,12},{5,13},{6,14},{7,15},{8,0},{9,1},... | collective-permute-start | bytes 1572872 | tf_op jit(solution)/shard_map/ppermute | solution.py:693
  238.4 10.4 %collective-permute-start.39 = (bf16[256,512]{1,0:T(8,128)(2,1)}, bf16[256,512]{1,0:T(8,128)(2,1)}, u32[]{:S(2)}, u32[]{:S(2)}) collective-permute-start(bf16[256,512]{1,0:T(8,128)(2,1)} %pad_maximum_fusion.2.refs_0_), channel_id=1, source_target_pairs={{0,17},{1,16},{2,19},{3,18},{4,21},{5,20},{6,23},{7,22},{8,25},{9,... | collective-permute-start | bytes 786440 | tf_op jit(solution)/shard_map/ppermute | solution.py:693
  239.5 13.0 %collective-permute-start.38 = (bf16[256,512]{1,0:T(8,128)(2,1)}, bf16[256,512]{1,0:T(8,128)(2,1)}, u32[]{:S(2)}, u32[]{:S(2)}) collective-permute-start(bf16[256,512]{1,0:T(8,128)(2,1)} %pad_maximum_fusion.2.refs_0_), channel_id=1, source_target_pairs={{0,16},{1,17},{2,18},{3,19},{4,20},{5,21},{6,22},{7,23},{8,24},{9,... | collective-permute-start | bytes 786440 | tf_op jit(solution)/shard_map/ppermute | solution.py:693
  240.3 13.2 %collective-permute-start.37 = (bf16[256,512]{1,0:T(8,128)(2,1)}, bf16[256,512]{1,0:T(8,128)(2,1)}, u32[]{:S(2)}, u32[]{:S(2)}) collective-permute-start(bf16[256,512]{1,0:T(8,128)(2,1)} %pad_maximum_fusion.2.refs_0_), channel_id=1, source_target_pairs={{0,1},{1,0},{2,3},{3,2},{4,5},{5,4},{6,7},{7,6},{8,9},{9,8},{10,11... | collective-permute-start | bytes 786440 | tf_op jit(solution)/shard_map/ppermute | solution.py:693
  241.8 26.0 %collective-permute-start.42 = (bf16[256,512]{1,0:T(8,128)(2,1)}, bf16[256,512]{1,0:T(8,128)(2,1)}, u32[]{:S(2)}, u32[]{:S(2)}) collective-permute-start(bf16[256,512]{1,0:T(8,128)(2,1)} %pad_maximum_fusion.2.refs_0_), channel_id=1, source_target_pairs={{0,8},{1,9},{2,10},{3,11},{4,12},{5,13},{6,14},{7,15},{8,0},{9,1},... | collective-permute-start | bytes 786440 | tf_op jit(solution)/shard_map/ppermute | solution.py:693
  263.4 4.4 %collective-permute-start.43 = (bf16[256,512]{1,0:T(8,128)(2,1)}, bf16[256,512]{1,0:T(8,128)(2,1)}, u32[]{:S(2)}, u32[]{:S(2)}) collective-permute-start(bf16[256,512]{1,0:T(8,128)(2,1)} %collective-permute-done.37.refs_1_), channel_id=1, source_target_pairs={{0,8},{1,9},{2,10},{3,11},{4,12},{5,13},{6,14},{7,15},{8,0},{9,1},... | collective-permute-start | bytes 786440 | tf_op jit(solution)/shard_map/ppermute | solution.py:693
  263.4 4.4 %collective-permute-start.44 = (bf16[256,512]{1,0:T(8,128)(2,1)}, bf16[256,512]{1,0:T(8,128)(2,1)}, u32[]{:S(2)}, u32[]{:S(2)}) collective-permute-start(bf16[256,512]{1,0:T(8,128)(2,1)} %collective-permute-done.38.refs_2_), channel_id=1, source_target_pairs={{0,8},{1,9},{2,10},{3,11},{4,12},{5,13},{6,14},{7,15},{8,0},{9,1},... | collective-permute-start | bytes 786440 | tf_op jit(solution)/shard_map/ppermute | solution.py:693
  263.9 3.9 %collective-permute-start.45 = (bf16[256,512]{1,0:T(8,128)(2,1)}, bf16[256,512]{1,0:T(8,128)(2,1)}, u32[]{:S(2)}, u32[]{:S(2)}) collective-permute-start(bf16[256,512]{1,0:T(8,128)(2,1)} %collective-permute-done.39.refs_3_), channel_id=1, source_target_pairs={{0,8},{1,9},{2,10},{3,11},{4,12},{5,13},{6,14},{7,15},{8,0},{9,1},... | collective-permute-start | bytes 786440 | tf_op jit(solution)/shard_map/ppermute | solution.py:693

commit v2 on v1

--- a/solution.py
+++ b/solution.py
@@ -883,11 +883,11 @@
     mine = [two_a, last_a, two_b, last_b]
     other = [other_a, sums.to_core(last_a), other_b, sums.to_core(last_b)]
     d_w_down, d_w_up = sums.unpack(mine, other, [(hidden, width), (width, hidden)], crossed=True)
-    small_got, d_lat_back, d_w_up = lax.optimization_barrier((small_got, d_lat_back, d_w_up))
+    small_got = after(small_got, d_w_up)
     small_mine = [small_block, *small_got]
     small_other = [sums.to_core(v) for v in small_mine]
-    d_latents = unsort_rows(0 * scene_info, [after(d_lat_back, small_mine)], scenes, F32)
-    squares = sums.unpack(small_mine, after(small_other, d_latents), [(width, width)] * 4)
+    squares = sums.unpack(small_mine, small_other, [(width, width)] * 4)
+    d_latents = unsort_rows(0 * scene_info, [after(d_lat_back, *squares)], scenes, F32)
     gains = gains.astype(F32)
     return (output[None], d_latents[None], d_tokens[None], *squares, d_w_up, d_w_down, gains[0], gains[1], gains[2])
 

time: 276 us -> 270 us (0.978)
  waiting for transfers between devices: 53.1 us -> 49.6 us
    all_to_all x1, waiting for transfers between devices: 9.95 us -> 5.4 us  [local(): lax.all_to_all(leaving, 'blk', 0, 0, axis_index_groups=lines, tiled=True)]
  transfers between devices with their start and end apart: 47 -> 47, of which waited for: 15 -> 18; matrix products, arithmetic and copies ran while one was open for 6% -> 6% of each run, Pallas kernels for 44% -> 45%
where the time goes in v2:
time: 270 us; the launch traced here: 266 us
  Pallas kernels  124 us (46%)
  starting transfers between devices  65.8 us (24%)
  waiting for transfers between devices  49.6 us (18%)
  local copies, waits for them, and re-layouts  13.3 us (5%)
  other arithmetic  11.4 us (4%)
    pallas_call x11, Pallas kernels, hbm_call(): pl.pallas_call(body, in_specs=[pl.BlockSpec(memory_space=pltpu.SMEM)] * s...  105 us
    ppermute x44, starting transfers between devices, flip(): return lax.ppermute(value, ('seq', 'blk'), pairs)  52.4 us
    ppermute x44, waiting for transfers between devices, flip(): return lax.ppermute(value, ('seq', 'blk'), pairs)  44.2 us
    pallas_call x8, Pallas kernels, vmem_call(): pl.pallas_call(kernel, in_specs=[in_smem] * smem + [in_vmem] * (len(args)...  18.7 us
    unnamed x20, local copies, waits for them, and re-layouts  8.21 us
    ppermute x1, starting transfers between devices, local(): tail = lax.ppermute(sent, 'blk', pairs)  7.52 us
    all_to_all x1, waiting for transfers between devices, local(): lax.all_to_all(leaving, 'blk', 0, 0, axis_index_groups=lines, tiled=True)  5.4 us
  transfers between devices with their start and end apart: 47, of which 18 were waited for; matrix products, arithmetic and copies ran while one was open for 6% of the time, Pallas kernels for 45%

profile of v2, /device:TPU:0, one launch (start us, length us, event | category | flops | bytes accessed | tf_op | source)
XLA Modules:
  0.0 266.2 jit_solution(12661173542426970973)
XLA Ops:
  0.6 3.0 %collective-permute-start.3 = (bf16[1024,512]{1,0:T(8,128)(2,1)}, bf16[1024,512]{1,0:T(8,128)(2,1)}, u32[]{:S(2)}, u32[]{:S(2)}) collective-permute-start(bf16[1024,512]{1,0:T(8,128)(2,1)} %bitcast.25), channel_id=1, source_target_pairs={{0,1},{1,0},{2,3},{3,2},{4,5},{5,4},{6,7},{7,6},{8,9},{9,8},{10,11... | collective-permute-start | bytes 3145736 | tf_op jit(solution)/shard_map/ppermute | solution.py:693
  3.7 2.8 %sort_rows.2 = (bf16[256,512]{1,0:T(8,128)(2,1)}, bf16[256,512]{1,0:T(8,128)(2,1)}, bf16[256,512]{1,0:T(8,128)(2,1)}, bf16[256,512]{1,0:T(8,128)(2,1)}) custom-call(s32[1]{0:T(128)} %bitcast.2.refs_0_, bf16[1024,512]{1,0:T(8,128)(2,1)} %bitcast.33), custom_call_target="tpu_custom_call" | custom-call | tf_op jit(solution)/shard_map/sort_rows/pallas_call | solution.py:140
  6.5 1.6 collective-permute-start
  8.1 2.6 collective-permute-start.1
  10.9 1.3 fusion.2
  12.2 2.8 %sort_rows.3 = (bf16[256,512]{1,0:T(8,128)(2,1)}, bf16[256,512]{1,0:T(8,128)(2,1)}, bf16[256,512]{1,0:T(8,128)(2,1)}, bf16[256,512]{1,0:T(8,128)(2,1)}) custom-call(s32[1]{0:T(128)} %bitcast.2.refs_0_, bf16[1024,512]{1,0:T(8,128)(2,1)} %bitcast.34), custom_call_target="tpu_custom_call" | custom-call | tf_op jit(solution)/shard_map/sort_rows/pallas_call | solution.py:140
  16.4 1.3 stack.65.refs_0_
  17.6 1.9 stack.66.refs_0_
  19.5 4.2 %keys_values.1 = (bf16[1024,512]{1,0:T(8,128)(2,1)}, bf16[1024,512]{1,0:T(8,128)(2,1)}) custom-call(bf16[1024,512]{1,0:T(8,128)(2,1)} %bitcast.26, f32[1,512]{1,0:T(1,128)} %bitcast.36, bf16[512,512]{1,0:T(8,128)(2,1)} %refs_2_.7, bf16[512,512]{1,0:T(8,128)(2,1)} %refs_3_.7), custom_call_target="tpu_custom_call" | custom-call | tf_op jit(solution)/shard_map/keys_values/pallas_call | solution.py:140
  23.8 1.3 pad_add_fusion.1.refs_0_
  25.0 1.3 pad_add_fusion.2.refs_0_
  26.3 3.5 %collective-permute-done.1.refs_9_ = bf16[256,512]{1,0:T(8,128)(2,1)} collective-permute-done((bf16[256,512]{1,0:T(8,128)(2,1)}, bf16[256,512]{1,0:T(8,128)(2,1)}, u32[]{:S(2)}, u32[]{:S(2)}) %collective-permute-start.1) | collective-permute-done | bytes 262176 | tf_op jit(solution)/shard_map/ppermute | solution.py:693
  29.8 2.3 slice_select_fusion
  32.2 7.5 %collective-permute-start.4 = (bf16[768,512]{1,0:T(8,128)(2,1)}, bf16[768,512]{1,0:T(8,128)(2,1)}, u32[]{:S(2)}, u32[]{:S(2)}) collective-permute-start(bf16[768,512]{1,0:T(8,128)(2,1)} %slice_select_fusion), channel_id=1, source_target_pairs={{0,2},{1,3},{2,4},{3,5},{4,6},{5,7},{8,10},{9,11},{10,12},{11,13},... | collective-permute-start | bytes 2359304 | tf_op jit(solution)/shard_map/ppermute | solution.py:791
  40.5 12.3 %attend.1 = (bf16[1024,512]{1,0:T(8,128)(2,1)}, f32[1024,512]{1,0:T(8,128)}, f32[8,1024]{1,0:T(8,128)}, f32[8,1024]{1,0:T(8,128)}, bf16[1024,512]{1,0:T(8,128)(2...) custom-call(s32[4]{0:T(128)} %pad_add_fusion.1.refs_0_, ...), custom_call_target="tpu_custom_call" | custom-call | tf_op jit(solution)/shard_map/attend/pallas_call | solution.py:140
  52.8 7.5 %collective-permute-done.5.refs_2_ = bf16[256,512]{1,0:T(8,128)(2,1)} collective-permute-done((bf16[256,512]{1,0:T(8,128)(2,1)}, bf16[256,512]{1,0:T(8,128)(2,1)}, u32[]{:S(2)}, u32[]{:S(2)}) %collective-permute-start.5) | collective-permute-done | bytes 262176 | tf_op jit(solution)/shard_map/ppermute | solution.py:693
  61.1 4.0 %collective-permute-start.7 = (bf16[256,512]{1,0:T(8,128)(2,1)}, bf16[256,512]{1,0:T(8,128)(2,1)}, u32[]{:S(2)}, u32[]{:S(2)}) collective-permute-start(bf16[256,512]{1,0:T(8,128)(2,1)} %get-tuple-element.205), channel_id=1, source_target_pairs={{0,6},{1,7},{2,4},{3,5},{4,2},{5,3},{6,0},{7,1},{8,14},{9,15},{10,... | collective-permute-start | bytes 786440 | tf_op jit(solution)/shard_map/ppermute | solution.py:693
  65.1 18.4 %finish.1 = (bf16[768,512]{1,0:T(8,128)(2,1)}, bf16[768,512]{1,0:T(8,128)(2,1)}, bf16[768,1024]{1,0:T(8,128)(2,1)}, f32[1024,128]{1,0:T(8,128)}, bf16[1024,512]{...) custom-call(s32[3]{0:T(128)} %pad_add_fusion.2.refs_0_, ...), custom_call_target="tpu_custom_call" | custom-call | tf_op jit(solution)/shard_map/finish/pallas_call | solution.py:140
  84.1 1.5 collective-permute-start.9
  85.7 2.4 collective-permute-start.10
  88.6 21.1 %mlp_back.1 = (f32[1024,512]{1,0:T(8,128)}, bf16[1024,512]{1,0:T(8,128)(2,1)}, bf16[1024,512]{1,0:T(8,128)(2,1)}, f32[8,1024]{1,0:T(8,128)}, f32[8,1024]{1,0:T(8...) custom-call(s32[7]{0:T(128)} %pad_add_fusion.refs_0_.info_ref, ...), custom_call_target="tpu_custom_call" | custom-call | tf_op jit(solution)/shard_map/mlp_back/pallas_call | solution.py:140
  109.9 7.3 %attention_back.2 = (bf16[768,512]{1,0:T(8,128)(2,1)}, f32[1024,512]{1,0:T(8,128)}, f32[512,512]{1,0:T(8,128)}, f32[512,512]{1,0:T(8,128)}, f32[8,512]{1,0:T(8,128)}) custom-call(s32[5]{0:T(128)} %stack.65.refs_0_, bf16[1024,512]{1,0:T(8,128)(2,1)} %get-tuple-element.209.refs_6_.refs_1_, bf16[512,512]{1,0:T(8,128)(2,1)} %refs_2_.7, ...), custom_call_target="tpu_custom_call" | custom-call | tf_op jit(solution)/shard_map/attention_back/pallas_call | solution.py:140
  117.2 1.5 collective-permute-start.15
  118.8 1.6 copy-done
  120.3 3.1 %split_sum.6 = (bf16[512,512]{1,0:T(8,128)(2,1)S(1)}, bf16[512,512]{1,0:T(8,128)(2,1)}, bf16[512,512]{1,0:T(8,128)(2,1)}, bf16[512,512]{1,0:T(8,128)(2,1)}) custom-call(s32[7]{0:T(128)S(1)} %copy-done.6, bf16[2048,512]{1,0:T(8,128)(2,1)S(1)} %copy-done, bf16[2048,512]{1,0:T(8,128)(2,1)} %collective-permute-done.11.refs_1_), custom_call_target="tpu_custom_call" | custom-call | tf_op jit(solution)/shard_map/split_sum/pallas_call | solution.py:46
  124.7 1.5 collective-permute-start.13
  126.3 1.5 collective-permute-start.14
  127.7 24.8 %attention_back.3 = (bf16[1024,512]{1,0:T(8,128)(2,1)}, bf16[1024,512]{1,0:T(8,128)(2,1)}, bf16[1024,512]{1,0:T(8,128)(2,1)}, bf16[1040,512]{1,0:T(8,128)(2,1)}, bf16[1040,512]{1,0:T(8,128)(2,1)}) custom-call(s32[8]{0:T(128)} %stack.66.refs_0_, bf16[1024,512]{1,0:T(8,128)(2,1)} %get-tuple-element.209.refs_6_.refs_1_, bf16[512,512]{1,0:T(8,128)(2,1)} %refs_2_.7, ...), custom_call_target="tpu_custom_call" | custom-call | tf_op jit(solution)/shard_map/attention_back/pallas_call | solution.py:140
  152.7 1.0 copy-done.3
  153.7 2.3 split_sum.7
  156.7 2.8 %pad_select_fusion = (bf16[1024,512]{1,0:T(8,128)(2,1)}, bf16[1024,512]{1,0:T(8,128)(2,1)}) fusion(bf16[768,512]{1,0:T(8,128)(2,1)} %collective-permute-done.15, pred[]{:T(512)S(6)} %eq.16, bf16[1024,512]{1,0:T(8,128)(2,1)S(1)} %copy-done.7, pred[]{:T(512)S(6)} %eq.18), kind=kLoop, calls=%fused_computation | loop fusion | flops 3145728 | bytes 3932162 | tf_op jit(solution)/shard_map/jit(_where)/select_n | solution.py:844
  160.1 1.4 collective-permute-start.17
  161.4 5.2 %collective-permute-start.18 = (bf16[128,512]{1,0:T(8,128)(2,1)}, bf16[128,512]{1,0:T(8,128)(2,1)}, u32[]{:S(2)}, u32[]{:S(2)}) collective-permute-start(bf16[128,512]{1,0:T(8,128)(2,1)} %get-tuple-element.280), channel_id=1, source_target_pairs={{0,4},{1,5},{2,6},{3,7},{4,0},{5,1},{6,2},{7,3},{8,12},{9,13},{10,... | collective-permute-start | bytes 393224 | tf_op jit(solution)/shard_map/ppermute | solution.py:693
  166.6 3.2 %unsort_rows.2 = bf16[1024,512]{1,0:T(8,128)(2,1)} custom-call(s32[1]{0:T(128)} %bitcast.2.refs_0_, bf16[256,512]{1,0:T(8,128)(2,1)} %get-tuple-element.287.refs_1_, bf16[256,512]{1,0:T(8,128)(2,1)} %collective-permute-done.8.refs_2_, bf16[256,512]{1,0:T(8,128)(2,1)} %collective-permute-done.9.refs_3_, bf16[256,512]{1,0:T(8,128)(2,1)} %collective-permute-done.10.refs_4_), custom_call_target="tpu_custom_call" | custom-call | tf_op jit(solution)/shard_map/unsort_rows/pallas_call | solution.py:140
  169.8 7.1 %collective-permute-done.18.refs_2_ = bf16[128,512]{1,0:T(8,128)(2,1)} collective-permute-done((bf16[128,512]{1,0:T(8,128)(2,1)}, bf16[128,512]{1,0:T(8,128)(2,1)}, u32[]{:S(2)}, u32[]{:S(2)}) %collective-permute-start.18) | collective-permute-done | bytes 131104 | tf_op jit(solution)/shard_map/ppermute | solution.py:693
  177.8 1.1 split_sum.8
  178.9 2.4 collective-permute-start.20
  181.4 1.2 copy-done.1
  182.6 1.5 split_sum.9
  184.1 1.6 collective-permute-start.21
  185.7 1.1 collective-permute-start.22
  187.7 1.0 collective-permute-start.24
  188.7 4.8 %collective-permute-done.21.refs_1_ = bf16[272,512]{1,0:T(8,128)(2,1)S(1)} collective-permute-done((bf16[272,512]{1,0:T(8,128)(2,1)S(1)}, bf16[272,512]{1,0:T(8,128)(2,1)S(1)}, u32[]{:S(2)}, u32[]{:S(2)}) %collective-permute-start.21) | collective-permute-done | bytes 278560 | tf_op jit(solution)/shard_map/ppermute | solution.py:693
  193.5 1.5 collective-permute-start.28
  195.2 3.5 %collective-permute-done.23.refs_3_ = bf16[272,512]{1,0:T(8,128)(2,1)S(1)} collective-permute-done((bf16[272,512]{1,0:T(8,128)(2,1)S(1)}, bf16[272,512]{1,0:T(8,128)(2,1)S(1)}, u32[]{:S(2)}, u32[]{:S(2)}) %collective-permute-start.23) | collective-permute-done | bytes 278560 | tf_op jit(solution)/shard_map/ppermute | solution.py:693
  198.8 1.5 collective-permute-done.24
  200.2 1.3 collective-permute-start.29
  202.3 3.7 %collective-permute-start.26 = (bf16[80,512]{1,0:T(8,128)(2,1)S(1)}, bf16[80,512]{1,0:T(8,128)(2,1)S(1)}, u32[]{:S(2)}, u32[]{:S(2)}) collective-permute-start(bf16[80,512]{1,0:T(8,128)(2,1)S(1)} %get-tuple-element.306), channel_id=1, source_target_pairs={{0,4},{1,5},{2,6},{3,7},{4,0},{5,1},{6,2},{7,3},{8,12},{9,13},{10,... | collective-permute-start | bytes 245768 | tf_op jit(solution)/shard_map/ppermute | solution.py:693
  207.5 3.6 %collective-permute-done.26.refs_2_ = bf16[80,512]{1,0:T(8,128)(2,1)S(1)} collective-permute-done((bf16[80,512]{1,0:T(8,128)(2,1)S(1)}, bf16[80,512]{1,0:T(8,128)(2,1)S(1)}, u32[]{:S(2)}, u32[]{:S(2)}) %collective-permute-start.26) | collective-permute-done | bytes 81952 | tf_op jit(solution)/shard_map/ppermute | solution.py:693
  211.1 1.3 collective-permute-done.27.refs_3_
  213.1 1.5 collective-permute-start.32
  218.7 2.8 %collective-permute-done.33 = bf16[64,512]{1,0:T(8,128)(2,1)S(1)} collective-permute-done((bf16[64,512]{1,0:T(8,128)(2,1)S(1)}, bf16[64,512]{1,0:T(8,128)(2,1)S(1)}, u32[]{:S(2)}, u32[]{:S(2)}) %collective-permute-start.33) | collective-permute-done | bytes 65568 | tf_op jit(solution)/shard_map/ppermute | solution.py:693
  222.8 1.6 collective-permute-start.34
  224.4 4.5 %token_back.1 = f32[1024,512]{1,0:T(8,128)} custom-call(bf16[1024,512]{1,0:T(8,128)(2,1)} %bitcast.29, f32[1,512]{1,0:T(1,128)} %bitcast.41, bf16[1024,512]{1,0:T(8,128)(2,1)} %get-tuple-element.319.refs_2_, bf16[1024,512]{1,0:T(8,128)(2,1)} %get-tuple-element.342.refs_3_, bf16[1024,512]{1,0:T(8,128)(2,1)} %collective-permute-done.30.refs_4_), custom_call_target="tpu_custom_call" | custom-call | tf_op jit(solution)/shard_map/token_back/pallas_call | solution.py:140
  228.9 2.5 collective-permute-done.34
  232.4 4.4 %all-to-all-start = ((bf16[4,256,512]{2,1,0:T(8,128)(2,1)}), bf16[4,256,512]{2,1,0:T(8,128)(2,1)}, u32[]{:S(2)}, u32[]{:S(2)}) async-start(bf16[4,256,512]{2,1,0:T(8,128)(2,1)} %bitcast.35), calls=%async_computation | async-start | bytes 2097152 | tf_op jit(solution)/shard_map/all_to_all | solution.py:881
  237.4 1.0 collective-permute-start.39
  238.5 0.9 collective-permute-start.38
  239.4 1.5 collective-permute-start.37
  240.9 6.6 %unpack.2 = (f32[2048,512]{1,0:T(8,128)}, f32[512,2048]{1,0:T(8,128)}) custom-call(s32[7]{0:T(128)S(1)} %copy-done.6, bf16[512,512]{1,0:T(8,128)(2,1)} %pad_maximum_fusion.refs_0_, bf16[512,512]{1,0:T(8,128)(2,1)} %collective-permute-done.31.refs_1_, bf16[512,512]{1,0:T(8,128)(2,1)} %constant_dynamic-update-slice_fusion.refs_2_, ...), custom_call_target="tpu_custom_call" | custom-call | tf_op jit(solution)/shard_map/unpack/pallas_call | solution.py:46
  247.6 3.7 %collective-permute-done.38.refs_2_ = bf16[256,512]{1,0:T(8,128)(2,1)S(1)} collective-permute-done((bf16[256,512]{1,0:T(8,128)(2,1)S(1)}, bf16[256,512]{1,0:T(8,128)(2,1)S(1)}, u32[]{:S(2)}, u32[]{:S(2)}) %collective-permute-start.38) | collective-permute-done | bytes 262176 | tf_op jit(solution)/shard_map/ppermute | solution.py:693
  254.5 2.8 %unpack.3 = (f32[512,512]{1,0:T(8,128)}, f32[512,512]{1,0:T(8,128)}, f32[512,512]{1,0:T(8,128)}, f32[512,512]{1,0:T(8,128)}) custom-call(s32[7]{0:T(128)S(1)} %copy-done.6, bf16[256,512]{1,0:T(8,128)(2,1)S(1)} %pad_maximum_fusion.2.refs_0_, bf16[256,512]{1,0:T(8,128)(2,1)S(1)} %collective-permute-done.37.refs_1_, ...), custom_call_target="tpu_custom_call" | custom-call | tf_op jit(solution)/shard_map/unpack/pallas_call | solution.py:46
  257.3 5.4 %all-to-all-done = bf16[4,256,512]{2,1,0:T(8,128)(2,1)} async-done(((bf16[4,256,512]{2,1,0:T(8,128)(2,1)}), bf16[4,256,512]{2,1,0:T(8,128)(2,1)}, u32[]{:S(2)}, u32[]{:S(2)}) %all-to-all-start) | async-done | bytes 1048608 | tf_op jit(solution)/shard_map/all_to_all | solution.py:881
  262.7 3.3 %unsort_rows.3 = f32[1024,512]{1,0:T(8,128)} custom-call(s32[1]{0:T(128)} %constant.61.clone.1.refs_0_, bf16[1024,512]{1,0:T(8,128)(2,1)} %bitcast.17.refs_1_), custom_call_target="tpu_custom_call" | custom-call | tf_op jit(solution)/shard_map/unsort_rows/pallas_call | solution.py:140
  (84 shorter events, 20.7 us)
Async XLA Ops:
  0.6 29.2 %collective-permute-start.3 = (bf16[1024,512]{1,0:T(8,128)(2,1)}, bf16[1024,512]{1,0:T(8,128)(2,1)}, u32[]{:S(2)}, u32[]{:S(2)}) collective-permute-start(bf16[1024,512]{1,0:T(8,128)(2,1)} %bitcast.25), channel_id=1, source_target_pairs={{0,1},{1,0},{2,3},{3,2},{4,5},{5,4},{6,7},{7,6},{8,9},{9,8},{10,11... | collective-permute-start | bytes 3145736 | tf_op jit(solution)/shard_map/ppermute | solution.py:693
  6.5 19.8 %collective-permute-start = (bf16[256,512]{1,0:T(8,128)(2,1)}, bf16[256,512]{1,0:T(8,128)(2,1)}, u32[]{:S(2)}, u32[]{:S(2)}) collective-permute-start(bf16[256,512]{1,0:T(8,128)(2,1)} %get-tuple-element.177), channel_id=1, source_target_pairs={{0,2},{1,3},{2,0},{3,1},{4,6},{5,7},{6,4},{7,5},{8,10},{9,11},{10,... | collective-permute-start | bytes 786440 | tf_op jit(solution)/shard_map/ppermute | solution.py:693
  8.1 21.7 %collective-permute-start.1 = (bf16[256,512]{1,0:T(8,128)(2,1)}, bf16[256,512]{1,0:T(8,128)(2,1)}, u32[]{:S(2)}, u32[]{:S(2)}) collective-permute-start(bf16[256,512]{1,0:T(8,128)(2,1)} %get-tuple-element.178), channel_id=1, source_target_pairs={{0,4},{1,5},{2,6},{3,7},{4,0},{5,1},{6,2},{7,3},{8,12},{9,13},{10,... | collective-permute-start | bytes 786440 | tf_op jit(solution)/shard_map/ppermute | solution.py:693
  10.7 19.1 %collective-permute-start.2 = (bf16[256,512]{1,0:T(8,128)(2,1)}, bf16[256,512]{1,0:T(8,128)(2,1)}, u32[]{:S(2)}, u32[]{:S(2)}) collective-permute-start(bf16[256,512]{1,0:T(8,128)(2,1)} %get-tuple-element.179), channel_id=1, source_target_pairs={{0,6},{1,7},{2,4},{3,5},{4,2},{5,3},{6,0},{7,1},{8,14},{9,15},{10,... | collective-permute-start | bytes 786440 | tf_op jit(solution)/shard_map/ppermute | solution.py:693
  32.2 28.1 %collective-permute-start.4 = (bf16[768,512]{1,0:T(8,128)(2,1)}, bf16[768,512]{1,0:T(8,128)(2,1)}, u32[]{:S(2)}, u32[]{:S(2)}) collective-permute-start(bf16[768,512]{1,0:T(8,128)(2,1)} %slice_select_fusion), channel_id=1, source_target_pairs={{0,2},{1,3},{2,4},{3,5},{4,6},{5,7},{8,10},{9,11},{10,12},{11,13},... | collective-permute-start | bytes 2359304 | tf_op jit(solution)/shard_map/ppermute | solution.py:791
  39.7 20.6 %collective-permute-start.5 = (bf16[256,512]{1,0:T(8,128)(2,1)}, bf16[256,512]{1,0:T(8,128)(2,1)}, u32[]{:S(2)}, u32[]{:S(2)}) collective-permute-start(bf16[256,512]{1,0:T(8,128)(2,1)} %get-tuple-element.199), channel_id=1, source_target_pairs={{0,2},{1,3},{2,0},{3,1},{4,6},{5,7},{6,4},{7,5},{8,10},{9,11},{10,... | collective-permute-start | bytes 786440 | tf_op jit(solution)/shard_map/ppermute | solution.py:693
  60.3 23.3 %collective-permute-start.6 = (bf16[256,512]{1,0:T(8,128)(2,1)}, bf16[256,512]{1,0:T(8,128)(2,1)}, u32[]{:S(2)}, u32[]{:S(2)}) collective-permute-start(bf16[256,512]{1,0:T(8,128)(2,1)} %get-tuple-element.204), channel_id=1, source_target_pairs={{0,4},{1,5},{2,6},{3,7},{4,0},{5,1},{6,2},{7,3},{8,12},{9,13},{10,... | collective-permute-start | bytes 786440 | tf_op jit(solution)/shard_map/ppermute | solution.py:693
  61.1 22.4 %collective-permute-start.7 = (bf16[256,512]{1,0:T(8,128)(2,1)}, bf16[256,512]{1,0:T(8,128)(2,1)}, u32[]{:S(2)}, u32[]{:S(2)}) collective-permute-start(bf16[256,512]{1,0:T(8,128)(2,1)} %get-tuple-element.205), channel_id=1, source_target_pairs={{0,6},{1,7},{2,4},{3,5},{4,2},{5,3},{6,0},{7,1},{8,14},{9,15},{10,... | collective-permute-start | bytes 786440 | tf_op jit(solution)/shard_map/ppermute | solution.py:693
  83.6 26.2 %collective-permute-start.8 = (bf16[256,512]{1,0:T(8,128)(2,1)}, bf16[256,512]{1,0:T(8,128)(2,1)}, u32[]{:S(2)}, u32[]{:S(2)}) collective-permute-start(bf16[256,512]{1,0:T(8,128)(2,1)} %get-tuple-element.219), channel_id=1, source_target_pairs={{0,2},{1,3},{2,0},{3,1},{4,6},{5,7},{6,4},{7,5},{8,10},{9,11},{10,... | collective-permute-start | bytes 786440 | tf_op jit(solution)/shard_map/ppermute | solution.py:693
  84.1 25.6 %collective-permute-start.9 = (bf16[256,512]{1,0:T(8,128)(2,1)}, bf16[256,512]{1,0:T(8,128)(2,1)}, u32[]{:S(2)}, u32[]{:S(2)}) collective-permute-start(bf16[256,512]{1,0:T(8,128)(2,1)} %get-tuple-element.220), channel_id=1, source_target_pairs={{0,4},{1,5},{2,6},{3,7},{4,0},{5,1},{6,2},{7,3},{8,12},{9,13},{10,... | collective-permute-start | bytes 786440 | tf_op jit(solution)/shard_map/ppermute | solution.py:693
  85.7 24.1 %collective-permute-start.10 = (bf16[256,512]{1,0:T(8,128)(2,1)}, bf16[256,512]{1,0:T(8,128)(2,1)}, u32[]{:S(2)}, u32[]{:S(2)}) collective-permute-start(bf16[256,512]{1,0:T(8,128)(2,1)} %get-tuple-element.221), channel_id=1, source_target_pairs={{0,6},{1,7},{2,4},{3,5},{4,2},{5,3},{6,0},{7,1},{8,14},{9,15},{10,... | collective-permute-start | bytes 786440 | tf_op jit(solution)/shard_map/ppermute | solution.py:693
  109.8 7.4 %collective-permute-start.11 = (bf16[2048,512]{1,0:T(8,128)(2,1)}, bf16[2048,512]{1,0:T(8,128)(2,1)}, u32[]{:S(2)}, u32[]{:S(2)}) collective-permute-start(bf16[2048,512]{1,0:T(8,128)(2,1)} %get-tuple-element.237), channel_id=1, source_target_pairs={{0,8},{1,9},{2,10},{3,11},{4,12},{5,13},{6,14},{7,15},{8,0},{9,1},... | collective-permute-start | bytes 6291464 | tf_op jit(solution)/shard_map/ppermute | solution.py:693
  109.9 8.9 %copy-start.6 = (s32[7]{0:T(128)S(1)}, s32[7]{0:T(128)}, u32[]{:S(2)}) copy-start(s32[7]{0:T(128)} %pad_add_fusion.refs_0_.info_ref) | copy-start | bytes 88
  117.2 35.4 %collective-permute-start.15 = (bf16[768,512]{1,0:T(8,128)(2,1)}, bf16[768,512]{1,0:T(8,128)(2,1)}, u32[]{:S(2)}, u32[]{:S(2)}) collective-permute-start(bf16[768,512]{1,0:T(8,128)(2,1)} %get-tuple-element.253), channel_id=1, source_target_pairs={{2,0},{3,1},{4,2},{5,3},{6,4},{7,5},{10,8},{11,9},{12,10},{13,11},... | collective-permute-start | bytes 2359304 | tf_op jit(solution)/shard_map/ppermute | solution.py:831
  118.8 1.6 copy-start
  123.4 0.8 copy-start.2
  124.2 28.3 %collective-permute-start.12 = (bf16[512,512]{1,0:T(8,128)(2,1)}, bf16[512,512]{1,0:T(8,128)(2,1)}, u32[]{:S(2)}, u32[]{:S(2)}) collective-permute-start(bf16[512,512]{1,0:T(8,128)(2,1)} %get-tuple-element.250), channel_id=1, source_target_pairs={{0,1},{1,0},{2,3},{3,2},{4,5},{5,4},{6,7},{7,6},{8,9},{9,8},{10,11... | collective-permute-start | bytes 1572872 | tf_op jit(solution)/shard_map/ppermute | solution.py:693
  124.7 27.8 %collective-permute-start.13 = (bf16[512,512]{1,0:T(8,128)(2,1)}, bf16[512,512]{1,0:T(8,128)(2,1)}, u32[]{:S(2)}, u32[]{:S(2)}) collective-permute-start(bf16[512,512]{1,0:T(8,128)(2,1)} %get-tuple-element.251), channel_id=1, source_target_pairs={{0,16},{1,17},{2,18},{3,19},{4,20},{5,21},{6,22},{7,23},{8,24},{9,... | collective-permute-start | bytes 1572872 | tf_op jit(solution)/shard_map/ppermute | solution.py:693
  126.3 26.3 %collective-permute-start.14 = (bf16[512,512]{1,0:T(8,128)(2,1)}, bf16[512,512]{1,0:T(8,128)(2,1)}, u32[]{:S(2)}, u32[]{:S(2)}) collective-permute-start(bf16[512,512]{1,0:T(8,128)(2,1)} %get-tuple-element.252), channel_id=1, source_target_pairs={{0,17},{1,16},{2,19},{3,18},{4,21},{5,20},{6,23},{7,22},{8,25},{9,... | collective-permute-start | bytes 1572872 | tf_op jit(solution)/shard_map/ppermute | solution.py:693
  152.6 24.3 %collective-permute-start.16 = (bf16[1040,512]{1,0:T(8,128)(2,1)}, bf16[1040,512]{1,0:T(8,128)(2,1)}, u32[]{:S(2)}, u32[]{:S(2)}) collective-permute-start(bf16[1040,512]{1,0:T(8,128)(2,1)} %get-tuple-element.275), channel_id=1, source_target_pairs={{0,8},{1,9},{2,10},{3,11},{4,12},{5,13},{6,14},{7,15},{8,0},{9,1},... | collective-permute-start | bytes 3194888 | tf_op jit(solution)/shard_map/ppermute | solution.py:693
  152.7 1.0 copy-start.3
  153.7 3.0 %copy-start.7 = (bf16[1024,512]{1,0:T(8,128)(2,1)S(1)}, bf16[1024,512]{1,0:T(8,128)(2,1)}, u32[]{:S(2)}) copy-start(bf16[1024,512]{1,0:T(8,128)(2,1)} %get-tuple-element.309) | copy-start | bytes 3145732
  156.1 0.7 copy-start.4
  159.6 46.4 %collective-permute-start.30 = (bf16[1024,512]{1,0:T(8,128)(2,1)}, bf16[1024,512]{1,0:T(8,128)(2,1)}, u32[]{:S(2)}, u32[]{:S(2)}) collective-permute-start(bf16[1024,512]{1,0:T(8,128)(2,1)} %get-tuple-element.311), channel_id=1, source_target_pairs={{0,1},{1,0},{2,3},{3,2},{4,5},{5,4},{6,7},{7,6},{8,9},{9,8},{10,11... | collective-permute-start | bytes 3145736 | tf_op jit(solution)/shard_map/ppermute | solution.py:693
  160.1 9.7 %collective-permute-start.17 = (bf16[128,512]{1,0:T(8,128)(2,1)}, bf16[128,512]{1,0:T(8,128)(2,1)}, u32[]{:S(2)}, u32[]{:S(2)}) collective-permute-start(bf16[128,512]{1,0:T(8,128)(2,1)} %get-tuple-element.279), channel_id=1, source_target_pairs={{0,2},{1,3},{2,0},{3,1},{4,6},{5,7},{6,4},{7,5},{8,10},{9,11},{10,... | collective-permute-start | bytes 393224 | tf_op jit(solution)/shard_map/ppermute | solution.py:693
  161.4 15.5 %collective-permute-start.18 = (bf16[128,512]{1,0:T(8,128)(2,1)}, bf16[128,512]{1,0:T(8,128)(2,1)}, u32[]{:S(2)}, u32[]{:S(2)}) collective-permute-start(bf16[128,512]{1,0:T(8,128)(2,1)} %get-tuple-element.280), channel_id=1, source_target_pairs={{0,4},{1,5},{2,6},{3,7},{4,0},{5,1},{6,2},{7,3},{8,12},{9,13},{10,... | collective-permute-start | bytes 393224 | tf_op jit(solution)/shard_map/ppermute | solution.py:693
  166.6 10.3 %collective-permute-start.19 = (bf16[128,512]{1,0:T(8,128)(2,1)}, bf16[128,512]{1,0:T(8,128)(2,1)}, u32[]{:S(2)}, u32[]{:S(2)}) collective-permute-start(bf16[128,512]{1,0:T(8,128)(2,1)} %get-tuple-element.281), channel_id=1, source_target_pairs={{0,6},{1,7},{2,4},{3,5},{4,2},{5,3},{6,0},{7,1},{8,14},{9,15},{10,... | collective-permute-start | bytes 393224 | tf_op jit(solution)/shard_map/ppermute | solution.py:693
  176.9 0.9 copy-start.5
  178.9 8.7 %collective-permute-start.20 = (bf16[128,512]{1,0:T(8,128)(2,1)S(1)}, bf16[128,512]{1,0:T(8,128)(2,1)S(1)}, u32[]{:S(2)}, u32[]{:S(2)}) collective-permute-start(bf16[128,512]{1,0:T(8,128)(2,1)S(1)} %split_sum.8), channel_id=1, source_target_pairs={{0,2},{1,3},{2,0},{3,1},{4,6},{5,7},{6,4},{7,5},{8,10},{9,11},{10,... | collective-permute-start | bytes 393224 | tf_op jit(solution)/shard_map/ppermute | solution.py:693
  181.4 1.2 copy-start.1
  184.1 9.4 %collective-permute-start.21 = (bf16[272,512]{1,0:T(8,128)(2,1)S(1)}, bf16[272,512]{1,0:T(8,128)(2,1)S(1)}, u32[]{:S(2)}, u32[]{:S(2)}) collective-permute-start(bf16[272,512]{1,0:T(8,128)(2,1)S(1)} %get-tuple-element.299), channel_id=1, source_target_pairs={{0,1},{1,0},{2,3},{3,2},{4,5},{5,4},{6,7},{7,6},{8,9},{9,8},{10,11... | collective-permute-start | bytes 835592 | tf_op jit(solution)/shard_map/ppermute | solution.py:693
  185.7 9.6 %collective-permute-start.22 = (bf16[272,512]{1,0:T(8,128)(2,1)S(1)}, bf16[272,512]{1,0:T(8,128)(2,1)S(1)}, u32[]{:S(2)}, u32[]{:S(2)}) collective-permute-start(bf16[272,512]{1,0:T(8,128)(2,1)S(1)} %get-tuple-element.300), channel_id=1, source_target_pairs={{0,16},{1,17},{2,18},{3,19},{4,20},{5,21},{6,22},{7,23},{8,24},{9,... | collective-permute-start | bytes 835592 | tf_op jit(solution)/shard_map/ppermute | solution.py:693
  186.8 12.0 %collective-permute-start.23 = (bf16[272,512]{1,0:T(8,128)(2,1)S(1)}, bf16[272,512]{1,0:T(8,128)(2,1)S(1)}, u32[]{:S(2)}, u32[]{:S(2)}) collective-permute-start(bf16[272,512]{1,0:T(8,128)(2,1)S(1)} %get-tuple-element.301), channel_id=1, source_target_pairs={{0,17},{1,16},{2,19},{3,18},{4,21},{5,20},{6,23},{7,22},{8,25},{9,... | collective-permute-start | bytes 835592 | tf_op jit(solution)/shard_map/ppermute | solution.py:693
  187.7 12.6 %collective-permute-start.24 = (bf16[256,512]{1,0:T(8,128)(2,1)S(1)}, bf16[256,512]{1,0:T(8,128)(2,1)S(1)}, u32[]{:S(2)}, u32[]{:S(2)}) collective-permute-start(bf16[256,512]{1,0:T(8,128)(2,1)S(1)} %pad_maximum_fusion.1), channel_id=1, source_target_pairs={{0,4},{1,5},{2,6},{3,7},{4,0},{5,1},{6,2},{7,3},{8,12},{9,13},{10,... | collective-permute-start | bytes 786440 | tf_op jit(solution)/shard_map/ppermute | solution.py:693
  193.5 13.9 %collective-permute-start.28 = (bf16[256,512]{1,0:T(8,128)(2,1)S(1)}, bf16[256,512]{1,0:T(8,128)(2,1)S(1)}, u32[]{:S(2)}, u32[]{:S(2)}) collective-permute-start(bf16[256,512]{1,0:T(8,128)(2,1)S(1)} %pad_maximum_fusion.1), channel_id=1, source_target_pairs={{0,1},{1,0},{2,3},{3,2},{4,5},{5,4},{6,7},{7,6},{8,9},{9,8},{10,11... | collective-permute-start | bytes 786440 | tf_op jit(solution)/shard_map/ppermute | solution.py:693
  200.2 12.1 %collective-permute-start.29 = (bf16[256,512]{1,0:T(8,128)(2,1)S(1)}, bf16[256,512]{1,0:T(8,128)(2,1)S(1)}, u32[]{:S(2)}, u32[]{:S(2)}) collective-permute-start(bf16[256,512]{1,0:T(8,128)(2,1)S(1)} %collective-permute-done.24), channel_id=1, source_target_pairs={{0,16},{1,17},{2,18},{3,19},{4,20},{5,21},{6,22},{7,23},{8,24},{9,... | collective-permute-start | bytes 786440 | tf_op jit(solution)/shard_map/ppermute | solution.py:693
  202.2 5.2 %collective-permute-start.25 = (bf16[80,512]{1,0:T(8,128)(2,1)S(1)}, bf16[80,512]{1,0:T(8,128)(2,1)S(1)}, u32[]{:S(2)}, u32[]{:S(2)}) collective-permute-start(bf16[80,512]{1,0:T(8,128)(2,1)S(1)} %get-tuple-element.305), channel_id=1, source_target_pairs={{0,2},{1,3},{2,0},{3,1},{4,6},{5,7},{6,4},{7,5},{8,10},{9,11},{10,... | collective-permute-start | bytes 245768 | tf_op jit(solution)/shard_map/ppermute | solution.py:693
  202.3 8.8 %collective-permute-start.26 = (bf16[80,512]{1,0:T(8,128)(2,1)S(1)}, bf16[80,512]{1,0:T(8,128)(2,1)S(1)}, u32[]{:S(2)}, u32[]{:S(2)}) collective-permute-start(bf16[80,512]{1,0:T(8,128)(2,1)S(1)} %get-tuple-element.306), channel_id=1, source_target_pairs={{0,4},{1,5},{2,6},{3,7},{4,0},{5,1},{6,2},{7,3},{8,12},{9,13},{10,... | collective-permute-start | bytes 245768 | tf_op jit(solution)/shard_map/ppermute | solution.py:693
  206.0 6.3 %collective-permute-start.27 = (bf16[80,512]{1,0:T(8,128)(2,1)S(1)}, bf16[80,512]{1,0:T(8,128)(2,1)S(1)}, u32[]{:S(2)}, u32[]{:S(2)}) collective-permute-start(bf16[80,512]{1,0:T(8,128)(2,1)S(1)} %get-tuple-element.307), channel_id=1, source_target_pairs={{0,6},{1,7},{2,4},{3,5},{4,2},{5,3},{6,0},{7,1},{8,14},{9,15},{10,... | collective-permute-start | bytes 245768 | tf_op jit(solution)/shard_map/ppermute | solution.py:693
  213.1 19.3 %collective-permute-start.36 = (bf16[512,512]{1,0:T(8,128)(2,1)}, bf16[512,512]{1,0:T(8,128)(2,1)}, u32[]{:S(2)}, u32[]{:S(2)}) collective-permute-start(bf16[512,512]{1,0:T(8,128)(2,1)} %constant_dynamic-update-slice_fusion.refs_2_), channel_id=1, source_target_pairs={{0,8},{1,9},{2,10},{3,11},{4,12},{5,13},{6,14},{7,15},{8,0},{9,1},... | collective-permute-start | bytes 1572872 | tf_op jit(solution)/shard_map/ppermute | solution.py:693
  213.1 19.3 %collective-permute-start.32 = (bf16[512,512]{1,0:T(8,128)(2,1)}, bf16[512,512]{1,0:T(8,128)(2,1)}, u32[]{:S(2)}, u32[]{:S(2)}) collective-permute-start(bf16[512,512]{1,0:T(8,128)(2,1)} %constant_dynamic-update-slice_fusion.refs_2_), channel_id=1, source_target_pairs={{0,1},{1,0},{2,3},{3,2},{4,5},{5,4},{6,7},{7,6},{8,9},{9,8},{10,11... | collective-permute-start | bytes 1572872 | tf_op jit(solution)/shard_map/ppermute | solution.py:693
  215.4 17.0 %collective-permute-start.35 = (bf16[512,512]{1,0:T(8,128)(2,1)}, bf16[512,512]{1,0:T(8,128)(2,1)}, u32[]{:S(2)}, u32[]{:S(2)}) collective-permute-start(bf16[512,512]{1,0:T(8,128)(2,1)} %pad_maximum_fusion.refs_0_), channel_id=1, source_target_pairs={{0,8},{1,9},{2,10},{3,11},{4,12},{5,13},{6,14},{7,15},{8,0},{9,1},... | collective-permute-start | bytes 1572872 | tf_op jit(solution)/shard_map/ppermute | solution.py:693
  215.7 16.7 %collective-permute-start.31 = (bf16[512,512]{1,0:T(8,128)(2,1)}, bf16[512,512]{1,0:T(8,128)(2,1)}, u32[]{:S(2)}, u32[]{:S(2)}) collective-permute-start(bf16[512,512]{1,0:T(8,128)(2,1)} %pad_maximum_fusion.refs_0_), channel_id=1, source_target_pairs={{0,16},{1,17},{2,18},{3,19},{4,20},{5,21},{6,22},{7,23},{8,24},{9,... | collective-permute-start | bytes 1572872 | tf_op jit(solution)/shard_map/ppermute | solution.py:693
  217.2 4.3 %collective-permute-start.33 = (bf16[64,512]{1,0:T(8,128)(2,1)S(1)}, bf16[64,512]{1,0:T(8,128)(2,1)S(1)}, u32[]{:S(2)}, u32[]{:S(2)}) collective-permute-start(bf16[64,512]{1,0:T(8,128)(2,1)S(1)} %get-tuple-element.318), channel_id=1, source_target_pairs={{0,2},{1,3},{2,0},{3,1},{4,6},{5,7},{6,4},{7,5},{8,10},{9,11},{10,... | collective-permute-start | bytes 196616 | tf_op jit(solution)/shard_map/ppermute | solution.py:693
  221.5 0.6 copy-start.8
  222.8 8.7 %collective-permute-start.34 = (bf16[128,512]{1,0:T(8,128)(2,1)}, bf16[128,512]{1,0:T(8,128)(2,1)}, u32[]{:S(2)}, u32[]{:S(2)}) collective-permute-start(bf16[128,512]{1,0:T(8,128)(2,1)} %constant_dynamic-update-slice_fusion.2), channel_id=1, source_target_pairs={{0,4},{1,5},{2,6},{3,7},{4,0},{5,1},{6,2},{7,3},{8,12},{9,13},{10,... | collective-permute-start | bytes 393224 | tf_op jit(solution)/shard_map/ppermute | solution.py:693
  232.4 30.3 %all-to-all-start = ((bf16[4,256,512]{2,1,0:T(8,128)(2,1)}), bf16[4,256,512]{2,1,0:T(8,128)(2,1)}, u32[]{:S(2)}, u32[]{:S(2)}) async-start(bf16[4,256,512]{2,1,0:T(8,128)(2,1)} %bitcast.35), calls=%async_computation | async-start | bytes 2097152 | tf_op jit(solution)/shard_map/all_to_all | solution.py:881
  236.8 4.1 %collective-permute-start.40 = (bf16[512,512]{1,0:T(8,128)(2,1)}, bf16[512,512]{1,0:T(8,128)(2,1)S(1)}, u32[]{:S(2)}, u32[]{:S(2)}) collective-permute-start(bf16[512,512]{1,0:T(8,128)(2,1)} %collective-permute-done.31.refs_1_), channel_id=1, source_target_pairs={{0,8},{1,9},{2,10},{3,11},{4,12},{5,13},{6,14},{7,15},{8,0},{9,1},... | collective-permute-start | bytes 1572872 | tf_op jit(solution)/shard_map/ppermute | solution.py:693
  236.9 4.0 %collective-permute-start.41 = (bf16[512,512]{1,0:T(8,128)(2,1)}, bf16[512,512]{1,0:T(8,128)(2,1)S(1)}, u32[]{:S(2)}, u32[]{:S(2)}) collective-permute-start(bf16[512,512]{1,0:T(8,128)(2,1)} %collective-permute-done.32.refs_3_), channel_id=1, source_target_pairs={{0,8},{1,9},{2,10},{3,11},{4,12},{5,13},{6,14},{7,15},{8,0},{9,1},... | collective-permute-start | bytes 1572872 | tf_op jit(solution)/shard_map/ppermute | solution.py:693
  237.4 10.2 %collective-permute-start.39 = (bf16[256,512]{1,0:T(8,128)(2,1)S(1)}, bf16[256,512]{1,0:T(8,128)(2,1)S(1)}, u32[]{:S(2)}, u32[]{:S(2)}) collective-permute-start(bf16[256,512]{1,0:T(8,128)(2,1)S(1)} %pad_maximum_fusion.2.refs_0_), channel_id=1, source_target_pairs={{0,17},{1,16},{2,19},{3,18},{4,21},{5,20},{6,23},{7,22},{8,25},{9,... | collective-permute-start | bytes 786440 | tf_op jit(solution)/shard_map/ppermute | solution.py:693
  238.5 12.9 %collective-permute-start.38 = (bf16[256,512]{1,0:T(8,128)(2,1)S(1)}, bf16[256,512]{1,0:T(8,128)(2,1)S(1)}, u32[]{:S(2)}, u32[]{:S(2)}) collective-permute-start(bf16[256,512]{1,0:T(8,128)(2,1)S(1)} %pad_maximum_fusion.2.refs_0_), channel_id=1, source_target_pairs={{0,16},{1,17},{2,18},{3,19},{4,20},{5,21},{6,22},{7,23},{8,24},{9,... | collective-permute-start | bytes 786440 | tf_op jit(solution)/shard_map/ppermute | solution.py:693
  239.4 12.8 %collective-permute-start.37 = (bf16[256,512]{1,0:T(8,128)(2,1)S(1)}, bf16[256,512]{1,0:T(8,128)(2,1)S(1)}, u32[]{:S(2)}, u32[]{:S(2)}) collective-permute-start(bf16[256,512]{1,0:T(8,128)(2,1)S(1)} %pad_maximum_fusion.2.refs_0_), channel_id=1, source_target_pairs={{0,1},{1,0},{2,3},{3,2},{4,5},{5,4},{6,7},{7,6},{8,9},{9,8},{10,11... | collective-permute-start | bytes 786440 | tf_op jit(solution)/shard_map/ppermute | solution.py:693
  240.9 12.4 %collective-permute-start.42 = (bf16[256,512]{1,0:T(8,128)(2,1)S(1)}, bf16[256,512]{1,0:T(8,128)(2,1)S(1)}, u32[]{:S(2)}, u32[]{:S(2)}) collective-permute-start(bf16[256,512]{1,0:T(8,128)(2,1)S(1)} %pad_maximum_fusion.2.refs_0_), channel_id=1, source_target_pairs={{0,8},{1,9},{2,10},{3,11},{4,12},{5,13},{6,14},{7,15},{8,0},{9,1},... | collective-permute-start | bytes 786440 | tf_op jit(solution)/shard_map/ppermute | solution.py:693
  252.2 1.5 collective-permute-start.43
  252.2 1.9 collective-permute-start.44
  252.7 1.8 collective-permute-start.45

commit v3 on v2

--- a/solution.py
+++ b/solution.py
@@ -88,6 +88,13 @@
             self.loads[j][2].wait()
         self.start_more(-1)
 
+    def need_block(self, ref, number):
+        j = [i for i, load in enumerate(self.loads) if load[1] is ref][number]
+        self.start_more(j)
+        if j in self.waiting:
+            self.waiting.discard(j)
+            self.loads[j][2].wait()
+
     def emit(self, ref, *where):
         for j, (out, held) in enumerate(self.stores):
             if held is ref:
@@ -106,7 +113,7 @@
             copy.wait()
 
 
-def hbm_call(kernel, name, outs, args, limit, scratch=(), smem=0, fixed_in=(), fixed_out=(), stores=None):
+def hbm_call(kernel, name, outs, args, limit, scratch=(), smem=0, fixed_in=(), fixed_out=(), stores=None, blocks=()):
     arrays = args[smem:]
     moves_in = [j for j in range(len(arrays)) if j not in fixed_in]
     moves_out = [j for j in range(len(outs)) if j not in fixed_out]
@@ -116,6 +123,7 @@
     resident = [(arrays[j].shape, arrays[j].dtype) for j in fixed_in] + [outs[j] for j in fixed_out]
     rest = sum(math.prod(shape) * jnp.dtype(dtype).itemsize for shape, dtype in resident)
     limit = max((limit << 20) + size, ROOM - rest)
+    more = sum(len(cuts(arrays[j].shape[0], 256)) - 1 for j in blocks)
 
     def body(*refs):
         scalars, refs = refs[:smem], refs[smem:]
@@ -124,7 +132,12 @@
         *kept, load_sems, store_sems = refs
         loads, kept_out = [], []
         for n, j in enumerate(moves_in):
-            loads.append((ins[j], kept[n], pltpu.make_async_copy(ins[j], kept[n], load_sems.at[n])))
+            for first, rows in cuts(arrays[j].shape[0], 256 if j in blocks else arrays[j].shape[0]):
+                source, target = ins[j], kept[n]
+                if j in blocks:
+                    source, target = source.at[pl.ds(first, rows)], target.at[pl.ds(first, rows)]
+                copy = pltpu.make_async_copy(source, target, load_sems.at[len(loads)])
+                loads.append((ins[j], kept[n], copy))
             ins[j] = kept[n]
         kept = kept[len(moves_in) :]
         for n, j in enumerate(moves_out):
@@ -143,7 +156,7 @@
         out_specs=place(len(outs), fixed_out),
         out_shape=[jax.ShapeDtypeStruct(shape, dtype) for shape, dtype in outs],
         scratch_shapes=[pltpu.VMEM(shape, dtype) for shape, dtype in held]
-        + [pltpu.SemaphoreType.DMA((max(len(moves_in), 1),)), pltpu.SemaphoreType.DMA((max(stores or len(moves_out), 1),))],
+        + [pltpu.SemaphoreType.DMA((max(len(moves_in) + more, 1),)), pltpu.SemaphoreType.DMA((max(stores or len(moves_out), 1),))],
         compiler_params=pltpu.CompilerParams(vmem_limit_bytes=min(limit, ROOM)),
         cost_estimate=pl.CostEstimate(flops=0, bytes_accessed=0, transcendentals=0),
         name=name,
@@ -355,10 +368,10 @@
     parts, flow, info_ref, *refs,
 ):
     cot_refs, refs = refs[:parts], refs[parts:]
-    wd_ref, slope_ref, wu_ref, state_ref, mixed_ref, factor_ref, gm_ref, wo_ref, inner_ref, mlp_ref, *refs = refs
+    wd_ref, wu_ref, slope_ref, state_ref, mixed_ref, factor_ref, gm_ref, wo_ref, inner_ref, mlp_ref, *refs = refs
     dstate_ref, late_ref, early_ref, dlate_ref, dearly_ref, keep_ref, send_ref, dwo_ref, dgain_ref = refs[:9]
     dpre_ref, dproj_ref, cot_ref = refs[9:]
-    flow.need(*cot_refs, wd_ref, slope_ref)
+    flow.need(*cot_refs, wd_ref)
     join(cot_refs, cot_ref)
     hidden, width = wd_ref.shape
 
@@ -377,6 +390,7 @@
     for start, size in cuts(cot_ref.shape[0], 256):
         rows = pl.ds(start, size)
         cot = cot_ref[rows, :]
+        flow.need_block(slope_ref, start // 256)
         d_mlp = None
         for first, step in cuts(hidden, 512):
             some = pl.ds(first, step)
@@ -421,10 +435,11 @@
         functools.partial(mlp_back_kernel, len(cots)),
         "mlp_back",
         outs,
-        (info, *cots, wd, slope, wu, state, mixed, factor, gm, wo, inner, mlp),
+        (info, *cots, wd, wu, slope, state, mixed, factor, gm, wo, inner, mlp),
         20,
         [((rows, hidden), BF16), (tall, BF16), (tall, BF16)],
         smem=1,
+        blocks=(len(cots) + 2,),
     )
 
 

time: 270 us -> 270 us (level)
  transfers between devices with their start and end apart: 47 -> 47, of which waited for: 18 -> 17; matrix products, arithmetic and copies ran while one was open for 6% -> 6% of each run, Pallas kernels for 45% -> 45%
where the time goes in v3:
time: 270 us; the launch traced here: 266 us
  Pallas kernels  124 us (46%)
  starting transfers between devices  65.7 us (24%)
  waiting for transfers between devices  48.9 us (18%)
  local copies, waits for them, and re-layouts  13.3 us (5%)
  other arithmetic  11.4 us (4%)
    pallas_call x11, Pallas kernels, hbm_call(): pl.pallas_call(body, in_specs=[pl.BlockSpec(memory_space=pltpu.SMEM)] * s...  106 us
    ppermute x44, starting transfers between devices, flip(): return lax.ppermute(value, ('seq', 'blk'), pairs)  52.3 us
    ppermute x44, waiting for transfers between devices, flip(): return lax.ppermute(value, ('seq', 'blk'), pairs)  43.8 us
    pallas_call x8, Pallas kernels, vmem_call(): pl.pallas_call(kernel, in_specs=[in_smem] * smem + [in_vmem] * (len(args)...  18.7 us
    unnamed x20, local copies, waits for them, and re-layouts  8.21 us
    ppermute x1, starting transfers between devices, local(): tail = lax.ppermute(sent, 'blk', pairs)  7.52 us
  transfers between devices with their start and end apart: 47, of which 17 were waited for; matrix products, arithmetic and copies ran while one was open for 6% of the time, Pallas kernels for 45%

profile of v3, /device:TPU:0, one launch (start us, length us, event | category | flops | bytes accessed | tf_op | source)
XLA Modules:
  0.0 266.2 jit_solution(12138035372897536619)
XLA Ops:
  0.6 3.0 %collective-permute-start.3 = (bf16[1024,512]{1,0:T(8,128)(2,1)}, bf16[1024,512]{1,0:T(8,128)(2,1)}, u32[]{:S(2)}, u32[]{:S(2)}) collective-permute-start(bf16[1024,512]{1,0:T(8,128)(2,1)} %bitcast.25), channel_id=1, source_target_pairs={{0,1},{1,0},{2,3},{3,2},{4,5},{5,4},{6,7},{7,6},{8,9},{9,8},{10,11... | collective-permute-start | bytes 3145736 | tf_op jit(solution)/shard_map/ppermute | solution.py:708
  3.7 2.8 %sort_rows.2 = (bf16[256,512]{1,0:T(8,128)(2,1)}, bf16[256,512]{1,0:T(8,128)(2,1)}, bf16[256,512]{1,0:T(8,128)(2,1)}, bf16[256,512]{1,0:T(8,128)(2,1)}) custom-call(s32[1]{0:T(128)} %bitcast.2.refs_0_, bf16[1024,512]{1,0:T(8,128)(2,1)} %bitcast.33), custom_call_target="tpu_custom_call" | custom-call | tf_op jit(solution)/shard_map/sort_rows/pallas_call | solution.py:153
  6.5 1.6 collective-permute-start
  8.1 2.6 collective-permute-start.1
  10.9 1.3 fusion.2
  12.2 2.8 %sort_rows.3 = (bf16[256,512]{1,0:T(8,128)(2,1)}, bf16[256,512]{1,0:T(8,128)(2,1)}, bf16[256,512]{1,0:T(8,128)(2,1)}, bf16[256,512]{1,0:T(8,128)(2,1)}) custom-call(s32[1]{0:T(128)} %bitcast.2.refs_0_, bf16[1024,512]{1,0:T(8,128)(2,1)} %bitcast.34), custom_call_target="tpu_custom_call" | custom-call | tf_op jit(solution)/shard_map/sort_rows/pallas_call | solution.py:153
  16.4 1.3 stack.65.refs_0_
  17.6 1.9 stack.66.refs_0_
  19.5 4.2 %keys_values.1 = (bf16[1024,512]{1,0:T(8,128)(2,1)}, bf16[1024,512]{1,0:T(8,128)(2,1)}) custom-call(bf16[1024,512]{1,0:T(8,128)(2,1)} %bitcast.26, f32[1,512]{1,0:T(1,128)} %bitcast.36, bf16[512,512]{1,0:T(8,128)(2,1)} %refs_2_.7, bf16[512,512]{1,0:T(8,128)(2,1)} %refs_3_.7), custom_call_target="tpu_custom_call" | custom-call | tf_op jit(solution)/shard_map/keys_values/pallas_call | solution.py:153
  23.8 1.3 pad_add_fusion.1.refs_0_
  25.0 1.3 pad_add_fusion.2.refs_0_
  26.3 3.5 %collective-permute-done.1.refs_9_ = bf16[256,512]{1,0:T(8,128)(2,1)} collective-permute-done((bf16[256,512]{1,0:T(8,128)(2,1)}, bf16[256,512]{1,0:T(8,128)(2,1)}, u32[]{:S(2)}, u32[]{:S(2)}) %collective-permute-start.1) | collective-permute-done | bytes 262176 | tf_op jit(solution)/shard_map/ppermute | solution.py:708
  29.8 2.3 slice_select_fusion
  32.2 7.5 %collective-permute-start.4 = (bf16[768,512]{1,0:T(8,128)(2,1)}, bf16[768,512]{1,0:T(8,128)(2,1)}, u32[]{:S(2)}, u32[]{:S(2)}) collective-permute-start(bf16[768,512]{1,0:T(8,128)(2,1)} %slice_select_fusion), channel_id=1, source_target_pairs={{0,2},{1,3},{2,4},{3,5},{4,6},{5,7},{8,10},{9,11},{10,12},{11,13},... | collective-permute-start | bytes 2359304 | tf_op jit(solution)/shard_map/ppermute | solution.py:806
  40.5 12.3 %attend.1 = (bf16[1024,512]{1,0:T(8,128)(2,1)}, f32[1024,512]{1,0:T(8,128)}, f32[8,1024]{1,0:T(8,128)}, f32[8,1024]{1,0:T(8,128)}, bf16[1024,512]{1,0:T(8,128)(2...) custom-call(s32[4]{0:T(128)} %pad_add_fusion.1.refs_0_, ...), custom_call_target="tpu_custom_call" | custom-call | tf_op jit(solution)/shard_map/attend/pallas_call | solution.py:153
  52.8 7.5 %collective-permute-done.5.refs_2_ = bf16[256,512]{1,0:T(8,128)(2,1)} collective-permute-done((bf16[256,512]{1,0:T(8,128)(2,1)}, bf16[256,512]{1,0:T(8,128)(2,1)}, u32[]{:S(2)}, u32[]{:S(2)}) %collective-permute-start.5) | collective-permute-done | bytes 262176 | tf_op jit(solution)/shard_map/ppermute | solution.py:708
  61.1 4.0 %collective-permute-start.7 = (bf16[256,512]{1,0:T(8,128)(2,1)}, bf16[256,512]{1,0:T(8,128)(2,1)}, u32[]{:S(2)}, u32[]{:S(2)}) collective-permute-start(bf16[256,512]{1,0:T(8,128)(2,1)} %get-tuple-element.205), channel_id=1, source_target_pairs={{0,6},{1,7},{2,4},{3,5},{4,2},{5,3},{6,0},{7,1},{8,14},{9,15},{10,... | collective-permute-start | bytes 786440 | tf_op jit(solution)/shard_map/ppermute | solution.py:708
  65.1 18.4 %finish.1 = (bf16[768,512]{1,0:T(8,128)(2,1)}, bf16[768,512]{1,0:T(8,128)(2,1)}, bf16[768,1024]{1,0:T(8,128)(2,1)}, f32[1024,128]{1,0:T(8,128)}, bf16[1024,512]{...) custom-call(s32[3]{0:T(128)} %pad_add_fusion.2.refs_0_, ...), custom_call_target="tpu_custom_call" | custom-call | tf_op jit(solution)/shard_map/finish/pallas_call | solution.py:153
  84.1 1.5 collective-permute-start.9
  85.7 2.4 collective-permute-start.10
  88.6 21.8 %mlp_back.1 = (f32[1024,512]{1,0:T(8,128)}, bf16[1024,512]{1,0:T(8,128)(2,1)}, bf16[1024,512]{1,0:T(8,128)(2,1)}, f32[8,1024]{1,0:T(8,128)}, f32[8,1024]{1,0:T(8...) custom-call(s32[7]{0:T(128)} %pad_add_fusion.refs_0_.info_ref, ...), custom_call_target="tpu_custom_call" | custom-call | tf_op jit(solution)/shard_map/mlp_back/pallas_call | solution.py:153
  110.6 7.3 %attention_back.2 = (bf16[768,512]{1,0:T(8,128)(2,1)}, f32[1024,512]{1,0:T(8,128)}, f32[512,512]{1,0:T(8,128)}, f32[512,512]{1,0:T(8,128)}, f32[8,512]{1,0:T(8,128)}) custom-call(s32[5]{0:T(128)} %stack.65.refs_0_, bf16[1024,512]{1,0:T(8,128)(2,1)} %get-tuple-element.209.refs_6_.refs_1_, bf16[512,512]{1,0:T(8,128)(2,1)} %refs_2_.7, ...), custom_call_target="tpu_custom_call" | custom-call | tf_op jit(solution)/shard_map/attention_back/pallas_call | solution.py:153
  117.9 1.5 collective-permute-start.15
  119.5 1.6 copy-done
  121.0 3.1 %split_sum.6 = (bf16[512,512]{1,0:T(8,128)(2,1)S(1)}, bf16[512,512]{1,0:T(8,128)(2,1)}, bf16[512,512]{1,0:T(8,128)(2,1)}, bf16[512,512]{1,0:T(8,128)(2,1)}) custom-call(s32[7]{0:T(128)S(1)} %copy-done.6, bf16[2048,512]{1,0:T(8,128)(2,1)S(1)} %copy-done, bf16[2048,512]{1,0:T(8,128)(2,1)} %collective-permute-done.11.refs_1_), custom_call_target="tpu_custom_call" | custom-call | tf_op jit(solution)/shard_map/split_sum/pallas_call | solution.py:46
  125.4 1.5 collective-permute-start.13
  126.9 1.5 collective-permute-start.14
  128.4 24.8 %attention_back.3 = (bf16[1024,512]{1,0:T(8,128)(2,1)}, bf16[1024,512]{1,0:T(8,128)(2,1)}, bf16[1024,512]{1,0:T(8,128)(2,1)}, bf16[1040,512]{1,0:T(8,128)(2,1)}, bf16[1040,512]{1,0:T(8,128)(2,1)}) custom-call(s32[8]{0:T(128)} %stack.66.refs_0_, bf16[1024,512]{1,0:T(8,128)(2,1)} %get-tuple-element.209.refs_6_.refs_1_, bf16[512,512]{1,0:T(8,128)(2,1)} %refs_2_.7, ...), custom_call_target="tpu_custom_call" | custom-call | tf_op jit(solution)/shard_map/attention_back/pallas_call | solution.py:153
  153.4 1.0 copy-done.3
  154.4 2.3 split_sum.7
  157.4 2.8 %pad_select_fusion = (bf16[1024,512]{1,0:T(8,128)(2,1)}, bf16[1024,512]{1,0:T(8,128)(2,1)}) fusion(bf16[768,512]{1,0:T(8,128)(2,1)} %collective-permute-done.15, pred[]{:T(512)S(6)} %eq.16, bf16[1024,512]{1,0:T(8,128)(2,1)S(1)} %copy-done.7, pred[]{:T(512)S(6)} %eq.18), kind=kLoop, calls=%fused_computation | loop fusion | flops 3145728 | bytes 3932162 | tf_op jit(solution)/shard_map/jit(_where)/select_n | solution.py:859
  160.8 2.0 collective-permute-start.17
  162.8 3.8 %collective-permute-start.18 = (bf16[128,512]{1,0:T(8,128)(2,1)}, bf16[128,512]{1,0:T(8,128)(2,1)}, u32[]{:S(2)}, u32[]{:S(2)}) collective-permute-start(bf16[128,512]{1,0:T(8,128)(2,1)} %get-tuple-element.280), channel_id=1, source_target_pairs={{0,4},{1,5},{2,6},{3,7},{4,0},{5,1},{6,2},{7,3},{8,12},{9,13},{10,... | collective-permute-start | bytes 393224 | tf_op jit(solution)/shard_map/ppermute | solution.py:708
  166.6 3.2 %unsort_rows.2 = bf16[1024,512]{1,0:T(8,128)(2,1)} custom-call(s32[1]{0:T(128)} %bitcast.2.refs_0_, bf16[256,512]{1,0:T(8,128)(2,1)} %get-tuple-element.287.refs_1_, bf16[256,512]{1,0:T(8,128)(2,1)} %collective-permute-done.8.refs_2_, bf16[256,512]{1,0:T(8,128)(2,1)} %collective-permute-done.9.refs_3_, bf16[256,512]{1,0:T(8,128)(2,1)} %collective-permute-done.10.refs_4_), custom_call_target="tpu_custom_call" | custom-call | tf_op jit(solution)/shard_map/unsort_rows/pallas_call | solution.py:153
  169.8 7.0 %collective-permute-done.18.refs_2_ = bf16[128,512]{1,0:T(8,128)(2,1)} collective-permute-done((bf16[128,512]{1,0:T(8,128)(2,1)}, bf16[128,512]{1,0:T(8,128)(2,1)}, u32[]{:S(2)}, u32[]{:S(2)}) %collective-permute-start.18) | collective-permute-done | bytes 131104 | tf_op jit(solution)/shard_map/ppermute | solution.py:708
  177.8 1.1 split_sum.8
  178.9 2.7 %collective-permute-start.20 = (bf16[128,512]{1,0:T(8,128)(2,1)S(1)}, bf16[128,512]{1,0:T(8,128)(2,1)S(1)}, u32[]{:S(2)}, u32[]{:S(2)}) collective-permute-start(bf16[128,512]{1,0:T(8,128)(2,1)S(1)} %split_sum.8), channel_id=1, source_target_pairs={{0,2},{1,3},{2,0},{3,1},{4,6},{5,7},{6,4},{7,5},{8,10},{9,11},{10,... | collective-permute-start | bytes 393224 | tf_op jit(solution)/shard_map/ppermute | solution.py:708
  181.6 1.2 copy-done.1
  182.8 1.5 split_sum.9
  184.3 1.6 collective-permute-start.21
  185.9 1.7 collective-permute-start.22
  187.9 1.0 collective-permute-start.24
  188.9 4.2 %collective-permute-done.21.refs_1_ = bf16[272,512]{1,0:T(8,128)(2,1)S(1)} collective-permute-done((bf16[272,512]{1,0:T(8,128)(2,1)S(1)}, bf16[272,512]{1,0:T(8,128)(2,1)S(1)}, u32[]{:S(2)}, u32[]{:S(2)}) %collective-permute-start.21) | collective-permute-done | bytes 278560 | tf_op jit(solution)/shard_map/ppermute | solution.py:708
  193.1 1.5 collective-permute-start.28
  195.5 3.8 %collective-permute-done.23.refs_3_ = bf16[272,512]{1,0:T(8,128)(2,1)S(1)} collective-permute-done((bf16[272,512]{1,0:T(8,128)(2,1)S(1)}, bf16[272,512]{1,0:T(8,128)(2,1)S(1)}, u32[]{:S(2)}, u32[]{:S(2)}) %collective-permute-start.23) | collective-permute-done | bytes 278560 | tf_op jit(solution)/shard_map/ppermute | solution.py:708
  199.3 1.5 collective-permute-done.24
  200.8 1.7 collective-permute-start.29
  203.3 3.6 %collective-permute-start.26 = (bf16[80,512]{1,0:T(8,128)(2,1)S(1)}, bf16[80,512]{1,0:T(8,128)(2,1)S(1)}, u32[]{:S(2)}, u32[]{:S(2)}) collective-permute-start(bf16[80,512]{1,0:T(8,128)(2,1)S(1)} %get-tuple-element.306), channel_id=1, source_target_pairs={{0,4},{1,5},{2,6},{3,7},{4,0},{5,1},{6,2},{7,3},{8,12},{9,13},{10,... | collective-permute-start | bytes 245768 | tf_op jit(solution)/shard_map/ppermute | solution.py:708
  208.4 3.7 %collective-permute-done.26.refs_2_ = bf16[80,512]{1,0:T(8,128)(2,1)S(1)} collective-permute-done((bf16[80,512]{1,0:T(8,128)(2,1)S(1)}, bf16[80,512]{1,0:T(8,128)(2,1)S(1)}, u32[]{:S(2)}, u32[]{:S(2)}) %collective-permute-start.26) | collective-permute-done | bytes 81952 | tf_op jit(solution)/shard_map/ppermute | solution.py:708
  212.1 1.2 collective-permute-done.27.refs_3_
  214.0 1.5 collective-permute-start.32
  217.4 1.2 collective-permute-start.33
  219.3 2.5 collective-permute-done.33
  223.0 2.0 collective-permute-start.34
  225.0 4.5 %token_back.1 = f32[1024,512]{1,0:T(8,128)} custom-call(bf16[1024,512]{1,0:T(8,128)(2,1)} %bitcast.29, f32[1,512]{1,0:T(1,128)} %bitcast.41, bf16[1024,512]{1,0:T(8,128)(2,1)} %get-tuple-element.319.refs_2_, bf16[1024,512]{1,0:T(8,128)(2,1)} %get-tuple-element.342.refs_3_, bf16[1024,512]{1,0:T(8,128)(2,1)} %collective-permute-done.30.refs_4_), custom_call_target="tpu_custom_call" | custom-call | tf_op jit(solution)/shard_map/token_back/pallas_call | solution.py:153
  229.5 2.2 collective-permute-done.34
  232.7 4.4 %all-to-all-start = ((bf16[4,256,512]{2,1,0:T(8,128)(2,1)}), bf16[4,256,512]{2,1,0:T(8,128)(2,1)}, u32[]{:S(2)}, u32[]{:S(2)}) async-start(bf16[4,256,512]{2,1,0:T(8,128)(2,1)} %bitcast.35), calls=%async_computation | async-start | bytes 2097152 | tf_op jit(solution)/shard_map/all_to_all | solution.py:896
  237.7 1.7 collective-permute-start.39
  239.6 1.5 collective-permute-start.37
  241.2 6.6 %unpack.2 = (f32[2048,512]{1,0:T(8,128)}, f32[512,2048]{1,0:T(8,128)}) custom-call(s32[7]{0:T(128)S(1)} %copy-done.6, bf16[512,512]{1,0:T(8,128)(2,1)} %pad_maximum_fusion.refs_0_, bf16[512,512]{1,0:T(8,128)(2,1)} %collective-permute-done.31.refs_1_, bf16[512,512]{1,0:T(8,128)(2,1)} %constant_dynamic-update-slice_fusion.refs_2_, ...), custom_call_target="tpu_custom_call" | custom-call | tf_op jit(solution)/shard_map/unpack/pallas_call | solution.py:46
  247.8 3.8 %collective-permute-done.38.refs_2_ = bf16[256,512]{1,0:T(8,128)(2,1)S(1)} collective-permute-done((bf16[256,512]{1,0:T(8,128)(2,1)S(1)}, bf16[256,512]{1,0:T(8,128)(2,1)S(1)}, u32[]{:S(2)}, u32[]{:S(2)}) %collective-permute-start.38) | collective-permute-done | bytes 262176 | tf_op jit(solution)/shard_map/ppermute | solution.py:708
  254.8 2.8 %unpack.3 = (f32[512,512]{1,0:T(8,128)}, f32[512,512]{1,0:T(8,128)}, f32[512,512]{1,0:T(8,128)}, f32[512,512]{1,0:T(8,128)}) custom-call(s32[7]{0:T(128)S(1)} %copy-done.6, bf16[256,512]{1,0:T(8,128)(2,1)S(1)} %pad_maximum_fusion.2.refs_0_, bf16[256,512]{1,0:T(8,128)(2,1)S(1)} %collective-permute-done.37.refs_1_, ...), custom_call_target="tpu_custom_call" | custom-call | tf_op jit(solution)/shard_map/unpack/pallas_call | solution.py:46
  257.6 5.1 %all-to-all-done = bf16[4,256,512]{2,1,0:T(8,128)(2,1)} async-done(((bf16[4,256,512]{2,1,0:T(8,128)(2,1)}), bf16[4,256,512]{2,1,0:T(8,128)(2,1)}, u32[]{:S(2)}, u32[]{:S(2)}) %all-to-all-start) | async-done | bytes 1048608 | tf_op jit(solution)/shard_map/all_to_all | solution.py:896
  262.7 3.3 %unsort_rows.3 = f32[1024,512]{1,0:T(8,128)} custom-call(s32[1]{0:T(128)} %constant.61.clone.1.refs_0_, bf16[1024,512]{1,0:T(8,128)(2,1)} %bitcast.17.refs_1_), custom_call_target="tpu_custom_call" | custom-call | tf_op jit(solution)/shard_map/unsort_rows/pallas_call | solution.py:153
  (84 shorter events, 19.4 us)
Async XLA Ops:
  0.6 29.2 %collective-permute-start.3 = (bf16[1024,512]{1,0:T(8,128)(2,1)}, bf16[1024,512]{1,0:T(8,128)(2,1)}, u32[]{:S(2)}, u32[]{:S(2)}) collective-permute-start(bf16[1024,512]{1,0:T(8,128)(2,1)} %bitcast.25), channel_id=1, source_target_pairs={{0,1},{1,0},{2,3},{3,2},{4,5},{5,4},{6,7},{7,6},{8,9},{9,8},{10,11... | collective-permute-start | bytes 3145736 | tf_op jit(solution)/shard_map/ppermute | solution.py:708
  6.5 19.8 %collective-permute-start = (bf16[256,512]{1,0:T(8,128)(2,1)}, bf16[256,512]{1,0:T(8,128)(2,1)}, u32[]{:S(2)}, u32[]{:S(2)}) collective-permute-start(bf16[256,512]{1,0:T(8,128)(2,1)} %get-tuple-element.177), channel_id=1, source_target_pairs={{0,2},{1,3},{2,0},{3,1},{4,6},{5,7},{6,4},{7,5},{8,10},{9,11},{10,... | collective-permute-start | bytes 786440 | tf_op jit(solution)/shard_map/ppermute | solution.py:708
  8.1 21.7 %collective-permute-start.1 = (bf16[256,512]{1,0:T(8,128)(2,1)}, bf16[256,512]{1,0:T(8,128)(2,1)}, u32[]{:S(2)}, u32[]{:S(2)}) collective-permute-start(bf16[256,512]{1,0:T(8,128)(2,1)} %get-tuple-element.178), channel_id=1, source_target_pairs={{0,4},{1,5},{2,6},{3,7},{4,0},{5,1},{6,2},{7,3},{8,12},{9,13},{10,... | collective-permute-start | bytes 786440 | tf_op jit(solution)/shard_map/ppermute | solution.py:708
  10.7 19.1 %collective-permute-start.2 = (bf16[256,512]{1,0:T(8,128)(2,1)}, bf16[256,512]{1,0:T(8,128)(2,1)}, u32[]{:S(2)}, u32[]{:S(2)}) collective-permute-start(bf16[256,512]{1,0:T(8,128)(2,1)} %get-tuple-element.179), channel_id=1, source_target_pairs={{0,6},{1,7},{2,4},{3,5},{4,2},{5,3},{6,0},{7,1},{8,14},{9,15},{10,... | collective-permute-start | bytes 786440 | tf_op jit(solution)/shard_map/ppermute | solution.py:708
  32.2 28.1 %collective-permute-start.4 = (bf16[768,512]{1,0:T(8,128)(2,1)}, bf16[768,512]{1,0:T(8,128)(2,1)}, u32[]{:S(2)}, u32[]{:S(2)}) collective-permute-start(bf16[768,512]{1,0:T(8,128)(2,1)} %slice_select_fusion), channel_id=1, source_target_pairs={{0,2},{1,3},{2,4},{3,5},{4,6},{5,7},{8,10},{9,11},{10,12},{11,13},... | collective-permute-start | bytes 2359304 | tf_op jit(solution)/shard_map/ppermute | solution.py:806
  39.7 20.6 %collective-permute-start.5 = (bf16[256,512]{1,0:T(8,128)(2,1)}, bf16[256,512]{1,0:T(8,128)(2,1)}, u32[]{:S(2)}, u32[]{:S(2)}) collective-permute-start(bf16[256,512]{1,0:T(8,128)(2,1)} %get-tuple-element.199), channel_id=1, source_target_pairs={{0,2},{1,3},{2,0},{3,1},{4,6},{5,7},{6,4},{7,5},{8,10},{9,11},{10,... | collective-permute-start | bytes 786440 | tf_op jit(solution)/shard_map/ppermute | solution.py:708
  60.3 23.3 %collective-permute-start.6 = (bf16[256,512]{1,0:T(8,128)(2,1)}, bf16[256,512]{1,0:T(8,128)(2,1)}, u32[]{:S(2)}, u32[]{:S(2)}) collective-permute-start(bf16[256,512]{1,0:T(8,128)(2,1)} %get-tuple-element.204), channel_id=1, source_target_pairs={{0,4},{1,5},{2,6},{3,7},{4,0},{5,1},{6,2},{7,3},{8,12},{9,13},{10,... | collective-permute-start | bytes 786440 | tf_op jit(solution)/shard_map/ppermute | solution.py:708
  61.1 22.4 %collective-permute-start.7 = (bf16[256,512]{1,0:T(8,128)(2,1)}, bf16[256,512]{1,0:T(8,128)(2,1)}, u32[]{:S(2)}, u32[]{:S(2)}) collective-permute-start(bf16[256,512]{1,0:T(8,128)(2,1)} %get-tuple-element.205), channel_id=1, source_target_pairs={{0,6},{1,7},{2,4},{3,5},{4,2},{5,3},{6,0},{7,1},{8,14},{9,15},{10,... | collective-permute-start | bytes 786440 | tf_op jit(solution)/shard_map/ppermute | solution.py:708
  83.6 26.9 %collective-permute-start.8 = (bf16[256,512]{1,0:T(8,128)(2,1)}, bf16[256,512]{1,0:T(8,128)(2,1)}, u32[]{:S(2)}, u32[]{:S(2)}) collective-permute-start(bf16[256,512]{1,0:T(8,128)(2,1)} %get-tuple-element.219), channel_id=1, source_target_pairs={{0,2},{1,3},{2,0},{3,1},{4,6},{5,7},{6,4},{7,5},{8,10},{9,11},{10,... | collective-permute-start | bytes 786440 | tf_op jit(solution)/shard_map/ppermute | solution.py:708
  84.1 26.3 %collective-permute-start.9 = (bf16[256,512]{1,0:T(8,128)(2,1)}, bf16[256,512]{1,0:T(8,128)(2,1)}, u32[]{:S(2)}, u32[]{:S(2)}) collective-permute-start(bf16[256,512]{1,0:T(8,128)(2,1)} %get-tuple-element.220), channel_id=1, source_target_pairs={{0,4},{1,5},{2,6},{3,7},{4,0},{5,1},{6,2},{7,3},{8,12},{9,13},{10,... | collective-permute-start | bytes 786440 | tf_op jit(solution)/shard_map/ppermute | solution.py:708
  85.7 24.8 %collective-permute-start.10 = (bf16[256,512]{1,0:T(8,128)(2,1)}, bf16[256,512]{1,0:T(8,128)(2,1)}, u32[]{:S(2)}, u32[]{:S(2)}) collective-permute-start(bf16[256,512]{1,0:T(8,128)(2,1)} %get-tuple-element.221), channel_id=1, source_target_pairs={{0,6},{1,7},{2,4},{3,5},{4,2},{5,3},{6,0},{7,1},{8,14},{9,15},{10,... | collective-permute-start | bytes 786440 | tf_op jit(solution)/shard_map/ppermute | solution.py:708
  110.5 7.4 %collective-permute-start.11 = (bf16[2048,512]{1,0:T(8,128)(2,1)}, bf16[2048,512]{1,0:T(8,128)(2,1)}, u32[]{:S(2)}, u32[]{:S(2)}) collective-permute-start(bf16[2048,512]{1,0:T(8,128)(2,1)} %get-tuple-element.237), channel_id=1, source_target_pairs={{0,8},{1,9},{2,10},{3,11},{4,12},{5,13},{6,14},{7,15},{8,0},{9,1},... | collective-permute-start | bytes 6291464 | tf_op jit(solution)/shard_map/ppermute | solution.py:708
  110.6 8.9 %copy-start.6 = (s32[7]{0:T(128)S(1)}, s32[7]{0:T(128)}, u32[]{:S(2)}) copy-start(s32[7]{0:T(128)} %pad_add_fusion.refs_0_.info_ref) | copy-start | bytes 88
  117.9 35.4 %collective-permute-start.15 = (bf16[768,512]{1,0:T(8,128)(2,1)}, bf16[768,512]{1,0:T(8,128)(2,1)}, u32[]{:S(2)}, u32[]{:S(2)}) collective-permute-start(bf16[768,512]{1,0:T(8,128)(2,1)} %get-tuple-element.253), channel_id=1, source_target_pairs={{2,0},{3,1},{4,2},{5,3},{6,4},{7,5},{10,8},{11,9},{12,10},{13,11},... | collective-permute-start | bytes 2359304 | tf_op jit(solution)/shard_map/ppermute | solution.py:846
  119.4 1.6 copy-start
  124.1 0.8 copy-start.2
  124.9 28.3 %collective-permute-start.12 = (bf16[512,512]{1,0:T(8,128)(2,1)}, bf16[512,512]{1,0:T(8,128)(2,1)}, u32[]{:S(2)}, u32[]{:S(2)}) collective-permute-start(bf16[512,512]{1,0:T(8,128)(2,1)} %get-tuple-element.250), channel_id=1, source_target_pairs={{0,1},{1,0},{2,3},{3,2},{4,5},{5,4},{6,7},{7,6},{8,9},{9,8},{10,11... | collective-permute-start | bytes 1572872 | tf_op jit(solution)/shard_map/ppermute | solution.py:708
  125.4 27.9 %collective-permute-start.13 = (bf16[512,512]{1,0:T(8,128)(2,1)}, bf16[512,512]{1,0:T(8,128)(2,1)}, u32[]{:S(2)}, u32[]{:S(2)}) collective-permute-start(bf16[512,512]{1,0:T(8,128)(2,1)} %get-tuple-element.251), channel_id=1, source_target_pairs={{0,16},{1,17},{2,18},{3,19},{4,20},{5,21},{6,22},{7,23},{8,24},{9,... | collective-permute-start | bytes 1572872 | tf_op jit(solution)/shard_map/ppermute | solution.py:708
  126.9 26.4 %collective-permute-start.14 = (bf16[512,512]{1,0:T(8,128)(2,1)}, bf16[512,512]{1,0:T(8,128)(2,1)}, u32[]{:S(2)}, u32[]{:S(2)}) collective-permute-start(bf16[512,512]{1,0:T(8,128)(2,1)} %get-tuple-element.252), channel_id=1, source_target_pairs={{0,17},{1,16},{2,19},{3,18},{4,21},{5,20},{6,23},{7,22},{8,25},{9,... | collective-permute-start | bytes 1572872 | tf_op jit(solution)/shard_map/ppermute | solution.py:708
  153.3 23.5 %collective-permute-start.16 = (bf16[1040,512]{1,0:T(8,128)(2,1)}, bf16[1040,512]{1,0:T(8,128)(2,1)}, u32[]{:S(2)}, u32[]{:S(2)}) collective-permute-start(bf16[1040,512]{1,0:T(8,128)(2,1)} %get-tuple-element.275), channel_id=1, source_target_pairs={{0,8},{1,9},{2,10},{3,11},{4,12},{5,13},{6,14},{7,15},{8,0},{9,1},... | collective-permute-start | bytes 3194888 | tf_op jit(solution)/shard_map/ppermute | solution.py:708
  153.4 1.0 copy-start.3
  154.4 3.0 %copy-start.7 = (bf16[1024,512]{1,0:T(8,128)(2,1)S(1)}, bf16[1024,512]{1,0:T(8,128)(2,1)}, u32[]{:S(2)}) copy-start(bf16[1024,512]{1,0:T(8,128)(2,1)} %get-tuple-element.309) | copy-start | bytes 3145732
  156.8 0.7 copy-start.4
  160.3 46.6 %collective-permute-start.30 = (bf16[1024,512]{1,0:T(8,128)(2,1)}, bf16[1024,512]{1,0:T(8,128)(2,1)}, u32[]{:S(2)}, u32[]{:S(2)}) collective-permute-start(bf16[1024,512]{1,0:T(8,128)(2,1)} %get-tuple-element.311), channel_id=1, source_target_pairs={{0,1},{1,0},{2,3},{3,2},{4,5},{5,4},{6,7},{7,6},{8,9},{9,8},{10,11... | collective-permute-start | bytes 3145736 | tf_op jit(solution)/shard_map/ppermute | solution.py:708
  160.8 9.0 %collective-permute-start.17 = (bf16[128,512]{1,0:T(8,128)(2,1)}, bf16[128,512]{1,0:T(8,128)(2,1)}, u32[]{:S(2)}, u32[]{:S(2)}) collective-permute-start(bf16[128,512]{1,0:T(8,128)(2,1)} %get-tuple-element.279), channel_id=1, source_target_pairs={{0,2},{1,3},{2,0},{3,1},{4,6},{5,7},{6,4},{7,5},{8,10},{9,11},{10,... | collective-permute-start | bytes 393224 | tf_op jit(solution)/shard_map/ppermute | solution.py:708
  162.8 14.1 %collective-permute-start.18 = (bf16[128,512]{1,0:T(8,128)(2,1)}, bf16[128,512]{1,0:T(8,128)(2,1)}, u32[]{:S(2)}, u32[]{:S(2)}) collective-permute-start(bf16[128,512]{1,0:T(8,128)(2,1)} %get-tuple-element.280), channel_id=1, source_target_pairs={{0,4},{1,5},{2,6},{3,7},{4,0},{5,1},{6,2},{7,3},{8,12},{9,13},{10,... | collective-permute-start | bytes 393224 | tf_op jit(solution)/shard_map/ppermute | solution.py:708
  166.6 10.2 %collective-permute-start.19 = (bf16[128,512]{1,0:T(8,128)(2,1)}, bf16[128,512]{1,0:T(8,128)(2,1)}, u32[]{:S(2)}, u32[]{:S(2)}) collective-permute-start(bf16[128,512]{1,0:T(8,128)(2,1)} %get-tuple-element.281), channel_id=1, source_target_pairs={{0,6},{1,7},{2,4},{3,5},{4,2},{5,3},{6,0},{7,1},{8,14},{9,15},{10,... | collective-permute-start | bytes 393224 | tf_op jit(solution)/shard_map/ppermute | solution.py:708
  176.8 0.9 copy-start.5
  178.9 9.0 %collective-permute-start.20 = (bf16[128,512]{1,0:T(8,128)(2,1)S(1)}, bf16[128,512]{1,0:T(8,128)(2,1)S(1)}, u32[]{:S(2)}, u32[]{:S(2)}) collective-permute-start(bf16[128,512]{1,0:T(8,128)(2,1)S(1)} %split_sum.8), channel_id=1, source_target_pairs={{0,2},{1,3},{2,0},{3,1},{4,6},{5,7},{6,4},{7,5},{8,10},{9,11},{10,... | collective-permute-start | bytes 393224 | tf_op jit(solution)/shard_map/ppermute | solution.py:708
  181.6 1.2 copy-start.1
  184.3 8.8 %collective-permute-start.21 = (bf16[272,512]{1,0:T(8,128)(2,1)S(1)}, bf16[272,512]{1,0:T(8,128)(2,1)S(1)}, u32[]{:S(2)}, u32[]{:S(2)}) collective-permute-start(bf16[272,512]{1,0:T(8,128)(2,1)S(1)} %get-tuple-element.299), channel_id=1, source_target_pairs={{0,1},{1,0},{2,3},{3,2},{4,5},{5,4},{6,7},{7,6},{8,9},{9,8},{10,11... | collective-permute-start | bytes 835592 | tf_op jit(solution)/shard_map/ppermute | solution.py:708
  185.9 9.6 %collective-permute-start.22 = (bf16[272,512]{1,0:T(8,128)(2,1)S(1)}, bf16[272,512]{1,0:T(8,128)(2,1)S(1)}, u32[]{:S(2)}, u32[]{:S(2)}) collective-permute-start(bf16[272,512]{1,0:T(8,128)(2,1)S(1)} %get-tuple-element.300), channel_id=1, source_target_pairs={{0,16},{1,17},{2,18},{3,19},{4,20},{5,21},{6,22},{7,23},{8,24},{9,... | collective-permute-start | bytes 835592 | tf_op jit(solution)/shard_map/ppermute | solution.py:708
  187.7 11.7 %collective-permute-start.23 = (bf16[272,512]{1,0:T(8,128)(2,1)S(1)}, bf16[272,512]{1,0:T(8,128)(2,1)S(1)}, u32[]{:S(2)}, u32[]{:S(2)}) collective-permute-start(bf16[272,512]{1,0:T(8,128)(2,1)S(1)} %get-tuple-element.301), channel_id=1, source_target_pairs={{0,17},{1,16},{2,19},{3,18},{4,21},{5,20},{6,23},{7,22},{8,25},{9,... | collective-permute-start | bytes 835592 | tf_op jit(solution)/shard_map/ppermute | solution.py:708
  187.9 12.9 %collective-permute-start.24 = (bf16[256,512]{1,0:T(8,128)(2,1)S(1)}, bf16[256,512]{1,0:T(8,128)(2,1)S(1)}, u32[]{:S(2)}, u32[]{:S(2)}) collective-permute-start(bf16[256,512]{1,0:T(8,128)(2,1)S(1)} %pad_maximum_fusion.1), channel_id=1, source_target_pairs={{0,4},{1,5},{2,6},{3,7},{4,0},{5,1},{6,2},{7,3},{8,12},{9,13},{10,... | collective-permute-start | bytes 786440 | tf_op jit(solution)/shard_map/ppermute | solution.py:708
  193.1 15.2 %collective-permute-start.28 = (bf16[256,512]{1,0:T(8,128)(2,1)S(1)}, bf16[256,512]{1,0:T(8,128)(2,1)S(1)}, u32[]{:S(2)}, u32[]{:S(2)}) collective-permute-start(bf16[256,512]{1,0:T(8,128)(2,1)S(1)} %pad_maximum_fusion.1), channel_id=1, source_target_pairs={{0,1},{1,0},{2,3},{3,2},{4,5},{5,4},{6,7},{7,6},{8,9},{9,8},{10,11... | collective-permute-start | bytes 786440 | tf_op jit(solution)/shard_map/ppermute | solution.py:708
  200.8 12.4 %collective-permute-start.29 = (bf16[256,512]{1,0:T(8,128)(2,1)S(1)}, bf16[256,512]{1,0:T(8,128)(2,1)S(1)}, u32[]{:S(2)}, u32[]{:S(2)}) collective-permute-start(bf16[256,512]{1,0:T(8,128)(2,1)S(1)} %collective-permute-done.24), channel_id=1, source_target_pairs={{0,16},{1,17},{2,18},{3,19},{4,20},{5,21},{6,22},{7,23},{8,24},{9,... | collective-permute-start | bytes 786440 | tf_op jit(solution)/shard_map/ppermute | solution.py:708
  203.2 5.2 %collective-permute-start.25 = (bf16[80,512]{1,0:T(8,128)(2,1)S(1)}, bf16[80,512]{1,0:T(8,128)(2,1)S(1)}, u32[]{:S(2)}, u32[]{:S(2)}) collective-permute-start(bf16[80,512]{1,0:T(8,128)(2,1)S(1)} %get-tuple-element.305), channel_id=1, source_target_pairs={{0,2},{1,3},{2,0},{3,1},{4,6},{5,7},{6,4},{7,5},{8,10},{9,11},{10,... | collective-permute-start | bytes 245768 | tf_op jit(solution)/shard_map/ppermute | solution.py:708
  203.3 8.8 %collective-permute-start.26 = (bf16[80,512]{1,0:T(8,128)(2,1)S(1)}, bf16[80,512]{1,0:T(8,128)(2,1)S(1)}, u32[]{:S(2)}, u32[]{:S(2)}) collective-permute-start(bf16[80,512]{1,0:T(8,128)(2,1)S(1)} %get-tuple-element.306), channel_id=1, source_target_pairs={{0,4},{1,5},{2,6},{3,7},{4,0},{5,1},{6,2},{7,3},{8,12},{9,13},{10,... | collective-permute-start | bytes 245768 | tf_op jit(solution)/shard_map/ppermute | solution.py:708
  206.9 6.3 %collective-permute-start.27 = (bf16[80,512]{1,0:T(8,128)(2,1)S(1)}, bf16[80,512]{1,0:T(8,128)(2,1)S(1)}, u32[]{:S(2)}, u32[]{:S(2)}) collective-permute-start(bf16[80,512]{1,0:T(8,128)(2,1)S(1)} %get-tuple-element.307), channel_id=1, source_target_pairs={{0,6},{1,7},{2,4},{3,5},{4,2},{5,3},{6,0},{7,1},{8,14},{9,15},{10,... | collective-permute-start | bytes 245768 | tf_op jit(solution)/shard_map/ppermute | solution.py:708
  214.0 18.7 %collective-permute-start.36 = (bf16[512,512]{1,0:T(8,128)(2,1)}, bf16[512,512]{1,0:T(8,128)(2,1)}, u32[]{:S(2)}, u32[]{:S(2)}) collective-permute-start(bf16[512,512]{1,0:T(8,128)(2,1)} %constant_dynamic-update-slice_fusion.refs_2_), channel_id=1, source_target_pairs={{0,8},{1,9},{2,10},{3,11},{4,12},{5,13},{6,14},{7,15},{8,0},{9,1},... | collective-permute-start | bytes 1572872 | tf_op jit(solution)/shard_map/ppermute | solution.py:708
  214.0 18.7 %collective-permute-start.32 = (bf16[512,512]{1,0:T(8,128)(2,1)}, bf16[512,512]{1,0:T(8,128)(2,1)}, u32[]{:S(2)}, u32[]{:S(2)}) collective-permute-start(bf16[512,512]{1,0:T(8,128)(2,1)} %constant_dynamic-update-slice_fusion.refs_2_), channel_id=1, source_target_pairs={{0,1},{1,0},{2,3},{3,2},{4,5},{5,4},{6,7},{7,6},{8,9},{9,8},{10,11... | collective-permute-start | bytes 1572872 | tf_op jit(solution)/shard_map/ppermute | solution.py:708
  216.3 16.3 %collective-permute-start.35 = (bf16[512,512]{1,0:T(8,128)(2,1)}, bf16[512,512]{1,0:T(8,128)(2,1)}, u32[]{:S(2)}, u32[]{:S(2)}) collective-permute-start(bf16[512,512]{1,0:T(8,128)(2,1)} %pad_maximum_fusion.refs_0_), channel_id=1, source_target_pairs={{0,8},{1,9},{2,10},{3,11},{4,12},{5,13},{6,14},{7,15},{8,0},{9,1},... | collective-permute-start | bytes 1572872 | tf_op jit(solution)/shard_map/ppermute | solution.py:708
  216.5 16.1 %collective-permute-start.31 = (bf16[512,512]{1,0:T(8,128)(2,1)}, bf16[512,512]{1,0:T(8,128)(2,1)}, u32[]{:S(2)}, u32[]{:S(2)}) collective-permute-start(bf16[512,512]{1,0:T(8,128)(2,1)} %pad_maximum_fusion.refs_0_), channel_id=1, source_target_pairs={{0,16},{1,17},{2,18},{3,19},{4,20},{5,21},{6,22},{7,23},{8,24},{9,... | collective-permute-start | bytes 1572872 | tf_op jit(solution)/shard_map/ppermute | solution.py:708
  217.4 4.3 %collective-permute-start.33 = (bf16[64,512]{1,0:T(8,128)(2,1)S(1)}, bf16[64,512]{1,0:T(8,128)(2,1)S(1)}, u32[]{:S(2)}, u32[]{:S(2)}) collective-permute-start(bf16[64,512]{1,0:T(8,128)(2,1)S(1)} %get-tuple-element.318), channel_id=1, source_target_pairs={{0,2},{1,3},{2,0},{3,1},{4,6},{5,7},{6,4},{7,5},{8,10},{9,11},{10,... | collective-permute-start | bytes 196616 | tf_op jit(solution)/shard_map/ppermute | solution.py:708
  221.8 0.6 copy-start.8
  223.0 8.7 %collective-permute-start.34 = (bf16[128,512]{1,0:T(8,128)(2,1)}, bf16[128,512]{1,0:T(8,128)(2,1)}, u32[]{:S(2)}, u32[]{:S(2)}) collective-permute-start(bf16[128,512]{1,0:T(8,128)(2,1)} %constant_dynamic-update-slice_fusion.2), channel_id=1, source_target_pairs={{0,4},{1,5},{2,6},{3,7},{4,0},{5,1},{6,2},{7,3},{8,12},{9,13},{10,... | collective-permute-start | bytes 393224 | tf_op jit(solution)/shard_map/ppermute | solution.py:708
  232.7 30.0 %all-to-all-start = ((bf16[4,256,512]{2,1,0:T(8,128)(2,1)}), bf16[4,256,512]{2,1,0:T(8,128)(2,1)}, u32[]{:S(2)}, u32[]{:S(2)}) async-start(bf16[4,256,512]{2,1,0:T(8,128)(2,1)} %bitcast.35), calls=%async_computation | async-start | bytes 2097152 | tf_op jit(solution)/shard_map/all_to_all | solution.py:896
  237.1 4.1 %collective-permute-start.40 = (bf16[512,512]{1,0:T(8,128)(2,1)}, bf16[512,512]{1,0:T(8,128)(2,1)S(1)}, u32[]{:S(2)}, u32[]{:S(2)}) collective-permute-start(bf16[512,512]{1,0:T(8,128)(2,1)} %collective-permute-done.31.refs_1_), channel_id=1, source_target_pairs={{0,8},{1,9},{2,10},{3,11},{4,12},{5,13},{6,14},{7,15},{8,0},{9,1},... | collective-permute-start | bytes 1572872 | tf_op jit(solution)/shard_map/ppermute | solution.py:708
  237.2 4.0 %collective-permute-start.41 = (bf16[512,512]{1,0:T(8,128)(2,1)}, bf16[512,512]{1,0:T(8,128)(2,1)S(1)}, u32[]{:S(2)}, u32[]{:S(2)}) collective-permute-start(bf16[512,512]{1,0:T(8,128)(2,1)} %collective-permute-done.32.refs_3_), channel_id=1, source_target_pairs={{0,8},{1,9},{2,10},{3,11},{4,12},{5,13},{6,14},{7,15},{8,0},{9,1},... | collective-permute-start | bytes 1572872 | tf_op jit(solution)/shard_map/ppermute | solution.py:708
  237.7 10.2 %collective-permute-start.39 = (bf16[256,512]{1,0:T(8,128)(2,1)S(1)}, bf16[256,512]{1,0:T(8,128)(2,1)S(1)}, u32[]{:S(2)}, u32[]{:S(2)}) collective-permute-start(bf16[256,512]{1,0:T(8,128)(2,1)S(1)} %pad_maximum_fusion.2.refs_0_), channel_id=1, source_target_pairs={{0,17},{1,16},{2,19},{3,18},{4,21},{5,20},{6,23},{7,22},{8,25},{9,... | collective-permute-start | bytes 786440 | tf_op jit(solution)/shard_map/ppermute | solution.py:708
  239.4 12.3 %collective-permute-start.38 = (bf16[256,512]{1,0:T(8,128)(2,1)S(1)}, bf16[256,512]{1,0:T(8,128)(2,1)S(1)}, u32[]{:S(2)}, u32[]{:S(2)}) collective-permute-start(bf16[256,512]{1,0:T(8,128)(2,1)S(1)} %pad_maximum_fusion.2.refs_0_), channel_id=1, source_target_pairs={{0,16},{1,17},{2,18},{3,19},{4,20},{5,21},{6,22},{7,23},{8,24},{9,... | collective-permute-start | bytes 786440 | tf_op jit(solution)/shard_map/ppermute | solution.py:708
  239.6 12.8 %collective-permute-start.37 = (bf16[256,512]{1,0:T(8,128)(2,1)S(1)}, bf16[256,512]{1,0:T(8,128)(2,1)S(1)}, u32[]{:S(2)}, u32[]{:S(2)}) collective-permute-start(bf16[256,512]{1,0:T(8,128)(2,1)S(1)} %pad_maximum_fusion.2.refs_0_), channel_id=1, source_target_pairs={{0,1},{1,0},{2,3},{3,2},{4,5},{5,4},{6,7},{7,6},{8,9},{9,8},{10,11... | collective-permute-start | bytes 786440 | tf_op jit(solution)/shard_map/ppermute | solution.py:708
  241.2 12.4 %collective-permute-start.42 = (bf16[256,512]{1,0:T(8,128)(2,1)S(1)}, bf16[256,512]{1,0:T(8,128)(2,1)S(1)}, u32[]{:S(2)}, u32[]{:S(2)}) collective-permute-start(bf16[256,512]{1,0:T(8,128)(2,1)S(1)} %pad_maximum_fusion.2.refs_0_), channel_id=1, source_target_pairs={{0,8},{1,9},{2,10},{3,11},{4,12},{5,13},{6,14},{7,15},{8,0},{9,1},... | collective-permute-start | bytes 786440 | tf_op jit(solution)/shard_map/ppermute | solution.py:708
  252.5 1.5 collective-permute-start.43
  252.5 1.9 collective-permute-start.44
  253.0 1.8 collective-permute-start.45
